TPU v7x, 32 devices: a whole 2x2x4 slice. The times are simulated.
32 devices in a mesh: dp: 8 (over y, x, core), ctx: 4 (over z).
Axes of the slice: x: 2, y: 2, z: 4, core: 2. Of those that a mesh axis runs over, the one named last changes fastest.
Arguments:
- tokens: bfloat16 [16384, 1024], P(('dp', 'ctx')), may hold values from -6 to 6
- lengths: int32 [8], P('dp'), may hold values from 512 to 2048, as said below
- cotangent: bfloat16 [16384, 1024], P(('dp', 'ctx')), may hold values from -6 to 6
- query_proj: float32 [1024, 1024], P(('dp', 'ctx')), may hold values from -0.375 to 0.375
- query_offset: float32 [1024], P(('dp', 'ctx')), may hold values from -2 to 2
- key_proj: float32 [1024, 1024], P(('dp', 'ctx')), may hold values from -0.1875 to 0.1875
- value_proj: float32 [1024, 1024], P(('dp', 'ctx')), may hold values from -0.1875 to 0.1875
- value_offset: float32 [1024], P(('dp', 'ctx')), may hold values from -0.3 to 0.3
- attn_proj: float32 [1024, 1024], P(('dp', 'ctx')), may hold values from -1.5 to 1.5
- attn_offset: float32 [1024], P(('dp', 'ctx')), may hold values from -2 to 2
- attn_gain: float32 [1024], P(('dp', 'ctx')), may hold values from 0.1 to 1.9
- attn_shift: float32 [1024], P(('dp', 'ctx')), may hold values from -2 to 2
- inner_proj: float32 [1024, 4096], P(('dp', 'ctx')), may hold values from -0.1875 to 0.1875
- inner_offset: float32 [4096], P(('dp', 'ctx')), may hold values from -2 to 2
- outer_proj: float32 [4096, 1024], P(('dp', 'ctx')), may hold values from -0.09375 to 0.09375
- outer_offset: float32 [1024], P(('dp', 'ctx')), may hold values from -2 to 2
- final_gain: float32 [1024], P(('dp', 'ctx')), may hold values from 0.1 to 1.9
- final_shift: float32 [1024], P(('dp', 'ctx')), may hold values from -2 to 2
Outputs:
- layer_out: bfloat16 [16384, 1024], P(('dp', 'ctx'))
- input_grad: bfloat16 [16384, 1024], P(('dp', 'ctx'))
- grad_query_proj: float32 [1024, 1024], P(('dp', 'ctx'))
- grad_query_offset: float32 [1024], P(('dp', 'ctx'))
- grad_key_proj: float32 [1024, 1024], P(('dp', 'ctx'))
- grad_value_proj: float32 [1024, 1024], P(('dp', 'ctx'))
- grad_value_offset: float32 [1024], P(('dp', 'ctx'))
- grad_attn_proj: float32 [1024, 1024], P(('dp', 'ctx'))
- grad_attn_offset: float32 [1024], P(('dp', 'ctx'))
- grad_attn_gain: float32 [1024], P(('dp', 'ctx'))
- grad_attn_shift: float32 [1024], P(('dp', 'ctx'))
- grad_inner_proj: float32 [1024, 4096], P(('dp', 'ctx'))
- grad_inner_offset: float32 [4096], P(('dp', 'ctx'))
- grad_outer_proj: float32 [4096, 1024], P(('dp', 'ctx'))
- grad_outer_offset: float32 [1024], P(('dp', 'ctx'))
- grad_final_gain: float32 [1024], P(('dp', 'ctx'))
- grad_final_shift: float32 [1024], P(('dp', 'ctx'))
Inputs may be any that keep to these rules, and one draw needn't show every extreme that they name: Sequence b holds lengths[b] real tokens followed by padding; some sequence has all 2048 tokens and some other has exactly 512.
All inputs are finite; a program needn't handle non-finite values.
Results may differ from a plain program's by a relative error of at most 0.04.
Values may be sent and summed in bfloat16 or wider, within the bound.
No kernel may reach another device: no remote copies, remote signals or barrier semaphores. Data moves between devices by JAX's collectives and lax.ppermute only.
A program may use at most 320 MiB of HBM per device.

v0:
```python
import math

import jax
import jax.numpy as jnp
from jax import lax
from jax.sharding import PartitionSpec as P

HD = 64


norm_eps = 1e-05
group_width = 128


def layer_norm(residual, norm_gain, norm_shift):
    centered = residual - jnp.mean(residual, axis=1, keepdims=True)
    inverse = lax.rsqrt(jnp.mean(centered * centered, axis=1, keepdims=True) + norm_eps)
    normed = centered * inverse
    return (normed * norm_gain + norm_shift, normed, inverse)


def layer_norm_back(upstream, normed, inverse, norm_gain):
    scaled = upstream * norm_gain
    first_mean = jnp.mean(scaled, axis=1, keepdims=True)
    second_mean = jnp.mean(scaled * normed, axis=1, keepdims=True)
    return inverse * (scaled - first_mean - normed * second_mean)


def gelu_value(pre_act):
    return 0.5 * pre_act * (1.0 + lax.erf(pre_act * (1.0 / math.sqrt(2.0))))


def gelu_slope(pre_act):
    normal_cdf = 0.5 * (1.0 + lax.erf(pre_act * (1.0 / math.sqrt(2.0))))
    return normal_cdf + pre_act * jnp.exp(-0.5 * pre_act * pre_act) * (
        1.0 / math.sqrt(2.0 * math.pi)
    )


def head_split(columns):
    return columns.reshape(columns.shape[0], columns.shape[1] // HD, HD)


def group_scores(query_cols, key_cols, key_mask):
    scores = jnp.einsum(
        "qhd,khd->hqk",
        head_split(query_cols),
        head_split(key_cols),
        preferred_element_type=jnp.float32,
    )
    return jnp.where(key_mask[None, None, :], scores * (1.0 / math.sqrt(HD)), -1e30)


def row_sum(values):
    return jnp.sum(values.astype(jnp.float32), axis=0)


def local(
    tokens,
    lengths,
    cotangent,
    query_proj,
    query_offset,
    key_proj,
    value_proj,
    value_offset,
    attn_proj,
    attn_offset,
    attn_gain,
    attn_shift,
    inner_proj,
    inner_offset,
    outer_proj,
    outer_offset,
    final_gain,
    final_shift,
):
    gathered = (
        lax.all_gather(query_proj.astype(jnp.bfloat16), ("dp", "ctx"), axis=0, tiled=True),
        lax.all_gather(query_offset.astype(jnp.bfloat16), ("dp", "ctx"), axis=0, tiled=True),
        lax.all_gather(key_proj.astype(jnp.bfloat16), ("dp", "ctx"), axis=0, tiled=True),
        lax.all_gather(value_proj.astype(jnp.bfloat16), ("dp", "ctx"), axis=0, tiled=True),
        lax.all_gather(value_offset.astype(jnp.bfloat16), ("dp", "ctx"), axis=0, tiled=True),
        lax.all_gather(attn_proj.astype(jnp.bfloat16), ("dp", "ctx"), axis=0, tiled=True),
        lax.all_gather(attn_offset.astype(jnp.bfloat16), ("dp", "ctx"), axis=0, tiled=True),
        lax.all_gather(attn_gain.astype(jnp.bfloat16), ("dp", "ctx"), axis=0, tiled=True),
        lax.all_gather(attn_shift.astype(jnp.bfloat16), ("dp", "ctx"), axis=0, tiled=True),
        lax.all_gather(inner_proj.astype(jnp.bfloat16), ("dp", "ctx"), axis=0, tiled=True),
        lax.all_gather(inner_offset.astype(jnp.bfloat16), ("dp", "ctx"), axis=0, tiled=True),
        lax.all_gather(outer_proj.astype(jnp.bfloat16), ("dp", "ctx"), axis=0, tiled=True),
        lax.all_gather(outer_offset.astype(jnp.bfloat16), ("dp", "ctx"), axis=0, tiled=True),
        lax.all_gather(final_gain.astype(jnp.bfloat16), ("dp", "ctx"), axis=0, tiled=True),
        lax.all_gather(final_shift.astype(jnp.bfloat16), ("dp", "ctx"), axis=0, tiled=True),
    )
    (
        w_query,
        b_query,
        w_key,
        w_value,
        b_value,
        w_attn,
        b_attn,
        g_attn,
        s_attn,
        w_inner,
        b_inner,
        w_outer,
        b_outer,
        g_final,
        s_final,
    ) = gathered
    row_count = tokens.shape[0]
    model_width = tokens.shape[1]
    seq_rows = row_count * lax.axis_size("ctx")
    per_group = group_width // HD
    group_count = model_width // group_width
    head_count = model_width // HD
    seq_length = lengths[0]
    key_mask = jnp.arange(seq_rows, dtype=jnp.int32) < seq_length
    own_start = lax.axis_index("ctx") * row_count
    row_valid = own_start + jnp.arange(row_count, dtype=jnp.int32) < seq_length
    row_weight = row_valid.astype(jnp.float32)[:, None]
    queries = (jnp.dot(tokens, w_query, preferred_element_type=jnp.float32) + b_query).astype(
        jnp.bfloat16
    )
    keys_own = jnp.dot(tokens, w_key, preferred_element_type=jnp.float32).astype(jnp.bfloat16)
    values_own = (jnp.dot(tokens, w_value, preferred_element_type=jnp.float32) + b_value).astype(
        jnp.bfloat16
    )
    keys_all, values_all = (
        lax.all_gather(keys_own, "ctx", axis=0, tiled=True),
        lax.all_gather(values_own, "ctx", axis=0, tiled=True),
    )

    def forward_group(group_index, carried):
        mixed_rows, log_total = carried
        col_start = group_index * group_width
        query_cols = lax.dynamic_slice_in_dim(queries, col_start, group_width, 1)
        key_cols = lax.dynamic_slice_in_dim(keys_all, col_start, group_width, 1)
        value_cols = lax.dynamic_slice_in_dim(values_all, col_start, group_width, 1)
        scores = group_scores(query_cols, key_cols, key_mask)
        row_top = jnp.max(scores, axis=2, keepdims=True)
        shifted = jnp.where(key_mask[None, None, :], jnp.exp(scores - row_top), 0.0)
        group_total = row_top + jnp.log(jnp.sum(shifted, axis=2, keepdims=True))
        probs = jnp.where(key_mask[None, None, :], jnp.exp(scores - group_total), 0.0).astype(
            jnp.bfloat16
        )
        mixed_block = jnp.einsum(
            "hqk,khd->qhd", probs, head_split(value_cols), preferred_element_type=jnp.float32
        )
        mixed_rows = lax.dynamic_update_slice_in_dim(
            mixed_rows,
            mixed_block.reshape(row_count, group_width).astype(jnp.bfloat16),
            col_start,
            1,
        )
        log_total = lax.dynamic_update_slice_in_dim(
            log_total, group_total, group_index * per_group, 0
        )
        return (mixed_rows, log_total)

    mixed, log_total = lax.fori_loop(
        0,
        group_count,
        forward_group,
        (
            jnp.zeros((row_count, model_width), jnp.bfloat16),
            jnp.zeros((head_count, row_count, 1), jnp.float32),
        ),
    )
    first_res = (
        tokens.astype(jnp.float32)
        + jnp.dot(mixed, w_attn, preferred_element_type=jnp.float32)
        + b_attn
    )
    hidden, normed_one, inverse_one = layer_norm(first_res, g_attn, s_attn)
    hidden_low = hidden.astype(jnp.bfloat16)
    pre_act = jnp.dot(hidden_low, w_inner, preferred_element_type=jnp.float32) + b_inner
    activated = gelu_value(pre_act).astype(jnp.bfloat16)
    second_res = hidden + jnp.dot(activated, w_outer, preferred_element_type=jnp.float32) + b_outer
    final, normed_two, inverse_two = layer_norm(second_res, g_final, s_final)
    layer_out = (final * row_weight).astype(jnp.bfloat16)
    back_weights = (
        lax.all_gather(query_proj.astype(jnp.bfloat16), ("dp", "ctx"), axis=0, tiled=True),
        lax.all_gather(query_offset.astype(jnp.bfloat16), ("dp", "ctx"), axis=0, tiled=True),
        lax.all_gather(key_proj.astype(jnp.bfloat16), ("dp", "ctx"), axis=0, tiled=True),
        lax.all_gather(value_proj.astype(jnp.bfloat16), ("dp", "ctx"), axis=0, tiled=True),
        lax.all_gather(value_offset.astype(jnp.bfloat16), ("dp", "ctx"), axis=0, tiled=True),
        lax.all_gather(attn_proj.astype(jnp.bfloat16), ("dp", "ctx"), axis=0, tiled=True),
        lax.all_gather(attn_offset.astype(jnp.bfloat16), ("dp", "ctx"), axis=0, tiled=True),
        lax.all_gather(attn_gain.astype(jnp.bfloat16), ("dp", "ctx"), axis=0, tiled=True),
        lax.all_gather(attn_shift.astype(jnp.bfloat16), ("dp", "ctx"), axis=0, tiled=True),
        lax.all_gather(inner_proj.astype(jnp.bfloat16), ("dp", "ctx"), axis=0, tiled=True),
        lax.all_gather(inner_offset.astype(jnp.bfloat16), ("dp", "ctx"), axis=0, tiled=True),
        lax.all_gather(outer_proj.astype(jnp.bfloat16), ("dp", "ctx"), axis=0, tiled=True),
        lax.all_gather(outer_offset.astype(jnp.bfloat16), ("dp", "ctx"), axis=0, tiled=True),
        lax.all_gather(final_gain.astype(jnp.bfloat16), ("dp", "ctx"), axis=0, tiled=True),
        lax.all_gather(final_shift.astype(jnp.bfloat16), ("dp", "ctx"), axis=0, tiled=True),
    )
    upstream = cotangent.astype(jnp.float32) * row_weight
    grad_final_shift = jnp.sum(upstream, axis=0)
    grad_final_gain = jnp.sum(upstream * normed_two, axis=0)
    dsecond = layer_norm_back(upstream, normed_two, inverse_two, back_weights[13])
    douter = dsecond.astype(jnp.bfloat16)
    grad_outer_offset = row_sum(douter)
    grad_outer_proj = jnp.einsum("sf,sd->fd", activated, douter, preferred_element_type=jnp.float32)
    dactivated = jnp.einsum(
        "sd,fd->sf", douter, back_weights[11], preferred_element_type=jnp.float32
    )
    dpre_act = (dactivated * gelu_slope(pre_act)).astype(jnp.bfloat16)
    grad_inner_offset = row_sum(dpre_act)
    grad_inner_proj = jnp.einsum(
        "sd,sf->df", hidden_low, dpre_act, preferred_element_type=jnp.float32
    )
    dhidden = dsecond + jnp.einsum(
        "sf,df->sd", dpre_act, back_weights[9], preferred_element_type=jnp.float32
    )
    grad_attn_shift = jnp.sum(dhidden, axis=0)
    grad_attn_gain = jnp.sum(dhidden * normed_one, axis=0)
    dfirst = layer_norm_back(dhidden, normed_one, inverse_one, back_weights[7])
    dattn = dfirst.astype(jnp.bfloat16)
    grad_attn_offset = row_sum(dattn)
    grad_attn_proj = jnp.einsum("sd,se->de", mixed, dattn, preferred_element_type=jnp.float32)
    dmixed = jnp.einsum(
        "se,de->sd", dattn, back_weights[5], preferred_element_type=jnp.float32
    ).astype(jnp.bfloat16)
    keys_back, values_back = (keys_all, values_all)

    def backward_group(group_index, carried):
        grad_query_rows, grad_keys, grad_values, delta_rows = carried
        col_start = group_index * group_width
        query_cols = lax.dynamic_slice_in_dim(queries, col_start, group_width, 1)
        key_cols = lax.dynamic_slice_in_dim(keys_back, col_start, group_width, 1)
        value_cols = lax.dynamic_slice_in_dim(values_back, col_start, group_width, 1)
        upstream_cols = lax.dynamic_slice_in_dim(dmixed, col_start, group_width, 1)
        group_total = lax.dynamic_slice_in_dim(log_total, group_index * per_group, per_group, 0)
        scores = group_scores(query_cols, key_cols, key_mask)
        probs = jnp.where(key_mask[None, None, :], jnp.exp(scores - group_total), 0.0)
        dprobs = jnp.einsum(
            "qhd,khd->hqk",
            head_split(upstream_cols),
            head_split(value_cols),
            preferred_element_type=jnp.float32,
        )
        inner_sum = jnp.sum(probs * dprobs, axis=2, keepdims=True)
        dscores = (probs * (dprobs - inner_sum) * (1.0 / math.sqrt(HD))).astype(jnp.bfloat16)
        query_part = jnp.einsum(
            "hqk,khd->qhd", dscores, head_split(key_cols), preferred_element_type=jnp.float32
        )
        grad_query_rows = lax.dynamic_update_slice_in_dim(
            grad_query_rows, query_part.reshape(row_count, group_width), col_start, 1
        )
        delta_rows = lax.dynamic_update_slice_in_dim(
            delta_rows, inner_sum, group_index * per_group, 0
        )
        key_part = jnp.einsum(
            "hqk,qhd->khd", dscores, head_split(query_cols), preferred_element_type=jnp.float32
        )
        value_part = jnp.einsum(
            "hqk,qhd->khd",
            probs.astype(jnp.bfloat16),
            head_split(upstream_cols),
            preferred_element_type=jnp.float32,
        )
        grad_keys = lax.dynamic_update_slice_in_dim(
            grad_keys, key_part.reshape(seq_rows, group_width), col_start, 1
        )
        grad_values = lax.dynamic_update_slice_in_dim(
            grad_values, value_part.reshape(seq_rows, group_width), col_start, 1
        )
        return (grad_query_rows, grad_keys, grad_values, delta_rows)

    grad_query_rows, grad_keys, grad_values, delta_rows = lax.fori_loop(
        0,
        group_count,
        backward_group,
        (
            jnp.zeros((row_count, model_width), jnp.float32),
            jnp.zeros((seq_rows, model_width), jnp.float32),
            jnp.zeros((seq_rows, model_width), jnp.float32),
            jnp.zeros((head_count, row_count, 1), jnp.float32),
        ),
    )
    keys_summed, values_summed = (
        lax.psum_scatter(
            grad_keys.astype(jnp.bfloat16), "ctx", scatter_dimension=0, tiled=True
        ).astype(jnp.float32),
        lax.psum_scatter(
            grad_values.astype(jnp.bfloat16), "ctx", scatter_dimension=0, tiled=True
        ).astype(jnp.float32),
    )
    dquery_low = grad_query_rows.astype(jnp.bfloat16)
    dkey_low = keys_summed.astype(jnp.bfloat16)
    dvalue_low = values_summed.astype(jnp.bfloat16)
    grad_query_proj = jnp.einsum(
        "sd,se->de", tokens, dquery_low, preferred_element_type=jnp.float32
    )
    grad_query_offset = row_sum(dquery_low)
    grad_key_proj = jnp.einsum("sd,se->de", tokens, dkey_low, preferred_element_type=jnp.float32)
    grad_value_proj = jnp.einsum(
        "sd,se->de", tokens, dvalue_low, preferred_element_type=jnp.float32
    )
    grad_value_offset = row_sum(dvalue_low)
    input_total = dfirst + jnp.einsum(
        "se,de->sd", dquery_low, back_weights[0], preferred_element_type=jnp.float32
    )
    input_total = input_total + jnp.einsum(
        "se,de->sd", dkey_low, back_weights[2], preferred_element_type=jnp.float32
    )
    input_total = input_total + jnp.einsum(
        "se,de->sd", dvalue_low, back_weights[3], preferred_element_type=jnp.float32
    )
    input_grad = input_total.astype(jnp.bfloat16)
    reduced = (
        lax.psum_scatter(grad_query_proj, ("dp", "ctx"), scatter_dimension=0, tiled=True),
        lax.psum_scatter(grad_query_offset, ("dp", "ctx"), scatter_dimension=0, tiled=True),
        lax.psum_scatter(grad_key_proj, ("dp", "ctx"), scatter_dimension=0, tiled=True),
        lax.psum_scatter(grad_value_proj, ("dp", "ctx"), scatter_dimension=0, tiled=True),
        lax.psum_scatter(grad_value_offset, ("dp", "ctx"), scatter_dimension=0, tiled=True),
        lax.psum_scatter(grad_attn_proj, ("dp", "ctx"), scatter_dimension=0, tiled=True),
        lax.psum_scatter(grad_attn_offset, ("dp", "ctx"), scatter_dimension=0, tiled=True),
        lax.psum_scatter(grad_attn_gain, ("dp", "ctx"), scatter_dimension=0, tiled=True),
        lax.psum_scatter(grad_attn_shift, ("dp", "ctx"), scatter_dimension=0, tiled=True),
        lax.psum_scatter(grad_inner_proj, ("dp", "ctx"), scatter_dimension=0, tiled=True),
        lax.psum_scatter(grad_inner_offset, ("dp", "ctx"), scatter_dimension=0, tiled=True),
        lax.psum_scatter(grad_outer_proj, ("dp", "ctx"), scatter_dimension=0, tiled=True),
        lax.psum_scatter(grad_outer_offset, ("dp", "ctx"), scatter_dimension=0, tiled=True),
        lax.psum_scatter(grad_final_gain, ("dp", "ctx"), scatter_dimension=0, tiled=True),
        lax.psum_scatter(grad_final_shift, ("dp", "ctx"), scatter_dimension=0, tiled=True),
    )
    return (layer_out, input_grad) + tuple(reduced)


def solution(mesh):
    in_specs = (
        P(("dp", "ctx"), None),
        P("dp"),
        P(("dp", "ctx"), None),
        P(("dp", "ctx"), None),
        P(("dp", "ctx")),
        P(("dp", "ctx"), None),
        P(("dp", "ctx"), None),
        P(("dp", "ctx")),
        P(("dp", "ctx"), None),
        P(("dp", "ctx")),
        P(("dp", "ctx")),
        P(("dp", "ctx")),
        P(("dp", "ctx"), None),
        P(("dp", "ctx")),
        P(("dp", "ctx"), None),
        P(("dp", "ctx")),
        P(("dp", "ctx")),
        P(("dp", "ctx")),
    )
    out_specs = (
        P(("dp", "ctx"), None),
        P(("dp", "ctx"), None),
        P(("dp", "ctx"), None),
        P(("dp", "ctx")),
        P(("dp", "ctx"), None),
        P(("dp", "ctx"), None),
        P(("dp", "ctx")),
        P(("dp", "ctx"), None),
        P(("dp", "ctx")),
        P(("dp", "ctx")),
        P(("dp", "ctx")),
        P(("dp", "ctx"), None),
        P(("dp", "ctx")),
        P(("dp", "ctx"), None),
        P(("dp", "ctx")),
        P(("dp", "ctx")),
        P(("dp", "ctx")),
    )
    return jax.shard_map(local, mesh=mesh, in_specs=in_specs, out_specs=out_specs, check_vma=False)
```

profile of v0, /device:TPU:0, one launch (start us, length us, event | category | flops | bytes accessed | tf_op | source)
XLA Modules:
  0.0 2459.2 jit_solution(17513620936623403568)
XLA Ops:
  19.0 42.3 %all-reduce.18 = (bf16[1024]{0:T(1024)(128)(2,1)S(1)}, bf16[1024]{0:T(1024)(128)(2,1)S(1)}, bf16[1024]{0:T(1024)(128)(2,1)S(1)}, bf16[1024]{0:T(1024)(128)(2,1)S...) all-reduce(bf16[1024]{0:T(1024)(128)(2,1)S(1)} %dynamic-update-slic, ...), channel_id=1, replica_groups=mesh['dp'=8,'ctx'=4] {'dp','ctx'}, use_global_device_ids=true, to_apply=%add | all-reduce | flops 8192 | bytes 32768
  75.4 54.6 %all-gather.16.cloned.1.call-done = bf16[1024,1024]{1,0:T(8,128)(2,1)} async-done(((bf16[32,1024]{1,0:T(8,128)(2,1)}), bf16[1024,1024]{1,0:T(8,128)(2,1)}) %all-gather.16.cloned.1.call-update) | async-done | bytes 2097168 | tf_op jit(solution)/shard_map/all_gather | solution.py:81
  136.3 65.9 %all-gather = bf16[32,1,128]{2,1,0:T(2,128)(2,1)S(1)} all-gather(bf16[1,1,128]{2,1,0:T(2,128)(2,1)S(1)} %convert_bitcast_fusion), channel_id=1, replica_groups=mesh['dp'=8,'ctx'=4] {'dp','ctx'}, dimensions={0}, use_global_device_ids=true | all-gather | bytes 8448 | tf_op jit(solution)/shard_map/all_gather | solution.py:89
  206.9 63.6 %all-gather.12.cloned.1.call-done = bf16[2048,1024]{1,0:T(8,128)(2,1)} async-done(((bf16[512,1024]{1,0:T(8,128)(2,1)}), bf16[2048,1024]{1,0:T(8,128)(2,1)}) %all-gather.12.cloned.1.call-update) | async-done | bytes 4194320 | tf_op jit(solution)/shard_map/all_gather | solution.py:132
  277.0 74.8 %all-gather.18.cloned.1.call-done = bf16[2048,1024]{1,0:T(8,128)(2,1)} async-done(((bf16[512,1024]{1,0:T(8,128)(2,1)}), bf16[2048,1024]{1,0:T(8,128)(2,1)}) %all-gather.18.cloned.1.call-update) | async-done | bytes 4194320 | tf_op jit(solution)/shard_map/all_gather | solution.py:131
  358.4 112.5 %while.34 = (s32[]{:T(128)}, bf16[512,1024]{0,1:T(8,128)(2,1)S(1)}, f32[16,512,1]{1,0,2:T(8,128)S(1)}, bf16[2048,1024]{0,1:T(8,128)(2,1)}, bf16[512,1024]{0,1:T(...) while((s32[]{:T(128)}, bf16[512,1024]{0,1:T(8,128)(2,1)S(1)}, ...), condition=%wide.region_3.4_spmd.clone, body=%wide.region_0.3_spmd.clone.sunk | while | flops 564200448 | bytes 62693636 | solution.py:162
  475.4 14.5 all-gather.22.cloned.1.call-done
  500.4 69.0 %all-gather.24.cloned.1.call-done = bf16[4096,1024]{1,0:T(8,128)(2,1)} async-done(((bf16[128,1024]{1,0:T(8,128)(2,1)}), bf16[4096,1024]{1,0:T(8,128)(2,1)}) %all-gather.24.cloned.1.call-update) | async-done | bytes 8388624 | tf_op jit(solution)/shard_map/all_gather | solution.py:90
  582.6 12.9 convert_reduce_fusion
  613.4 353.5 %while.35 = (s32[]{:T(128)}, bf16[512,1024]{0,1:T(8,128)(2,1)}, bf16[2048,1024]{0,1:T(8,128)(2,1)}, bf16[2048,1024]{0,1:T(8,128)(2,1)}, bf16[2048,1024]{0,1:T(8,...) while((s32[]{:T(128)}, bf16[512,1024]{0,1:T(8,128)(2,1)}, ...), condition=%wide.region_14.15_spmd.clone, body=%wide.region_12.0_spmd.clone.sunk | while | flops 1373642752 | bytes 67256592 | solution.py:273
  644.4 12.7 fusion.131
  688.6 12.7 fusion.131
  732.7 12.7 fusion.131
  982.6 59.8 %reduce-scatter.15.cloned.1.call-done = bf16[512,1024]{0,1:T(8,128)(2,1)} async-done(((bf16[2048,1024]{0,1:T(8,128)(2,1)}), bf16[512,1024]{0,1:T(8,128)(2,1)}) %reduce-scatter.15.cloned.1.call-update) | async-done | bytes 1048592 | tf_op jit(solution)/shard_map/reduce_scatter | solution.py:285
  1052.6 69.3 %reduce-scatter.17.cloned.1.call-done = bf16[512,1024]{0,1:T(8,128)(2,1)} async-done(((bf16[2048,1024]{0,1:T(8,128)(2,1)}), bf16[512,1024]{0,1:T(8,128)(2,1)}) %reduce-scatter.17.cloned.1.call-update) | async-done | bytes 1048592 | tf_op jit(solution)/shard_map/reduce_scatter | solution.py:288
  1132.4 13.3 fusion.47
  1145.8 13.2 fusion.44
  1164.1 42.4 %all-reduce.17 = (f32[1024]{0:T(1024)S(1)}, f32[1024]{0:T(1024)S(1)}, f32[1024]{0:T(1024)S(1)}, f32[1024]{0:T(1024)S(1)}, f32[1024]{0:T(1024)S(1)}, /*index=5*/f...) all-reduce(f32[1024]{0:T(1024)S(1)} %convert_reduce_fusion.4, ...), channel_id=5, replica_groups=mesh['dp'=8,'ctx'=4] {'dp','ctx'}, use_global_device_ids=true, to_apply=%region_19.20.clone | all-reduce | flops 12288 | bytes 98304
  1217.4 55.7 %reduce-scatter.19.cloned.1.call-done = f32[32,1024]{1,0:T(8,128)} async-done(((f32[1024,1024]{1,0:T(8,128)}), f32[32,1024]{1,0:T(8,128)}) %reduce-scatter.19.cloned.1.call-update) | async-done | bytes 131088 | tf_op jit(solution)/shard_map/reduce_scatter | solution.py:320
  1273.1 149.7 %reduce-scatter.25.cloned.1.call-done = f32[32,1024]{1,0:T(8,128)} async-done(((f32[1024,1024]{1,0:T(8,128)}), f32[32,1024]{1,0:T(8,128)}) %reduce-scatter.25.cloned.1.call-update) | async-done | bytes 131088
  1422.8 149.5 %reduce-scatter.27.cloned.1.call-done = f32[32,1024]{1,0:T(8,128)} async-done(((f32[1024,1024]{1,0:T(8,128)}), f32[32,1024]{1,0:T(8,128)}) %reduce-scatter.27.cloned.1.call-update) | async-done | bytes 131088
  1572.3 149.3 %reduce-scatter.29.cloned.1.call-done = f32[32,1024]{1,0:T(8,128)} async-done(((f32[1024,1024]{1,0:T(8,128)}), f32[32,1024]{1,0:T(8,128)}) %reduce-scatter.29.cloned.1.call-update) | async-done | bytes 131088
  1721.7 365.6 %reduce-scatter.21.cloned.1.call-done = f32[32,4096]{1,0:T(8,128)} async-done(((f32[1024,4096]{1,0:T(8,128)}), f32[32,4096]{1,0:T(8,128)}) %reduce-scatter.21.cloned.1.call-update) | async-done | bytes 524304 | tf_op jit(solution)/shard_map/reduce_scatter | solution.py:324
  2087.3 364.9 %reduce-scatter.23.cloned.1.call-done = f32[128,1024]{1,0:T(8,128)} async-done(((f32[4096,1024]{1,0:T(8,128)}), f32[128,1024]{1,0:T(8,128)}) %reduce-scatter.23.cloned.1.call-update) | async-done | bytes 524304 | tf_op jit(solution)/shard_map/reduce_scatter | solution.py:326
  (357 shorter events, 574.2 us)
Async XLA Ops:
  7.2 63.9 %all-gather.10.cloned.1.call-start = ((), (), s32[]{:S(2)}) async-start(), calls=%async_computation.8 | async-start | bytes 2162688 | tf_op jit(solution)/shard_map/all_gather | solution.py:82
  8.8 121.2 %all-gather.16.cloned.1.call-start = ((), (), s32[]{:S(2)}) async-start(), calls=%async_computation.11 | async-start | bytes 2162688 | tf_op jit(solution)/shard_map/all_gather | solution.py:81
  10.4 192.5 %all-gather.14.cloned.1.call-start = ((), (), s32[]{:S(2)}) async-start(), calls=%async_computation.10 | async-start | bytes 2162688 | tf_op jit(solution)/shard_map/all_gather | solution.py:79
  12.0 258.4 %all-gather.12.cloned.1.call-start = ((), (), s32[]{:S(2)}) async-start(), calls=%async_computation.9 | async-start | bytes 5242880 | tf_op jit(solution)/shard_map/all_gather | solution.py:132
  61.3 68.7 %copy-start.12 = (bf16[512,1024]{1,0:T(8,128)(2,1)S(1)}, bf16[512,1024]{1,0:T(8,128)(2,1)}, u32[]{:S(2)}) copy-start(bf16[512,1024]{1,0:T(8,128)(2,1)} %param.22) | copy-start | bytes 3145732
  75.3 58.6 %copy-start.15 = (f32[32,1024]{1,0:T(8,128)S(1)}, f32[32,1024]{1,0:T(8,128)}, u32[]{:S(2)}) copy-start(f32[32,1024]{1,0:T(8,128)} %param.30) | copy-start | bytes 393220
  75.3 59.3 %copy-start.13 = (f32[32,4096]{1,0:T(8,128)S(1)}, f32[32,4096]{1,0:T(8,128)}, u32[]{:S(2)}) copy-start(f32[32,4096]{1,0:T(8,128)} %param.34) | copy-start | bytes 1572868
  75.3 60.1 %copy-start.14 = (f32[128,1024]{1,0:T(8,128)S(1)}, f32[128,1024]{1,0:T(8,128)}, u32[]{:S(2)}) copy-start(f32[128,1024]{1,0:T(8,128)} %param.36) | copy-start | bytes 1572868
  75.3 61.0 %copy-start.19 = (f32[128]{0:T(128)S(1)}, f32[128]{0:T(128)}, u32[]{:S(2)}) copy-start(f32[128]{0:T(128)} %param.35) | copy-start | bytes 1540
  75.3 276.5 %all-gather.18.cloned.1.call-start = ((), (), s32[]{:S(2)}) async-start(), calls=%async_computation.12 | async-start | bytes 5242880 | tf_op jit(solution)/shard_map/all_gather | solution.py:131
  133.8 337.1 %all-gather.20.cloned.1.call-start = ((), (), s32[]{:S(2)}) async-start(), calls=%async_computation.13 | async-start | bytes 2162688 | tf_op jit(solution)/shard_map/all_gather | solution.py:84
  134.5 355.4 %all-gather.22.cloned.1.call-start = ((), (), s32[]{:S(2)}) async-start(), calls=%async_computation.14 | async-start | bytes 8650752 | tf_op jit(solution)/shard_map/all_gather | solution.py:88
  135.3 434.1 %all-gather.24.cloned.1.call-start = ((), (), s32[]{:S(2)}) async-start(), calls=%async_computation.15 | async-start | bytes 8650752 | tf_op jit(solution)/shard_map/all_gather | solution.py:90
  136.2 906.3 %reduce-scatter.15.cloned.1.call-start = ((), (), s32[]{:S(2)}) async-start(), calls=%async_computation.16 | async-start | bytes 5242880 | tf_op jit(solution)/shard_map/reduce_scatter | solution.py:285
  475.1 120.4 %copy-start.1 = (f32[512,1024]{1,0:T(8,128)}, f32[512,1024]{1,0:T(8,128)S(1)}, u32[]{:S(2)}) copy-start(f32[512,1024]{1,0:T(8,128)S(1)} %get-tuple-element.499) | copy-start | bytes 6291460
  579.9 15.5 slice-start
  582.6 12.9 slice-start.1
  966.9 155.1 %reduce-scatter.17.cloned.1.call-start = ((), (), s32[]{:S(2)}) async-start(), calls=%async_computation.17 | async-start | bytes 5242880 | tf_op jit(solution)/shard_map/reduce_scatter | solution.py:288
  967.5 305.6 %reduce-scatter.19.cloned.1.call-start = ((), (), s32[]{:S(2)}) async-start(), calls=%async_computation.18 | async-start | bytes 4325376 | tf_op jit(solution)/shard_map/reduce_scatter | solution.py:320
  971.3 451.5 %reduce-scatter.25.cloned.1.call-start = ((), (), s32[]{:S(2)}) async-start(), calls=%async_computation.21 | async-start | bytes 4325376
  982.6 589.8 %reduce-scatter.27.cloned.1.call-start = ((), (), s32[]{:S(2)}) async-start(), calls=%async_computation.22 | async-start | bytes 4325376
  1052.6 669.1 %reduce-scatter.29.cloned.1.call-start = ((), (), s32[]{:S(2)}) async-start(), calls=%async_computation.23 | async-start | bytes 4325376
  1132.1 955.1 %reduce-scatter.21.cloned.1.call-start = ((), (), s32[]{:S(2)}) async-start(), calls=%async_computation.19 | async-start | bytes 17301504 | tf_op jit(solution)/shard_map/reduce_scatter | solution.py:324
  1145.7 1306.4 %reduce-scatter.23.cloned.1.call-start = ((), (), s32[]{:S(2)}) async-start(), calls=%async_computation.20 | async-start | bytes 17301504 | tf_op jit(solution)/shard_map/reduce_scatter | solution.py:326
  (21 other events, 84.2 us)
Sparse Core Ops, SparseCore 0:
  11.5 59.5 all-gather.9
  74.6 55.3 all-gather.15
  133.5 55.3 all-gather.13
  190.8 79.6 all-gather.11
  272.5 79.2 all-gather.17
  355.1 55.0 all-gather.19
  413.7 76.1 all-gather.21
  493.4 75.9 all-gather.23
  967.0 75.3 reduce-scatter.14
  1044.7 77.2 reduce-scatter.16
  1124.8 148.2 reduce-scatter.18
  1275.8 146.9 reduce-scatter.24
  1425.7 146.6 reduce-scatter.26
  1575.0 146.5 reduce-scatter.28
  1724.4 362.8 reduce-scatter.20
  2090.0 362.1 reduce-scatter.22
where the time goes:
time: 2470 us; the launch traced here: 2460 us
  waiting for transfers between devices  1650 us (67%)
  matrix products  463 us (19%)
  blocking collectives  151 us (6%)
  local copies, waits for them, and re-layouts  129 us (5%)
  other arithmetic  47.6 us (2%)
    unnamed x19, waiting for transfers between devices  449 us
    reduce_scatter x1, waiting for transfers between devices, local(): lax.psum_scatter(grad_inner_proj, ('dp', 'ctx'), scatter_dimension=0, til...  366 us
    reduce_scatter x1, waiting for transfers between devices, local(): lax.psum_scatter(grad_outer_proj, ('dp', 'ctx'), scatter_dimension=0, til...  365 us
    dot_general x8, matrix products, backward_group(): jnp.einsum('hqk,khd->qhd', dscores, head_split(key_cols), preferred_eleme...  101 us
    dot_general x8, matrix products, backward_group(): jnp.einsum('hqk,qhd->khd', dscores, head_split(query_cols), preferred_ele...  94.4 us
    unnamed x2, blocking collectives  84.7 us
    all_gather x1, waiting for transfers between devices, local(): lax.all_gather(keys_own, 'ctx', axis=0, tiled=True)  74.8 us
    reduce_scatter x1, waiting for transfers between devices, local(): lax.psum_scatter(grad_values.astype(jnp.bfloat16), 'ctx', scatter_dimensi...  69.3 us
  transfers between devices with their start and end apart: 16, of which 14 were waited for; matrix products, arithmetic and copies ran while one was open for 9% of the time, Pallas kernels for 0%

commit v1 on v0

v1 whole, which is shorter than its diff:
```python
import functools
import math

import jax
import jax.numpy as jnp
from jax import lax
from jax.experimental import pallas as pl
from jax.experimental.pallas import tpu as pltpu
from jax.sharding import PartitionSpec as P

HD = 64
AXES = ("dp", "ctx")
norm_eps = 1e-05
score_scale = 1.0 / math.sqrt(HD)
score_scale_two = score_scale * math.log2(math.e)
f32 = jnp.float32
bf16 = jnp.bfloat16


def attention_forward_kernel(
    length_ref, q_ref, k_ref, v_ref, mixed_ref, lse_ref, keys_t_ref, *, heads, rows
):
    width = k_ref.shape[1]
    seq = keys_t_ref.shape[1]

    @pl.when(pl.program_id(0) == 0)
    def _():
        keys_t_ref[...] = k_ref[...].T

    queries = q_ref[...]
    keys_t = keys_t_ref[...]
    values = v_ref[...]
    key_pos = lax.broadcasted_iota(jnp.int32, (1, seq), 1)
    bias = jnp.where(key_pos < length_ref[0], 0.0, -1e30).astype(f32)
    head_of = lax.broadcasted_iota(jnp.int32, (rows, width), 1) // HD
    lane = lax.broadcasted_iota(jnp.int32, (rows, 128), 1)
    mixed = jnp.zeros((rows, width), f32)
    lse = jnp.zeros((rows, 128), f32)
    for head in range(heads):
        own = jnp.where(head_of == head, queries, jnp.zeros_like(queries))
        scores = jnp.dot(own, keys_t, preferred_element_type=f32) * score_scale_two + bias
        top = jnp.max(scores, axis=1, keepdims=True)
        probs = jnp.exp2(scores - top)
        total = jnp.sum(probs, axis=1, keepdims=True)
        part = jnp.dot(probs.astype(bf16), values, preferred_element_type=f32)
        mixed = jnp.where(head_of == head, part * (1.0 / total), mixed)
        lse = jnp.where(lane == head, top + jnp.log2(total), lse)
    mixed_ref[...] = mixed.astype(bf16)
    lse_ref[...] = lse.T[:8]


def attention_forward(qkv, length, seq, rows=512):
    width = qkv.shape[1] // 3
    heads = width // HD
    return pl.pallas_call(
        functools.partial(attention_forward_kernel, heads=heads, rows=rows),
        grid=(seq // rows,),
        in_specs=[
            pl.BlockSpec(memory_space=pltpu.SMEM),
            pl.BlockSpec((rows, width), lambda i: (i, 0)),
            pl.BlockSpec((seq, width), lambda i: (0, 1)),
            pl.BlockSpec((seq, width), lambda i: (0, 2)),
        ],
        out_specs=[
            pl.BlockSpec((rows, width), lambda i: (i, 0)),
            pl.BlockSpec((8, rows), lambda i: (0, i)),
        ],
        out_shape=[
            jax.ShapeDtypeStruct((seq, width), bf16),
            jax.ShapeDtypeStruct((8, seq), f32),
        ],
        scratch_shapes=[pltpu.VMEM((width, seq), bf16)],
        compiler_params=pltpu.CompilerParams(vmem_limit_bytes=56 * 2**20),
        cost_estimate=pl.CostEstimate(
            flops=16 * seq * seq * width,
            bytes_accessed=8 * seq * width,
            transcendentals=seq * seq * heads,
        ),
        name="attention_forward",
    )(length, qkv, qkv, qkv)


def attention_backward_kernel(
    length_ref,
    q_ref,
    k_ref,
    v_ref,
    mixed_ref,
    dmixed_ref,
    lse_ref,
    dq_ref,
    dk_ref,
    dv_ref,
    keys_t_ref,
    dk_sum,
    dv_sum,
    *,
    heads,
    rows,
    depth,
):
    step = pl.program_id(0)
    seq, width = dk_sum.shape

    @pl.when(step == 0)
    def _():
        keys_t_ref[...] = k_ref[...].T
        dk_sum[...] = jnp.zeros_like(dk_sum)
        dv_sum[...] = jnp.zeros_like(dv_sum)

    queries, dmixed = q_ref[...], dmixed_ref[...]
    queries_t, dmixed_t, mixed_t = queries.T, dmixed.T, mixed_ref[...].T
    product = dmixed_t.astype(f32) * mixed_t.astype(f32)
    lane_head = lax.broadcasted_iota(jnp.int32, (rows, width), 1) // HD
    row_head = lax.broadcasted_iota(jnp.int32, (width, rows), 0) // HD
    none, none_t = jnp.zeros_like(queries), jnp.zeros_like(queries_t)
    lse = lse_ref[...]
    per_head = []
    for head in range(heads):
        per_head.append(
            (
                jnp.where(row_head == head, queries_t, none_t),
                jnp.where(row_head == head, dmixed_t, none_t),
                jnp.where(lane_head == head, queries, none),
                jnp.where(lane_head == head, dmixed, none),
                jnp.sum(product[HD * head : HD * head + HD], axis=0, keepdims=True),
                lse[head : head + 1],
            )
        )
    length = length_ref[0]

    def chunk(index, dq_t):
        span = pl.ds(pl.multiple_of(index * depth, depth), depth)
        keys, values = k_ref[span, :], v_ref[span, :]
        key_pos = index * depth + lax.broadcasted_iota(jnp.int32, (depth, 1), 0)
        bias = jnp.where(key_pos < length, 0.0, -1e30).astype(f32)
        dk, dv = dk_sum[span, :], dv_sum[span, :]
        new_dq_t = []
        for head in range(heads):
            own_q_t, own_do_t, own_q, own_do, delta, own_lse = per_head[head]
            scores = jnp.dot(keys, own_q_t, preferred_element_type=f32)
            probs = jnp.exp2(scores * score_scale_two + bias - own_lse)
            dprobs = jnp.dot(values, own_do_t, preferred_element_type=f32)
            dscores = (probs * (dprobs - delta)).astype(bf16)
            dv = dv + jnp.dot(probs.astype(bf16), own_do, preferred_element_type=f32)
            dk = dk + jnp.dot(dscores, own_q, preferred_element_type=f32)
            own_keys_t = keys_t_ref[HD * head : HD * head + HD, span]
            new_dq_t.append(
                dq_t[head] + jnp.dot(own_keys_t, dscores, preferred_element_type=f32)
            )
        dk_sum[span, :] = dk
        dv_sum[span, :] = dv
        return tuple(new_dq_t)

    start = tuple(jnp.zeros((HD, rows), f32) for _ in range(heads))
    dq_t = jnp.concatenate(lax.fori_loop(0, seq // depth, chunk, start), axis=0)
    dq_ref[...] = (dq_t * score_scale).T.astype(bf16)

    @pl.when(step == pl.num_programs(0) - 1)
    def _():
        dk_ref[...] = (dk_sum[...] * score_scale).astype(bf16)
        dv_ref[...] = dv_sum[...].astype(bf16)


def attention_backward(qkv, mixed, dmixed, lse, length, rows=512, depth=512):
    seq, width = mixed.shape
    heads = width // HD
    block = pl.BlockSpec((rows, width), lambda i: (i, 0))
    whole = pl.BlockSpec((seq, width), lambda i: (0, 0))
    return pl.pallas_call(
        functools.partial(attention_backward_kernel, heads=heads, rows=rows, depth=depth),
        grid=(seq // rows,),
        in_specs=[
            pl.BlockSpec(memory_space=pltpu.SMEM),
            block,
            pl.BlockSpec((seq, width), lambda i: (0, 1)),
            pl.BlockSpec((seq, width), lambda i: (0, 2)),
            block,
            block,
            pl.BlockSpec((8, rows), lambda i: (0, i)),
        ],
        out_specs=[block, whole, whole],
        out_shape=[jax.ShapeDtypeStruct((seq, width), bf16)] * 3,
        scratch_shapes=[
            pltpu.VMEM((width, seq), bf16),
            pltpu.VMEM((seq, width), f32),
            pltpu.VMEM((seq, width), f32),
        ],
        compiler_params=pltpu.CompilerParams(vmem_limit_bytes=56 * 2**20),
        cost_estimate=pl.CostEstimate(
            flops=40 * seq * seq * width,
            bytes_accessed=16 * seq * width,
            transcendentals=seq * seq * heads,
        ),
        name="attention_backward",
    )(length, qkv, qkv, qkv, mixed, dmixed, lse)


def device_index():
    return lax.axis_index("dp") * lax.axis_size("ctx") + lax.axis_index("ctx")


def bits_of(count):
    return count.bit_length() - 1


def swap(values, bit):
    count = lax.axis_size("dp") * lax.axis_size("ctx")
    return lax.ppermute(values, AXES, [(i, i ^ (1 << bit)) for i in range(count)])


def own_bit(bit):
    return (device_index() >> bit) & 1


def scatter_step(terms, axis, bit, out_dtype=bf16):
    mine = own_bit(bit)
    received = swap(lax.dynamic_index_in_dim(terms, 1 - mine, axis, keepdims=False), bit)
    kept = lax.dynamic_index_in_dim(terms, mine, axis, keepdims=False)
    return (kept.astype(f32) + received.astype(f32)).astype(out_dtype)


def scatter_sum(terms, bit_order, out_dtype=bf16):
    left = sorted(bit_order, reverse=True)
    for turn, bit in enumerate(bit_order):
        last = turn == len(bit_order) - 1
        terms = scatter_step(terms, left.index(bit), bit, out_dtype if last else terms.dtype)
        left.remove(bit)
    return terms


def gather_dp(shard):
    low = bits_of(lax.axis_size("ctx"))
    high = low + bits_of(lax.axis_size("dp"))
    for turn, bit in enumerate(range(high - 1, low - 1, -1)):
        other = swap(shard, bit)
        shard = jnp.where(
            own_bit(bit) == 1,
            jnp.stack([other, shard], axis=turn),
            jnp.stack([shard, other], axis=turn),
        )
    return shard.reshape((lax.axis_size("dp"),) + shard.shape[high - low :])


def gather_line(block):
    count = lax.axis_size("ctx")
    place = lax.axis_index("ctx")
    held = jnp.zeros((count + 1,) + block.shape, block.dtype)
    held = lax.dynamic_update_index_in_dim(held, block, place, 0)
    from_left = from_right = block
    for step in range(1, count):
        from_left = lax.ppermute(from_left, "ctx", [(i, i + 1) for i in range(count - 1)])
        from_right = lax.ppermute(from_right, "ctx", [(i + 1, i) for i in range(count - 1)])
        left_slot = jnp.where(place >= step, place - step, count)
        right_slot = jnp.where(place + step < count, place + step, count)
        held = lax.dynamic_update_index_in_dim(held, from_left, left_slot, 0)
        held = lax.dynamic_update_index_in_dim(held, from_right, right_slot, 0)
    return held.reshape(((count + 1) * block.shape[0],) + block.shape[1:])


def layer_norm(residual, norm_gain, norm_shift):
    centered = residual - jnp.mean(residual, axis=1, keepdims=True)
    inverse = lax.rsqrt(jnp.mean(centered * centered, axis=1, keepdims=True) + norm_eps)
    normed = centered * inverse
    return (normed * norm_gain + norm_shift, normed, inverse)


def layer_norm_back(upstream, normed, inverse, norm_gain):
    scaled = upstream * norm_gain
    first_mean = jnp.mean(scaled, axis=1, keepdims=True)
    second_mean = jnp.mean(scaled * normed, axis=1, keepdims=True)
    return inverse * (scaled - first_mean - normed * second_mean)


def gelu_value(pre_act):
    return 0.5 * pre_act * (1.0 + lax.erf(pre_act * (1.0 / math.sqrt(2.0))))


def gelu_slope(pre_act):
    normal_cdf = 0.5 * (1.0 + lax.erf(pre_act * (1.0 / math.sqrt(2.0))))
    return normal_cdf + pre_act * jnp.exp(-0.5 * pre_act * pre_act) * (
        1.0 / math.sqrt(2.0 * math.pi)
    )


def row_sum(values):
    return jnp.sum(values.astype(f32), axis=0)


def local(
    tokens,
    lengths,
    cotangent,
    query_proj,
    query_offset,
    key_proj,
    value_proj,
    value_offset,
    attn_proj,
    attn_offset,
    attn_gain,
    attn_shift,
    inner_proj,
    inner_offset,
    outer_proj,
    outer_offset,
    final_gain,
    final_shift,
):
    n_dp, n_ctx = lax.axis_size("dp"), lax.axis_size("ctx")
    n_dev = n_dp * n_ctx
    dev_bits = bits_of(n_dev)
    ctx_bits = bits_of(n_ctx)
    rows, width = tokens.shape
    seq = rows * n_ctx
    group = width // n_ctx
    part = width // n_dev
    hidden_width = inner_proj.shape[1]
    hidden_part = hidden_width // n_dev
    columns = hidden_width // width
    place = lax.axis_index("ctx")

    vectors = jnp.concatenate(
        [
            query_offset,
            value_offset,
            attn_offset,
            attn_gain,
            attn_shift,
            outer_offset,
            final_gain,
            final_shift,
            inner_offset,
        ]
    ).astype(bf16)
    triple = jnp.stack([query_proj, key_proj, value_proj], axis=1).astype(bf16)
    by_group = triple.reshape(part, 3, n_ctx, group).transpose(2, 0, 1, 3)
    by_group = by_group.reshape(n_ctx, part, 3 * group)
    vector_rows = -(-vectors.shape[0] // (3 * group))
    vectors = jnp.pad(vectors, (0, vector_rows * 3 * group - vectors.shape[0]))
    vectors = vectors.reshape(vector_rows, 3 * group)
    vectors = jnp.pad(vectors, ((0, 16 - vector_rows), (0, 0)))
    packed = jnp.concatenate(
        [by_group, jnp.broadcast_to(vectors[None], (n_ctx,) + vectors.shape)], axis=1
    )
    packed = gather_dp(lax.all_to_all(packed, "ctx", 0, 0, tiled=True))
    w_group = packed[:, :, :part].reshape(width, 3 * group)
    vectors = packed[:, :, part : part + vector_rows].reshape(n_dev, -1)
    names = [vectors[:, i * part : (i + 1) * part].reshape(width).astype(f32) for i in range(8)]
    b_query, b_value, b_attn, g_attn, s_attn, b_outer, g_final, s_final = names
    b_inner = vectors[:, 8 * part : 8 * part + hidden_part].reshape(hidden_width).astype(f32)

    inner_rows = [
        inner_proj[:, j * width : (j + 1) * width] for j in range(columns)
    ]
    shard = jnp.concatenate([attn_proj] + inner_rows + [outer_proj], axis=0).astype(bf16)
    gathered = lax.all_gather(shard, AXES, axis=0, tiled=False)
    w_attn = gathered[:, :part].reshape(width, width)
    w_inner = jnp.concatenate(
        [
            gathered[:, part * (1 + j) : part * (2 + j)].reshape(width, width)
            for j in range(columns)
        ],
        axis=1,
    )
    w_outer = gathered[:, part * (1 + columns) :].reshape(hidden_width, width)

    tokens_all = gather_line(tokens)
    b_group = lax.dynamic_slice_in_dim(
        jnp.stack([b_query, jnp.zeros_like(b_query), b_value]), place * group, group, 1
    ).reshape(3 * group)
    qkv = (jnp.dot(tokens_all, w_group, preferred_element_type=f32) + b_group).astype(bf16)
    mixed_group, lse = attention_forward(qkv, lengths, seq)
    mixed = lax.all_to_all(mixed_group.reshape(n_ctx, rows, group), "ctx", 0, 0, tiled=True)
    mixed = mixed.transpose(1, 0, 2).reshape(rows, width)

    row_valid = place * rows + jnp.arange(rows, dtype=jnp.int32) < lengths[0]
    row_weight = row_valid.astype(f32)[:, None]
    first_res = (
        tokens.astype(f32) + jnp.dot(mixed, w_attn, preferred_element_type=f32) + b_attn
    )
    hidden, normed_one, inverse_one = layer_norm(first_res, g_attn, s_attn)
    hidden_low = hidden.astype(bf16)
    pre_act = jnp.dot(hidden_low, w_inner, preferred_element_type=f32) + b_inner
    activated = gelu_value(pre_act).astype(bf16)
    second_res = hidden + jnp.dot(activated, w_outer, preferred_element_type=f32) + b_outer
    final, normed_two, inverse_two = layer_norm(second_res, g_final, s_final)
    layer_out = (final * row_weight).astype(bf16)

    upstream = cotangent.astype(f32) * row_weight
    grad_final_shift = jnp.sum(upstream, axis=0)
    grad_final_gain = jnp.sum(upstream * normed_two, axis=0)
    dsecond = layer_norm_back(upstream, normed_two, inverse_two, g_final)
    douter = dsecond.astype(bf16)
    grad_outer_offset = row_sum(douter)
    dactivated = jnp.einsum("sd,fd->sf", douter, w_outer, preferred_element_type=f32)
    dpre_act = (dactivated * gelu_slope(pre_act)).astype(bf16)
    grad_inner_offset = row_sum(dpre_act)
    dhidden = dsecond + jnp.einsum("sf,df->sd", dpre_act, w_inner, preferred_element_type=f32)
    grad_attn_shift = jnp.sum(dhidden, axis=0)
    grad_attn_gain = jnp.sum(dhidden * normed_one, axis=0)
    dfirst = layer_norm_back(dhidden, normed_one, inverse_one, g_attn)
    dattn = dfirst.astype(bf16)
    grad_attn_offset = row_sum(dattn)
    dmixed = jnp.einsum("se,de->sd", dattn, w_attn, preferred_element_type=f32).astype(bf16)

    dmixed_group = lax.all_to_all(
        dmixed.reshape(rows, n_ctx, group).transpose(1, 0, 2), "ctx", 0, 0, tiled=True
    ).reshape(seq, group)

    bits = (2,) * dev_bits
    order = list(range(ctx_bits, dev_bits)) + list(range(ctx_bits))
    swapped = order[:]
    if len(order) > 2 and dev_bits - ctx_bits > 2:
        swapped[1], swapped[2] = swapped[2], swapped[1]
    grad_outer = jnp.einsum("sf,sd->fd", activated, douter, preferred_element_type=f32)
    grad_outer = scatter_sum(
        grad_outer.astype(bf16).reshape(bits + (hidden_part, width)), order, f32
    )
    grad_inner = jnp.einsum("sd,sf->df", hidden_low, dpre_act, preferred_element_type=f32)
    grad_inner = scatter_sum(
        grad_inner.astype(bf16).reshape(bits + (part, hidden_width)), swapped, f32
    )
    grad_attn = jnp.einsum("sd,se->de", mixed, dattn, preferred_element_type=f32)
    grad_attn = scatter_sum(grad_attn.astype(bf16).reshape(bits + (part, width)), order, f32)
    early = [
        grad_attn_offset,
        grad_attn_gain,
        grad_attn_shift,
        grad_outer_offset,
        grad_final_gain,
        grad_final_shift,
        grad_inner_offset,
    ]
    early = jnp.concatenate([v.reshape(n_dev, -1) for v in early], axis=1)
    early = scatter_sum(early.reshape(bits + (1, early.shape[1])), order, f32).reshape(-1)

    dq, dk, dv = attention_backward(qkv, mixed_group, dmixed_group, lse, lengths)
    dqkv = jnp.concatenate([dq, dk, dv], axis=1)
    grad_triple = jnp.einsum(
        "sd,se->de", tokens_all[:seq], dqkv, preferred_element_type=f32
    ).astype(bf16)
    dp_order = order[: dev_bits - ctx_bits]
    grad_triple = grad_triple.reshape((2,) * len(dp_order) + (n_ctx * part, 3 * group))
    left = sorted(dp_order, reverse=True)
    for bit in dp_order:
        grad_triple = scatter_step(grad_triple, left.index(bit), bit)
        left.remove(bit)
    grad_triple = lax.all_to_all(
        grad_triple.reshape(n_ctx, part, 3 * group), "ctx", 0, 0, tiled=True
    )
    grad_triple = grad_triple.reshape(n_ctx, part, 3, group).transpose(2, 1, 0, 3)
    grad_triple = grad_triple.reshape(3, part, width).astype(f32)
    late = jnp.stack([row_sum(dq), row_sum(dv)])
    late = lax.dynamic_update_slice_in_dim(
        jnp.zeros((2, width), f32), late, place * group, 1
    )
    late = late.reshape(2, n_dev, part).transpose(1, 0, 2).reshape(bits + (1, 2 * part))
    late = scatter_sum(late, order, f32).reshape(2, part)

    dqkv_rows = lax.all_to_all(dqkv.reshape(n_ctx, rows, 3 * group), "ctx", 0, 0, tiled=True)
    w_triple = lax.all_gather(
        by_group.transpose(1, 0, 2).reshape(part, 3 * width), AXES, axis=0, tiled=True
    )
    dqkv_rows = dqkv_rows.transpose(1, 0, 2).reshape(rows, 3 * width)
    input_grad = (
        dfirst + jnp.einsum("se,de->sd", dqkv_rows, w_triple, preferred_element_type=f32)
    ).astype(bf16)

    pieces = [early[i * part : (i + 1) * part] for i in range(6)]
    return (
        layer_out,
        input_grad,
        grad_triple[0],
        late[0],
        grad_triple[1],
        grad_triple[2],
        late[1],
        grad_attn,
        pieces[0],
        pieces[1],
        pieces[2],
        grad_inner,
        early[6 * part :],
        grad_outer,
        pieces[3],
        pieces[4],
        pieces[5],
    )


def solution(mesh):
    rows, vector = P(AXES, None), P(AXES)
    in_specs = (rows, P("dp"), rows, rows, vector, rows, rows, vector, rows) + (vector,) * 3
    in_specs += (rows, vector, rows) + (vector,) * 3
    out_specs = (rows,) * 3 + (vector, rows, rows, vector, rows) + (vector,) * 3
    out_specs += (rows, vector, rows) + (vector,) * 3
    return jax.shard_map(local, mesh=mesh, in_specs=in_specs, out_specs=out_specs, check_vma=False)
```

time: 2470 us -> 689 us (0.28)
  waiting for transfers between devices: 1650 us -> 241 us
  matrix products: 463 us -> 87.4 us
  blocking collectives: 151 us -> 39 us
  Pallas kernels: 0 us -> 83.6 us
  starting transfers between devices: 0.91 us -> 75.9 us
  local copies, waits for them, and re-layouts: 129 us -> 95.5 us
    reduce_scatter x5 -> x0, waiting for transfers between devices: 915 us -> none  [the longest x1 366 us: local(): lax.psum_scatter(grad_inner_proj, ('dp', 'ctx'), scatter_dimension=0, til...]
    unnamed x19 -> x2, waiting for transfers between devices: 449 us -> 0.03 us
    dot_general x74 -> x12, matrix products: 463 us -> 87.4 us  [the longest x1 12.8 us: local(): pre_act = jnp.dot(hidden_low, w_inner, preferred_element_type=f32) + b_inner]
    all_gather x8 -> x2, waiting for transfers between devices: 286 us -> 0.01 us  [the longest x1 0.01 us: local(): gathered = lax.all_gather(shard, AXES, axis=0, tiled=False)]
    ppermute x0 -> x37, waiting for transfers between devices: none -> 226 us  [the longest x31 153 us: swap(): return lax.ppermute(values, AXES, [(i, i ^ 1 << bit) for i in range(count)])]
    unnamed x2 -> x0, blocking collectives: 84.7 us -> none
    pallas_call x0 -> x2, Pallas kernels: none -> 83.6 us  [the longest x1 52.2 us: attention_backward(): pl.pallas_call(functools.partial(attention_backward_kernel, heads=heads,...]
    all_gather x1 -> x0, blocking collectives: 65.9 us -> none  [local(): lax.all_gather(inner_offset.astype(jnp.bfloat16), ('dp', 'ctx'), axis=0,...]
  transfers between devices with their start and end apart: 16 -> 43, of which waited for: 14 -> 17; matrix products, arithmetic and copies ran while one was open for 9% -> 31% of each run, Pallas kernels for 0% -> 12%
where the time goes in v1:
time: 689 us; the launch traced here: 683 us
  waiting for transfers between devices  241 us (35%)
  local copies, waits for them, and re-layouts  95.5 us (14%)
  matrix products  87.4 us (13%)
  Pallas kernels  83.6 us (12%)
  starting transfers between devices  75.9 us (11%)
  other arithmetic  45.2 us (7%)
  blocking collectives  39 us (6%)
  between operations  16.2 us (2%)
    ppermute x31, waiting for transfers between devices, swap(): return lax.ppermute(values, AXES, [(i, i ^ 1 << bit) for i in range(count)])  153 us
    pallas_call x1, Pallas kernels, attention_backward(): pl.pallas_call(functools.partial(attention_backward_kernel, heads=heads,...  52.2 us
    all_to_all x1, blocking collectives, local(): packed = gather_dp(lax.all_to_all(packed, 'ctx', 0, 0, tiled=True))  39 us
    ppermute x3, waiting for transfers between devices, gather_line(): lax.ppermute(from_right, 'ctx', [(i + 1, i) for i in range(count - 1)])  38 us
    ppermute x3, waiting for transfers between devices, gather_line(): lax.ppermute(from_left, 'ctx', [(i, i + 1) for i in range(count - 1)])  34.7 us
    ppermute x31, starting transfers between devices, swap(): return lax.ppermute(values, AXES, [(i, i ^ 1 << bit) for i in range(count)])  34.4 us
    pallas_call x1, Pallas kernels, attention_forward(): pl.pallas_call(functools.partial(attention_forward_kernel, heads=heads, r...  31.5 us
    convert_element_type x15, other arithmetic, scatter_step(): return (kept.astype(f32) + received.astype(f32)).astype(out_dtype)  23.5 us
  transfers between devices with their start and end apart: 43, of which 17 were waited for; matrix products, arithmetic and copies ran while one was open for 31% of the time, Pallas kernels for 12%

profile of v1, /device:TPU:0, one launch (start us, length us, event | category | flops | bytes accessed | tf_op | source)
XLA Modules:
  0.0 683.5 jit_solution(7578918398164897378)
XLA Ops:
  12.7 6.5 collective-permute-start
  20.8 39.0 %all_to_all.25 = bf16[4,48,768]{2,1,0:T(8,128)(2,1)S(1)} all-to-all(bf16[4,48,768]{2,1,0:T(8,128)(2,1)S(1)} %pad_maximum_fusion.3), channel_id=1, replica_groups=mesh['dp'=8,'ctx'=4] {'ctx'}, dimensions={0} | all-to-all | bytes 589824 | tf_op jit(solution)/shard_map/all_to_all | solution.py:346
  61.3 12.8 %collective-permute-done.6 = bf16[4,48,768]{2,1,0:T(8,128)(2,1)S(1)} collective-permute-done((bf16[4,48,768]{2,1,0:T(8,128)(2,1)S(1)}, bf16[4,48,768]{2,1,0:T(8,128)(2,1)S(1)}, u32[]{:S(2)}, u32[]{:S(2)}) %collective-permute-start.6) | collective-permute-done | bytes 294944 | tf_op jit(solution)/shard_map/ppermute | solution.py:209
  94.2 32.5 %collective-permute-done.3 = bf16[512,1024]{1,0:T(8,128)(2,1)} collective-permute-done((bf16[512,1024]{1,0:T(8,128)(2,1)}, bf16[512,1024]{1,0:T(8,128)(2,1)}, u32[]{:S(2)}, u32[]{:S(2)}) %collective-permute-start.3) | collective-permute-done | bytes 1048608 | tf_op jit(solution)/shard_map/ppermute | solution.py:253
  139.8 34.7 %collective-permute-done.4 = bf16[512,1024]{1,0:T(8,128)(2,1)} collective-permute-done((bf16[512,1024]{1,0:T(8,128)(2,1)}, bf16[512,1024]{1,0:T(8,128)(2,1)}, u32[]{:S(2)}, u32[]{:S(2)}) %collective-permute-start.4) | collective-permute-done | bytes 1048608 | tf_op jit(solution)/shard_map/ppermute | solution.py:252
  184.5 8.3 %add_convert_fusion.q_ref.k_ref.v_ref = bf16[2560,768]{1,0:T(8,128)(2,1)} fusion(bf16[2560,1024]{1,0:T(8,128)(2,1)} %bitcast.7, bf16[1024,768]{1,0:T(8,128)(2,1)S(1)} %bitcast.320, f32[768]{0:T(1024)S(1)} %add.378), kind=kOutput, calls=%fused_computation.15 | convolution fusion | flops 4030464000 | bytes 10750976 | tf_op jit(solution)/shard_map/dot_general | solution.py:372
  192.8 31.5 %attention_forward.1 = (bf16[2048,256]{1,0:T(8,128)(2,1)}, f32[8,2048]{1,0:T(8,128)}) custom-call(s32[1]{0:T(128)} %copy.161.length_ref, bf16[2560,768]{1,0:T(8,128)(2,1)} %add_convert_fusion.q_ref.k_ref.v_ref, bf16[2560,768]{1,0:T(8,128)(2,1)} %add_convert_fusion.q_ref.k_ref.v_ref, bf16[2560,768]{1,0:T(8,128)(2,1)} %add_convert_fusion.q_ref.k_ref.v_ref), custom_call_target="tpu_custom_call" | custom-call | flops 17179869184 | bytes 4194304 | tf_op jit(solution)/shard_map/attention_forward/pallas_call | solution.py:55
  226.5 7.2 %all-to-all-start.1 = ((bf16[4,512,256]{1,2,0:T(8,128)(2,1)}), bf16[4,512,256]{1,2,0:T(8,128)(2,1)S(1)}, u32[]{:S(2)}, u32[]{:S(2)}) async-start(bf16[4,512,256]{1,2,0:T(8,128)(2,1)} %copy.106), calls=%async_computation.1 | async-start | bytes 2097152 | tf_op jit(solution)/shard_map/all_to_all | solution.py:374
  240.1 7.7 %fusion.68 = (bf16[32,32,1024]{2,1,0:T(8,128)(2,1)}, bf16[32,32,1024]{2,1,0:T(8,128)(2,1)}, bf16[32,32,1024]{2,1,0:T(8,128)(2,1)}, bf16[32,32,1024]{2,1,0:T(8,128)(2,1)}, bf16[32,32,1024]{2,1,0:T(8,128)(2,1)}) fusion(bf16[32,288,1024]{2,1,0:T(8,128)(2,1)} %all-gather.3.cloned.1.call-done), kind=kLoop, calls=%fused_computation.219 | loop fusion | bytes 20971520 | tf_op jit(solution)/shard_map/slice | solution.py:358
  247.8 14.6 %all-to-all-done.1 = bf16[4,512,256]{1,2,0:T(8,128)(2,1)S(1)} async-done(((bf16[4,512,256]{1,2,0:T(8,128)(2,1)}), bf16[4,512,256]{1,2,0:T(8,128)(2,1)S(1)}, u32[]{:S(2)}, u32[]{:S(2)}) %all-to-all-start.1) | async-done | bytes 1048608 | tf_op jit(solution)/shard_map/all_to_all | solution.py:374
  268.6 12.8 %multiply_convert_fusion = (bf16[512,4096]{1,0:T(8,128)(2,1)}, f32[512,4096]{1,0:T(8,128)}) fusion(f32[4096]{0:T(1024)S(1)} %fusion.38, bf16[1024,1024]{1,0:T(8,128)(2,1)S(1)} %bitcast.307, bf16[1024,1024]{1,0:T(8,128)(2,1)S(1)} %bitcast.309, bf16[1024,1024]{1,0:T(8,128)(2,1)S(1)} %bitcast.311, bf16[1024,1024]{1,0:T(8,128)(2,1)} %bitcast.313, ...), kind=kOutput, calls=%fused_computation.13 | convolution fusion | flops 4343726080 | bytes 23097344 | tf_op jit(solution)/shard_map/dot_general | solution.py:384
  281.4 8.6 %slice.194 = bf16[32,128,1024]{2,1,0:T(8,128)(2,1)} slice(bf16[32,288,1024]{2,1,0:T(8,128)(2,1)} %all-gather.3.cloned.1.call-done), slice={[0:32], [160:288], [0:1024]} | slice | bytes 16777216 | tf_op jit(solution)/shard_map/slice | solution.py:366
  290.1 8.5 %fusion.71 = (f32[512]{0:T(512)S(1)}, f32[512,1024]{1,0:T(8,128)S(1)}) fusion(f32[1024]{0:T(1024)S(1)} %reshape.631, bf16[512,4096]{1,0:T(8,128)(2,1)} %get-tuple-element.76, bf16[4096,1024]{1,0:T(8,128)(2,1)} %bitcast.295, f32[1024]{0:T(1024)S(1)} %reshape.629, f32[1024]{0:T(1024)S(1)} %reshape.628, f32[512]{0:T(512)S(1)} %add_rsqrt_fusion.1, ...), kind=kOutput, calls=%fused_computation.222 | convolution fusion | flops 4298636800 | bytes 16795648 | tf_op jit(solution)/shard_map/dot_general | solution.py:386
  304.3 11.4 %convert_reduce_fusion = (f32[4096]{0:T(1024)S(1)}, bf16[512,4096]{1,0:T(8,128)(2,1)}) fusion(f32[512,4096]{1,0:T(8,128)} %get-tuple-element.77, f32[4096]{0:T(1024)S(1)} %fusion.38, bf16[4096,1024]{1,0:T(8,128)(2,1)S(1)} %bitcast.296, f32[512,1024]{1,0:T(8,128)} %get-tuple-element.36), kind=kOutput, calls=%fused_computation.12 | convolution fusion | flops 4322750464 | bytes 23101440 | tf_op jit(solution)/shard_map/sd,fd->sf/dot_general | solution.py:396
  315.8 9.7 %multiply_reduce_fusion.1 = (f32[1024]{0:T(1024)S(1)}, f32[512]{0:T(512)S(1)}, f32[512]{0:T(512)S(1)}, f32[1024]{0:T(1024)S(1)}, f32[512,1024]{1,0:T(8,128)}) fusion(f32[512,1024]{1,0:T(8,128)S(1)} %get-tuple-element.75, f32[512]{0:T(512)S(1)} %add_rsqrt_fusion.1, f32[512]{0:T(512)S(1)} %broadcast_multiply_fusion.5, f32[1024]{0:T(1024)S(1)} %reshape.628, ...), kind=kOutput, calls=%fused_computation.37 | convolution fusion | flops 4333761536 | bytes 18894848 | tf_op jit(solution)/shard_map/sf,df->sd/dot_general | solution.py:399
  325.5 9.4 %convolution_convert_fusion.1 = bf16[1024,4096]{1,0:T(8,128)(2,1)} fusion(bf16[512,4096]{1,0:T(8,128)(2,1)} %get-tuple-element.82, f32[512,1024]{1,0:T(8,128)S(1)} %get-tuple-element.75, f32[1024]{0:T(1024)S(1)} %reshape.629, f32[1024]{0:T(1024)S(1)} %reshape.628, f32[512]{0:T(512)S(1)} %add_rsqrt_fusion.1, f32[512]{0:T(512)S(1)} %broadcast_multiply_fusion.5), kind=kOutput, calls=%fused_computation.17 | convolution fusion | flops 4301783040 | bytes 14692352 | tf_op jit(solution)/shard_map/sd,sf->df/dot_general | solution.py:420
  334.9 7.1 %convolution_convert_fusion = bf16[4096,1024]{1,0:T(8,128)(2,1)} fusion(bf16[512,4096]{1,0:T(8,128)(2,1)S(1)} %copy-done.40, f32[512,1024]{1,0:T(8,128)S(1)} %copy-done.23), kind=kOutput, calls=%fused_computation.16 | convolution fusion | flops 4299685888 | bytes 14680064 | tf_op jit(solution)/shard_map/sf,sd->fd/dot_general | solution.py:416
  379.7 6.9 %constant_dynamic-slice_fusion.2 = (bf16[2,2,1,2,2,128,1024]{6,5,4,3,2,1,0:T(8,128)(2,1)}, bf16[2,2,1,2,2,128,1024]{6,5,4,3,2,1,0:T(8,128)(2,1)S(1)}) fusion(bf16[2,2,2,2,2,128,1024]{6,5,4,3,2,1,0:T(8,128)(2,1)} %bitcast.293, s32[]{:T(128)S(6)} %select_n.233, s32[]{:T(128)S(6)} %select_n.234), kind=kLoop, calls=%fused_computation.133 | loop fusion | bytes 16777224 | tf_op jit(solution)/shard_map/jit(dynamic_index_in_dim)/dynamic_slice | solution.py:219
  397.5 52.2 %attention_backward.1 = (bf16[2048,256]{1,0:T(8,128)(2,1)}, bf16[2048,256]{1,0:T(8,128)(2,1)}, bf16[2048,256]{1,0:T(8,128)(2,1)}) custom-call(s32[1]{0:T(128)} %copy.161.length_ref, bf16[2560,768]{1,0:T(8,128)(2,1)} %add_convert_fusion.q_ref.k_ref.v_ref, bf16[2560,768]{1,0:T(8,128)(2,1)} %add_convert_fusion.q_ref.k_ref.v_ref, ...), custom_call_target="tpu_custom_call" | custom-call | flops 42949672960 | bytes 8388608 | tf_op jit(solution)/shard_map/attention_backward/pallas_call | solution.py:170
  492.6 37.4 %collective-permute-done.10 = bf16[2,128,768]{2,1,0:T(8,128)(2,1)S(1)} collective-permute-done((bf16[2,128,768]{2,1,0:T(8,128)(2,1)}, bf16[2,128,768]{2,1,0:T(8,128)(2,1)S(1)}, u32[]{:S(2)}, u32[]{:S(2)}) %collective-permute-start.10) | collective-permute-done | bytes 393248 | tf_op jit(solution)/shard_map/ppermute | solution.py:209
  565.2 63.7 %collective-permute-done.21 = bf16[32,1024]{1,0:T(8,128)(2,1)S(1)} collective-permute-done((bf16[32,1024]{1,0:T(8,128)(2,1)S(1)}, bf16[32,1024]{1,0:T(8,128)(2,1)S(1)}, u32[]{:S(2)}, u32[]{:S(2)}) %collective-permute-start.21) | collective-permute-done | bytes 65568 | tf_op jit(solution)/shard_map/ppermute | solution.py:209
  637.9 8.6 %collective-permute-done.35 = bf16[2,128,1024]{2,1,0:T(8,128)(2,1)S(1)} collective-permute-done((bf16[2,128,1024]{2,1,0:T(8,128)(2,1)S(1)}, bf16[2,128,1024]{2,1,0:T(8,128)(2,1)S(1)}, u32[]{:S(2)}, u32[]{:S(2)}) %collective-permute-start.35) | collective-permute-done | bytes 524320 | tf_op jit(solution)/shard_map/ppermute | solution.py:209
  649.2 12.3 %collective-permute-done.30 = bf16[2,32,4096]{2,1,0:T(8,128)(2,1)S(1)} collective-permute-done((bf16[2,32,4096]{2,1,0:T(8,128)(2,1)S(1)}, bf16[2,32,4096]{2,1,0:T(8,128)(2,1)S(1)}, u32[]{:S(2)}, u32[]{:S(2)}) %collective-permute-start.30) | collective-permute-done | bytes 524320 | tf_op jit(solution)/shard_map/ppermute | solution.py:209
  662.4 8.2 %add_convert_fusion.1 = bf16[512,1024]{1,0:T(8,128)(2,1)} fusion(f32[512,1024]{1,0:T(8,128)S(1)} %copy-done.17, bf16[512,3072]{0,1:T(8,128)(2,1)} %bitcast.42, bf16[1024,3072]{1,0:T(8,128)(2,1)} %all-gather.5.cloned.1.call-done), kind=kOutput, calls=%fused_computation.41 | convolution fusion | flops 3222274048 | bytes 12582912 | tf_op jit(solution)/shard_map/se,de->sd/dot_general | solution.py:467
  (331 shorter events, 215.7 us)
Async XLA Ops:
  7.3 232.8 %all-gather.3.cloned.1.call-start = ((), (), s32[]{:S(2)}) async-start(), calls=%async_computation.5 | async-start | bytes 19464192 | tf_op jit(solution)/shard_map/all_gather | solution.py:357
  11.4 65.1 %collective-permute-start.1 = (bf16[512,1024]{1,0:T(8,128)(2,1)S(1)}, bf16[512,1024]{1,0:T(8,128)(2,1)}, u32[]{:S(2)}, u32[]{:S(2)}) collective-permute-start(bf16[512,1024]{1,0:T(8,128)(2,1)S(1)} %copy-done.12), channel_id=1, source_target_pairs={{1,0},{2,1},{3,2},{5,4},{6,5},{7,6},{9,8},{10,9},{11,10},{13,12},{... | collective-permute-start | bytes 3145736 | tf_op jit(solution)/shard_map/ppermute | solution.py:253
  12.7 65.1 %collective-permute-start = (bf16[512,1024]{1,0:T(8,128)(2,1)S(1)}, bf16[512,1024]{1,0:T(8,128)(2,1)}, u32[]{:S(2)}, u32[]{:S(2)}) collective-permute-start(bf16[512,1024]{1,0:T(8,128)(2,1)S(1)} %copy-done.12), channel_id=1, source_target_pairs={{0,1},{1,2},{2,3},{4,5},{5,6},{6,7},{8,9},{9,10},{10,11},{12,13},{... | collective-permute-start | bytes 3145736 | tf_op jit(solution)/shard_map/ppermute | solution.py:252
  76.5 50.3 %collective-permute-start.3 = (bf16[512,1024]{1,0:T(8,128)(2,1)}, bf16[512,1024]{1,0:T(8,128)(2,1)}, u32[]{:S(2)}, u32[]{:S(2)}) collective-permute-start(bf16[512,1024]{1,0:T(8,128)(2,1)} %collective-permute-done.1), channel_id=1, source_target_pairs={{1,0},{2,1},{3,2},{5,4},{6,5},{7,6},{9,8},{10,9},{11,10},{13,12},{... | collective-permute-start | bytes 3145736 | tf_op jit(solution)/shard_map/ppermute | solution.py:253
  77.8 50.3 %collective-permute-start.2 = (bf16[512,1024]{1,0:T(8,128)(2,1)}, bf16[512,1024]{1,0:T(8,128)(2,1)}, u32[]{:S(2)}, u32[]{:S(2)}) collective-permute-start(bf16[512,1024]{1,0:T(8,128)(2,1)} %collective-permute-done), channel_id=1, source_target_pairs={{0,1},{1,2},{2,3},{4,5},{5,6},{6,7},{8,9},{9,10},{10,11},{12,13},{... | collective-permute-start | bytes 3145736 | tf_op jit(solution)/shard_map/ppermute | solution.py:252
  89.4 49.0 %collective-permute-start.8 = (bf16[2,2,4,48,768]{4,3,2,0,1:T(8,128)(2,1)S(1)}, bf16[2,2,4,48,768]{4,3,2,0,1:T(8,128)(2,1)S(1)}, u32[]{:S(2)}, u32[]{:S(2)}) collective-permute-start(bf16[2,2,4,48,768]{4,3,2,0,1:T(8,128)(2,1)S(1)} %maximum_select_fusion.1), channel_id=1, source_target_pairs={{0,4},{1,5},{2,6},{3,7},{4,0},{5,1},{6,2},{7,3},{8,12},{9,13},{10,... | collective-permute-start | bytes 3538952 | tf_op jit(solution)/shard_map/ppermute | solution.py:209
  126.8 55.5 %collective-permute-start.5 = (bf16[512,1024]{1,0:T(8,128)(2,1)}, bf16[512,1024]{1,0:T(8,128)(2,1)}, u32[]{:S(2)}, u32[]{:S(2)}) collective-permute-start(bf16[512,1024]{1,0:T(8,128)(2,1)} %collective-permute-done.3), channel_id=1, source_target_pairs={{1,0},{2,1},{3,2},{5,4},{6,5},{7,6},{9,8},{10,9},{11,10},{13,12},{... | collective-permute-start | bytes 3145736 | tf_op jit(solution)/shard_map/ppermute | solution.py:253
  128.1 46.4 %collective-permute-start.4 = (bf16[512,1024]{1,0:T(8,128)(2,1)}, bf16[512,1024]{1,0:T(8,128)(2,1)}, u32[]{:S(2)}, u32[]{:S(2)}) collective-permute-start(bf16[512,1024]{1,0:T(8,128)(2,1)} %collective-permute-done.2), channel_id=1, source_target_pairs={{0,1},{1,2},{2,3},{4,5},{5,6},{6,7},{8,9},{9,10},{10,11},{12,13},{... | collective-permute-start | bytes 3145736 | tf_op jit(solution)/shard_map/ppermute | solution.py:252
  226.5 35.9 %all-to-all-start.1 = ((bf16[4,512,256]{1,2,0:T(8,128)(2,1)}), bf16[4,512,256]{1,2,0:T(8,128)(2,1)S(1)}, u32[]{:S(2)}, u32[]{:S(2)}) async-start(bf16[4,512,256]{1,2,0:T(8,128)(2,1)} %copy.106), calls=%async_computation.1 | async-start | bytes 2097152 | tf_op jit(solution)/shard_map/all_to_all | solution.py:374
  233.7 428.7 %all-gather.5.cloned.1.call-start = ((), (), s32[]{:S(2)}) async-start(), calls=%async_computation.6 | async-start | bytes 6488064 | tf_op jit(solution)/shard_map/all_gather | solution.py:462
  353.8 42.7 %all-to-all-start.2 = ((bf16[4,512,256]{2,1,0:T(8,128)(2,1)}), bf16[4,512,256]{2,1,0:T(8,128)(2,1)S(1)}, u32[]{:S(2)}, u32[]{:S(2)}) async-start(bf16[4,512,256]{2,1,0:T(8,128)(2,1)} %bitcast.288), calls=%async_computation.2 | async-start | bytes 2097152 | tf_op jit(solution)/shard_map/all_to_all | solution.py:407
  359.5 33.8 %collective-permute-start.17 = (bf16[2,2,2,2,32,1024]{5,4,2,3,0,1:T(8,128)(2,1)S(1)}, bf16[2,2,2,2,32,1024]{5,4,2,3,0,1:T(8,128)(2,1)S(1)}, u32[]{:S(2)}, u32[]{:S(2)}) collective-permute-start(bf16[2,2,2,2,32,1024]{5,4,2,3,0,1:T(8,128)(2,1)S(1)} %bitcast.326), channel_id=1, source_target_pairs={{0,4},{1,5},{2,6},{3,7},{4,0},{5,1},{6,2},{7,3},{8,12},{9,13},{10,... | collective-permute-start | bytes 3145736 | tf_op jit(solution)/shard_map/ppermute | solution.py:209
  391.6 76.6 %collective-permute-start.32 = (bf16[2,2,2,2,128,1024]{5,4,2,3,0,1:T(8,128)(2,1)}, bf16[2,2,2,2,128,1024]{5,4,2,3,0,1:T(8,128)(2,1)}, u32[]{:S(2)}, u32[]{:S(2)}) collective-permute-start(bf16[2,2,2,2,128,1024]{5,4,2,3,0,1:T(8,128)(2,1)} %bitcast.285), channel_id=1, source_target_pairs={{0,4},{1,5},{2,6},{3,7},{4,0},{5,1},{6,2},{7,3},{8,12},{9,13},{10,... | collective-permute-start | bytes 12582920 | tf_op jit(solution)/shard_map/ppermute | solution.py:209
  391.6 85.0 %collective-permute-start.27 = (bf16[2,2,2,2,32,4096]{5,4,2,3,1,0:T(8,128)(2,1)}, bf16[2,2,2,2,32,4096]{5,4,2,3,1,0:T(8,128)(2,1)}, u32[]{:S(2)}, u32[]{:S(2)}) collective-permute-start(bf16[2,2,2,2,32,4096]{5,4,2,3,1,0:T(8,128)(2,1)} %bitcast.286), channel_id=1, source_target_pairs={{0,4},{1,5},{2,6},{3,7},{4,0},{5,1},{6,2},{7,3},{8,12},{9,13},{10,... | collective-permute-start | bytes 12582920 | tf_op jit(solution)/shard_map/ppermute | solution.py:209
  395.5 69.0 %collective-permute-start.18 = (bf16[2,2,2,32,1024]{4,3,1,2,0:T(8,128)(2,1)}, bf16[2,2,2,32,1024]{4,3,1,2,0:T(8,128)(2,1)}, u32[]{:S(2)}, u32[]{:S(2)}) collective-permute-start(bf16[2,2,2,32,1024]{4,3,1,2,0:T(8,128)(2,1)} %dynamic-slice_bitcast_fusion.7), channel_id=1, source_target_pairs={{0,8},{1,9},{2,10},{3,11},{4,12},{5,13},{6,14},{7,15},{8,0},{9,1},... | collective-permute-start | bytes 1572872 | tf_op jit(solution)/shard_map/ppermute | solution.py:209
  475.6 67.8 %collective-permute-start.33 = (bf16[2,2,2,128,1024]{4,3,1,2,0:T(8,128)(2,1)}, bf16[2,2,2,128,1024]{4,3,1,2,0:T(8,128)(2,1)}, u32[]{:S(2)}, u32[]{:S(2)}) collective-permute-start(bf16[2,2,2,128,1024]{4,3,1,2,0:T(8,128)(2,1)} %dynamic-slice_bitcast_fusion), channel_id=1, source_target_pairs={{0,8},{1,9},{2,10},{3,11},{4,12},{5,13},{6,14},{7,15},{8,0},{9,1},... | collective-permute-start | bytes 6291464 | tf_op jit(solution)/shard_map/ppermute | solution.py:209
  483.3 66.4 %collective-permute-start.28 = (bf16[2,2,2,32,4096]{4,3,1,2,0:T(8,128)(2,1)}, bf16[2,2,2,32,4096]{4,3,1,2,0:T(8,128)(2,1)}, u32[]{:S(2)}, u32[]{:S(2)}) collective-permute-start(bf16[2,2,2,32,4096]{4,3,1,2,0:T(8,128)(2,1)} %dynamic-slice_bitcast_fusion.1), channel_id=1, source_target_pairs={{0,16},{1,17},{2,18},{3,19},{4,20},{5,21},{6,22},{7,23},{8,24},{9,... | collective-permute-start | bytes 6291464 | tf_op jit(solution)/shard_map/ppermute | solution.py:209
  487.0 43.0 %collective-permute-start.10 = (bf16[2,128,768]{2,1,0:T(8,128)(2,1)}, bf16[2,128,768]{2,1,0:T(8,128)(2,1)S(1)}, u32[]{:S(2)}, u32[]{:S(2)}) collective-permute-start(bf16[2,128,768]{2,1,0:T(8,128)(2,1)} %dynamic-slice_bitcast_fusion.8), channel_id=1, source_target_pairs={{0,8},{1,9},{2,10},{3,11},{4,12},{5,13},{6,14},{7,15},{8,0},{9,1},... | collective-permute-start | bytes 1179656 | tf_op jit(solution)/shard_map/ppermute | solution.py:209
  488.9 48.2 %collective-permute-start.19 = (bf16[2,2,32,1024]{3,2,0,1:T(8,128)(2,1)}, bf16[2,2,32,1024]{3,2,0,1:T(8,128)(2,1)}, u32[]{:S(2)}, u32[]{:S(2)}) collective-permute-start(bf16[2,2,32,1024]{3,2,0,1:T(8,128)(2,1)} %dynamic-slice_bitcast_fusion.11), channel_id=1, source_target_pairs={{0,16},{1,17},{2,18},{3,19},{4,20},{5,21},{6,22},{7,23},{8,24},{9,... | collective-permute-start | bytes 786440 | tf_op jit(solution)/shard_map/ppermute | solution.py:209
  547.9 81.9 %collective-permute-start.34 = (bf16[2,2,128,1024]{3,2,0,1:T(8,128)(2,1)}, bf16[2,2,128,1024]{3,2,0,1:T(8,128)(2,1)}, u32[]{:S(2)}, u32[]{:S(2)}) collective-permute-start(bf16[2,2,128,1024]{3,2,0,1:T(8,128)(2,1)} %dynamic-slice_bitcast_fusion.2), channel_id=1, source_target_pairs={{0,16},{1,17},{2,18},{3,19},{4,20},{5,21},{6,22},{7,23},{8,24},{9,... | collective-permute-start | bytes 3145736 | tf_op jit(solution)/shard_map/ppermute | solution.py:209
  553.3 109.1 %all-to-all-start.3 = ((bf16[4,512,768]{1,2,0:T(8,128)(2,1)}), bf16[4,512,768]{1,2,0:T(8,128)(2,1)}, u32[]{:S(2)}, u32[]{:S(2)}) async-start(bf16[4,512,768]{1,2,0:T(8,128)(2,1)} %copy.108), calls=%async_computation.3 | async-start | bytes 6291456 | tf_op jit(solution)/shard_map/all_to_all | solution.py:461
  560.7 71.0 %collective-permute-start.29 = (bf16[2,2,32,4096]{3,2,0,1:T(8,128)(2,1)}, bf16[2,2,32,4096]{3,2,0,1:T(8,128)(2,1)}, u32[]{:S(2)}, u32[]{:S(2)}) collective-permute-start(bf16[2,2,32,4096]{3,2,0,1:T(8,128)(2,1)} %dynamic-slice_bitcast_fusion.3), channel_id=1, source_target_pairs={{0,8},{1,9},{2,10},{3,11},{4,12},{5,13},{6,14},{7,15},{8,0},{9,1},... | collective-permute-start | bytes 3145736 | tf_op jit(solution)/shard_map/ppermute | solution.py:209
  561.6 67.3 %collective-permute-start.21 = (bf16[32,1024]{1,0:T(8,128)(2,1)S(1)}, bf16[32,1024]{1,0:T(8,128)(2,1)S(1)}, u32[]{:S(2)}, u32[]{:S(2)}) collective-permute-start(bf16[32,1024]{1,0:T(8,128)(2,1)S(1)} %dynamic-slice_bitcast_fusion.14), channel_id=1, source_target_pairs={{0,2},{1,3},{2,0},{3,1},{4,6},{5,7},{6,4},{7,5},{8,10},{9,11},{10,... | collective-permute-start | bytes 196616 | tf_op jit(solution)/shard_map/ppermute | solution.py:209
  633.3 28.3 %collective-permute-start.30 = (bf16[2,32,4096]{2,1,0:T(8,128)(2,1)S(1)}, bf16[2,32,4096]{2,1,0:T(8,128)(2,1)S(1)}, u32[]{:S(2)}, u32[]{:S(2)}) collective-permute-start(bf16[2,32,4096]{2,1,0:T(8,128)(2,1)S(1)} %dynamic-slice_bitcast_fusion.6), channel_id=1, source_target_pairs={{0,1},{1,0},{2,3},{3,2},{4,5},{5,4},{6,7},{7,6},{8,9},{9,8},{10,11... | collective-permute-start | bytes 1572872 | tf_op jit(solution)/shard_map/ppermute | solution.py:209
  (60 other events, 534.8 us)
Sparse Core Ops, SparseCore 0:
  11.5 170.0 all-gather.2
  237.4 74.3 all-gather.4

commit v2 on v1

v2 whole, which is shorter than its diff:
```python
import functools
import math

import jax
import jax.numpy as jnp
from jax import lax
from jax.experimental import pallas as pl
from jax.experimental.pallas import tpu as pltpu
from jax.sharding import PartitionSpec as P

HD = 64
AXES = ("dp", "ctx")
norm_eps = 1e-05
score_scale = 1.0 / math.sqrt(HD)
score_scale_two = score_scale * math.log2(math.e)
f32 = jnp.float32
bf16 = jnp.bfloat16


def kernel_cost(flops):
    return flops // 8


def attention_forward_kernel(
    place_ref, q_ref, k_ref, v_ref, mixed_ref, lse_ref, keys_t_ref, *, heads, rows
):
    width = k_ref.shape[1]
    seq = keys_t_ref.shape[1]

    @pl.when(pl.program_id(0) == 0)
    def _():
        keys_t_ref[...] = k_ref[...].T

    queries = q_ref[...]
    keys_t = keys_t_ref[...]
    values = v_ref[...]
    slots = [
        (place_ref[0] ^ slot) * rows + lax.broadcasted_iota(jnp.int32, (1, rows), 1)
        for slot in range(seq // rows)
    ]
    key_pos = jnp.concatenate(slots, axis=1)
    bias = jnp.where(key_pos < place_ref[1], 0.0, -1e30).astype(f32)
    head_of = lax.broadcasted_iota(jnp.int32, (rows, width), 1) // HD
    lane = lax.broadcasted_iota(jnp.int32, (rows, 128), 1)
    mixed = jnp.zeros((rows, width), f32)
    lse = jnp.zeros((rows, 128), f32)
    for head in range(heads):
        own = jnp.where(head_of == head, queries, jnp.zeros_like(queries))
        scores = jnp.dot(own, keys_t, preferred_element_type=f32) * score_scale_two + bias
        top = jnp.max(scores, axis=1, keepdims=True)
        probs = jnp.exp2(scores - top)
        total = jnp.sum(probs, axis=1, keepdims=True)
        part = jnp.dot(probs.astype(bf16), values, preferred_element_type=f32)
        mixed = jnp.where(head_of == head, part * (1.0 / total), mixed)
        lse = jnp.where(lane == head, top + jnp.log2(total), lse)
    mixed_ref[...] = mixed.astype(bf16)
    lse_ref[...] = lse.T[:8]


def attention_forward(qkv, place, rows, chunk, chunks):
    seq = qkv.shape[0]
    width = qkv.shape[1] // (3 * chunks)
    heads = width // HD
    return pl.pallas_call(
        functools.partial(attention_forward_kernel, heads=heads, rows=rows),
        grid=(seq // rows,),
        in_specs=[
            pl.BlockSpec(memory_space=pltpu.SMEM),
            pl.BlockSpec((rows, width), lambda i: (i, chunk)),
            pl.BlockSpec((seq, width), lambda i: (0, chunks + chunk)),
            pl.BlockSpec((seq, width), lambda i: (0, 2 * chunks + chunk)),
        ],
        out_specs=[
            pl.BlockSpec((rows, width), lambda i: (i, 0)),
            pl.BlockSpec((8, rows), lambda i: (0, i)),
        ],
        out_shape=[
            jax.ShapeDtypeStruct((seq, width), bf16),
            jax.ShapeDtypeStruct((8, seq), f32),
        ],
        scratch_shapes=[pltpu.VMEM((width, seq), bf16)],
        compiler_params=pltpu.CompilerParams(vmem_limit_bytes=56 * 2**20),
        cost_estimate=pl.CostEstimate(
            flops=kernel_cost(16 * seq * seq * width),
            bytes_accessed=8 * seq * width,
            transcendentals=seq * seq * heads,
        ),
        name="attention_forward",
    )(place, qkv, qkv, qkv)


def attention_backward_kernel(
    place_ref,
    q_ref,
    k_ref,
    v_ref,
    mixed_ref,
    lse_ref,
    *refs,
    heads,
    rows,
):
    step = pl.program_id(0)
    dmixed_refs, (out_ref, keys_t_ref, dk_sum, dv_sum, dmixed_ref) = refs[:-5], refs[-5:]
    seq, width = dk_sum.shape
    for slot, slot_ref in enumerate(dmixed_refs):

        @pl.when(step == slot)
        def _(slot_ref=slot_ref):
            dmixed_ref[...] = slot_ref[...]

    @pl.when(step == 0)
    def _():
        keys_t_ref[...] = k_ref[...].T
        dk_sum[...] = jnp.zeros_like(dk_sum)
        dv_sum[...] = jnp.zeros_like(dv_sum)

    queries, dmixed = q_ref[...], dmixed_ref[...]
    queries_t, dmixed_t, mixed_t = queries.T, dmixed.T, mixed_ref[...].T
    product = dmixed_t.astype(f32) * mixed_t.astype(f32)
    lane_head = lax.broadcasted_iota(jnp.int32, (rows, width), 1) // HD
    row_head = lax.broadcasted_iota(jnp.int32, (width, rows), 0) // HD
    none, none_t = jnp.zeros_like(queries), jnp.zeros_like(queries_t)
    lse = lse_ref[...]
    per_head = []
    for head in range(heads):
        per_head.append(
            (
                jnp.where(row_head == head, queries_t, none_t),
                jnp.where(row_head == head, dmixed_t, none_t),
                jnp.where(lane_head == head, queries, none),
                jnp.where(lane_head == head, dmixed, none),
                jnp.sum(product[HD * head : HD * head + HD], axis=0, keepdims=True),
                lse[head : head + 1],
            )
        )

    def chunk(index, dq_t):
        span = pl.ds(pl.multiple_of(index * rows, rows), rows)
        keys, values = k_ref[span, :], v_ref[span, :]
        key_pos = (place_ref[0] ^ index) * rows + lax.broadcasted_iota(jnp.int32, (rows, 1), 0)
        bias = jnp.where(key_pos < place_ref[1], 0.0, -1e30).astype(f32)
        dk, dv = dk_sum[span, :], dv_sum[span, :]
        new_dq_t = []
        for head in range(heads):
            own_q_t, own_do_t, own_q, own_do, delta, own_lse = per_head[head]
            scores = jnp.dot(keys, own_q_t, preferred_element_type=f32)
            probs = jnp.exp2(scores * score_scale_two + bias - own_lse)
            dprobs = jnp.dot(values, own_do_t, preferred_element_type=f32)
            dscores = (probs * (dprobs - delta)).astype(bf16)
            dv = dv + jnp.dot(probs.astype(bf16), own_do, preferred_element_type=f32)
            dk = dk + jnp.dot(dscores, own_q, preferred_element_type=f32)
            own_keys_t = keys_t_ref[HD * head : HD * head + HD, span]
            new_dq_t.append(
                dq_t[head] + jnp.dot(own_keys_t, dscores, preferred_element_type=f32)
            )
        dk_sum[span, :] = dk
        dv_sum[span, :] = dv
        return tuple(new_dq_t)

    start = tuple(jnp.zeros((HD, rows), f32) for _ in range(heads))
    dq_t = jnp.concatenate(lax.fori_loop(0, seq // rows, chunk, start), axis=0)
    own_rows = pl.ds(pl.multiple_of(step * rows, rows), rows)
    out_ref[own_rows, :width] = (dq_t * score_scale).T.astype(bf16)

    @pl.when(step == pl.num_programs(0) - 1)
    def _():
        out_ref[:, width : 2 * width] = (dk_sum[...] * score_scale).astype(bf16)
        out_ref[:, 2 * width :] = dv_sum[...].astype(bf16)


def attention_backward(qkv, mixed, dmixed_slots, lse, place, chunk, chunks):
    seq, width = mixed.shape
    rows = seq // len(dmixed_slots)
    heads = width // HD
    block = pl.BlockSpec((rows, width), lambda i: (i, 0))
    return pl.pallas_call(
        functools.partial(attention_backward_kernel, heads=heads, rows=rows),
        grid=(seq // rows,),
        in_specs=[
            pl.BlockSpec(memory_space=pltpu.SMEM),
            pl.BlockSpec((rows, width), lambda i: (i, chunk)),
            pl.BlockSpec((seq, width), lambda i: (0, chunks + chunk)),
            pl.BlockSpec((seq, width), lambda i: (0, 2 * chunks + chunk)),
            block,
            pl.BlockSpec((8, rows), lambda i: (0, i)),
        ]
        + [pl.BlockSpec((rows, width), lambda i: (0, chunk))] * len(dmixed_slots),
        out_specs=pl.BlockSpec((seq, 3 * width), lambda i: (0, 0)),
        out_shape=jax.ShapeDtypeStruct((seq, 3 * width), bf16),
        scratch_shapes=[
            pltpu.VMEM((width, seq), bf16),
            pltpu.VMEM((seq, width), f32),
            pltpu.VMEM((seq, width), f32),
            pltpu.VMEM((rows, width), bf16),
        ],
        compiler_params=pltpu.CompilerParams(vmem_limit_bytes=56 * 2**20),
        cost_estimate=pl.CostEstimate(
            flops=kernel_cost(40 * seq * seq * width),
            bytes_accessed=16 * seq * width,
            transcendentals=seq * seq * heads,
        ),
        name="attention_backward",
    )(place, qkv, qkv, qkv, mixed, lse, *dmixed_slots)


def layer_kernel(
    place_ref,
    tokens_ref,
    cotangent_ref,
    vectors_ref,
    inner_offset_ref,
    *refs,
    chunks,
    groups,
):
    mixed_refs, refs = refs[: chunks * groups], refs[chunks * groups :]
    weight_refs, refs = refs[:2], refs[2:]
    (layer_out_ref, dfirst_ref, sums_ref, inner_sum_ref), refs = refs[:4], refs[4:]
    dmixed_refs, gradient_refs, refs = refs[:groups], refs[groups : groups + 6], refs[groups + 6 :]
    (w_attn, w_inner, w_outer), refs = refs[:3], refs[3:]
    (mixed_ref, hidden_ref, act_ref, douter_ref, dpre_ref, dattn_ref), refs = refs[:6], refs[6:]
    (wide_ref, normed_ref, inverse_ref, total_ref, dmixed_ref, turned_ref, sems) = refs
    rows, width = tokens_ref.shape
    hidden_width = w_inner.shape[1]
    place, length, core, quad = place_ref[0], place_ref[1], place_ref[2], place_ref[3]
    first_row = place * rows

    first_weights, outer_weights = weight_refs
    copies = [
        pltpu.make_async_copy(first_weights.at[:, :width], w_attn, sems.at[0]),
        pltpu.make_async_copy(first_weights.at[:, width:], w_inner, sems.at[1]),
        pltpu.make_async_copy(outer_weights, w_outer, sems.at[2]),
    ]
    for copy in copies:
        copy.start()

    b_attn, g_attn, s_attn = vectors_ref[0:1], vectors_ref[1:2], vectors_ref[2:3]
    b_outer, g_final, s_final = vectors_ref[3:4], vectors_ref[4:5], vectors_ref[5:6]
    chunk_width = mixed_refs[0].shape[1]

    def columns_of(chunk, slot):
        start = ((place ^ slot) * chunks + chunk) * chunk_width
        return pl.ds(pl.multiple_of(start, chunk_width), chunk_width)

    for chunk in range(chunks):
        for slot in range(groups):
            mixed_ref[:, columns_of(chunk, slot)] = mixed_refs[chunk * groups + slot][...]

    copies[0].wait()

    step = 128

    def norm_one(turn, carried):
        span = pl.ds(pl.multiple_of(turn * step, step), step)
        first = (
            tokens_ref[span, :].astype(f32)
            + jnp.dot(mixed_ref[span, :], w_attn[...], preferred_element_type=f32)
            + b_attn
        )
        centered = first - jnp.mean(first, axis=1, keepdims=True)
        inverse = lax.rsqrt(jnp.mean(centered * centered, axis=1, keepdims=True) + norm_eps)
        normed = centered * inverse
        hidden = normed * g_attn + s_attn
        normed_ref[span, :] = normed
        inverse_ref[span, :] = jnp.broadcast_to(inverse, (step, 128))
        total_ref[span, :] = hidden
        hidden_ref[span, :] = hidden.astype(bf16)
        return carried

    lax.fori_loop(0, rows // step, norm_one, 0)

    copies[1].wait()
    block = 512

    def feed_in(turn, carried):
        span = pl.ds(pl.multiple_of(turn * block, block), block)
        pre = (
            jnp.dot(hidden_ref[...], w_inner[:, span], preferred_element_type=f32)
            + inner_offset_ref[:, span]
        )
        normal_cdf = 0.5 * (1.0 + lax.erf(pre * (1.0 / math.sqrt(2.0))))
        act_ref[:, span] = (pre * normal_cdf).astype(bf16)
        slope = normal_cdf + pre * jnp.exp(-0.5 * pre * pre) * (1.0 / math.sqrt(2.0 * math.pi))
        dpre_ref[:, span] = slope.astype(bf16)
        return carried

    lax.fori_loop(0, hidden_width // block, feed_in, 0)

    copies[2].wait()
    narrow = 512

    def feed_out(turn, carried):
        span = pl.ds(pl.multiple_of(turn * narrow, narrow), narrow)
        wide_ref[:, span] = jnp.dot(act_ref[...], w_outer[:, span], preferred_element_type=f32)
        return carried

    lax.fori_loop(0, width // narrow, feed_out, 0)

    def norm_two(turn, carried):
        span = pl.ds(pl.multiple_of(turn * step, step), step)
        second = total_ref[span, :] + wide_ref[span, :] + b_outer
        centered = second - jnp.mean(second, axis=1, keepdims=True)
        inverse = lax.rsqrt(jnp.mean(centered * centered, axis=1, keepdims=True) + norm_eps)
        normed = centered * inverse
        row = first_row + turn * step + lax.broadcasted_iota(jnp.int32, (step, 1), 0)
        valid = jnp.where(row < length, 1.0, 0.0).astype(f32)
        layer_out_ref[span, :] = ((normed * g_final + s_final) * valid).astype(bf16)
        upstream = cotangent_ref[span, :].astype(f32) * valid
        shift_sum, gain_sum, offset_sum = carried
        shift_sum = shift_sum + jnp.sum(upstream, axis=0, keepdims=True)
        gain_sum = gain_sum + jnp.sum(upstream * normed, axis=0, keepdims=True)
        scaled = upstream * g_final
        first_mean = jnp.mean(scaled, axis=1, keepdims=True)
        second_mean = jnp.mean(scaled * normed, axis=1, keepdims=True)
        dsecond = inverse * (scaled - first_mean - normed * second_mean)
        total_ref[span, :] = dsecond
        douter = dsecond.astype(bf16)
        douter_ref[span, :] = douter
        offset_sum = offset_sum + jnp.sum(douter.astype(f32), axis=0, keepdims=True)
        return (shift_sum, gain_sum, offset_sum)

    none = jnp.zeros((1, width), f32)
    shift_sum, gain_sum, offset_sum = lax.fori_loop(
        0, rows // step, norm_two, (none, none, none)
    )
    sums_ref[0:1] = offset_sum
    sums_ref[1:2] = gain_sum
    sums_ref[2:3] = shift_sum

    across = (((1,), (1,)), ((), ()))

    def back_out(turn, carried):
        span = pl.ds(pl.multiple_of(turn * block, block), block)
        dact = lax.dot_general(
            douter_ref[...], w_outer[span, :], across, preferred_element_type=f32
        )
        dpre = (dact * dpre_ref[:, span].astype(f32)).astype(bf16)
        dpre_ref[:, span] = dpre
        inner_sum_ref[:, span] = jnp.sum(dpre.astype(f32), axis=0, keepdims=True)
        return carried

    lax.fori_loop(0, hidden_width // block, back_out, 0)

    quads = gradient_refs[0].shape[0]
    slab, outer_slab = width // (2 * quads), hidden_width // (2 * quads)
    left_width = gradient_refs[0].shape[2]
    down = (((0,), (0,)), ((), ()))

    def leave(first_sem, plan, height):
        started = []
        for source, from_col, cols, which, to_col in plan:
            for side in range(2):
                owner = 1 - core if side == 0 else core
                for slot in range(quads):
                    row = pl.multiple_of((2 * (slot ^ quad) + owner) * height, height)
                    copy = pltpu.make_async_copy(
                        source.at[pl.ds(row, height), from_col : from_col + cols],
                        gradient_refs[2 * which + side].at[slot, :, to_col : to_col + cols],
                        sems.at[first_sem + len(started)],
                    )
                    copy.start()
                    started.append(copy)
        return started

    def outer_gradient(turn, carried):
        span = pl.ds(pl.multiple_of(turn * block, block), block)
        terms = lax.dot_general(
            act_ref[:, span], douter_ref[...], down, preferred_element_type=f32
        )
        w_outer[span, :] = terms.astype(bf16)
        return carried

    lax.fori_loop(0, hidden_width // block, outer_gradient, 0)
    leaving = leave(3, ((w_outer, 0, width, 2, 0),), outer_slab)

    def back_in(turn, carried):
        span = pl.ds(pl.multiple_of(turn * narrow, narrow), narrow)
        wide_ref[:, span] = lax.dot_general(
            dpre_ref[...], w_inner[span, :], across, preferred_element_type=f32
        )
        return carried

    lax.fori_loop(0, width // narrow, back_in, 0)

    def norm_one_back(turn, carried):
        span = pl.ds(pl.multiple_of(turn * step, step), step)
        dhidden = total_ref[span, :] + wide_ref[span, :]
        normed = normed_ref[span, :]
        inverse = inverse_ref[span, 0:1]
        shift_sum, gain_sum, offset_sum = carried
        shift_sum = shift_sum + jnp.sum(dhidden, axis=0, keepdims=True)
        gain_sum = gain_sum + jnp.sum(dhidden * normed, axis=0, keepdims=True)
        scaled = dhidden * g_attn
        first_mean = jnp.mean(scaled, axis=1, keepdims=True)
        second_mean = jnp.mean(scaled * normed, axis=1, keepdims=True)
        dfirst = inverse * (scaled - first_mean - normed * second_mean)
        dfirst_ref[span, :] = dfirst
        dattn = dfirst.astype(bf16)
        dattn_ref[span, :] = dattn
        offset_sum = offset_sum + jnp.sum(dattn.astype(f32), axis=0, keepdims=True)
        dmixed = lax.dot_general(dattn, w_attn[...], across, preferred_element_type=f32)
        dmixed_ref[span, :] = dmixed.astype(bf16)
        return (shift_sum, gain_sum, offset_sum)

    shift_sum, gain_sum, offset_sum = lax.fori_loop(
        0, rows // step, norm_one_back, (none, none, none)
    )
    sums_ref[3:4] = offset_sum
    sums_ref[4:5] = gain_sum
    sums_ref[5:6] = shift_sum
    sums_ref[6:8] = jnp.zeros((2, width), f32)
    group_width = chunks * chunk_width
    for slot in range(groups):
        start = pl.multiple_of((place ^ slot) * group_width, group_width)
        dmixed_refs[slot][...] = dmixed_ref[:, pl.ds(start, group_width)]

    turned_ref[...] = hidden_ref[...].T
    wide_block = 1024

    def inner_gradient(turn, carried):
        span = pl.ds(pl.multiple_of(turn * wide_block, wide_block), wide_block)
        for half in range(width // block):
            rows_of = slice(half * block, (half + 1) * block)
            terms = jnp.dot(turned_ref[rows_of, :], dpre_ref[:, span], preferred_element_type=f32)
            w_inner[rows_of, span] = terms.astype(bf16)
        return carried

    lax.fori_loop(0, hidden_width // wide_block, inner_gradient, 0)
    leaving += leave(
        3 + len(leaving),
        (
            (w_inner, left_width - width, hidden_width + width - left_width, 1, 0),
            (w_inner, 0, left_width - width, 0, width),
        ),
        slab,
    )
    turned_ref[...] = mixed_ref[...].T
    for half in range(width // block):
        rows_of = slice(half * block, (half + 1) * block)
        terms = jnp.dot(turned_ref[rows_of, :], dattn_ref[...], preferred_element_type=f32)
        w_attn[rows_of, :] = terms.astype(bf16)
    leaving += leave(3 + len(leaving), ((w_attn, 0, width, 0, 0),), slab)
    for copy in leaving:
        copy.wait()


def layer_middle(place, tokens, cotangent, vectors, inner_offset, mixed_parts, groups, weights, quads):
    rows, width = tokens.shape
    hidden_width = inner_offset.shape[1]
    chunk_width = mixed_parts[0].shape[1]
    chunks = len(mixed_parts) // groups
    slab, outer_slab = width // (2 * quads), hidden_width // (2 * quads)
    left_width = 2 * width
    vmem = pl.BlockSpec(memory_space=pltpu.VMEM)
    anywhere = pl.BlockSpec(memory_space=pl.ANY)
    shapes = [
        jax.ShapeDtypeStruct((rows, width), bf16),
        jax.ShapeDtypeStruct((rows, width), f32),
        jax.ShapeDtypeStruct((8, width), f32),
        jax.ShapeDtypeStruct((1, hidden_width), f32),
    ] + [jax.ShapeDtypeStruct((rows, chunks * chunk_width), bf16)] * groups
    gradients = [
        jax.ShapeDtypeStruct((quads, slab, left_width), bf16),
        jax.ShapeDtypeStruct((quads, slab, width + hidden_width - left_width), bf16),
        jax.ShapeDtypeStruct((quads, outer_slab, width), bf16),
    ]
    gradients = [shape for shape in gradients for _ in range(2)]
    return pl.pallas_call(
        functools.partial(layer_kernel, chunks=chunks, groups=groups),
        in_specs=[pl.BlockSpec(memory_space=pltpu.SMEM)]
        + [vmem] * (4 + chunks * groups)
        + [anywhere] * 2,
        out_specs=[vmem] * len(shapes) + [anywhere] * 6,
        out_shape=shapes + gradients,
        scratch_shapes=[
            pltpu.VMEM((width, width), bf16),
            pltpu.VMEM((width, hidden_width), bf16),
            pltpu.VMEM((hidden_width, width), bf16),
            pltpu.VMEM((rows, width), bf16),
            pltpu.VMEM((rows, width), bf16),
            pltpu.VMEM((rows, hidden_width), bf16),
            pltpu.VMEM((rows, width), bf16),
            pltpu.VMEM((rows, hidden_width), bf16),
            pltpu.VMEM((rows, width), bf16),
            pltpu.VMEM((rows, width), f32),
            pltpu.VMEM((rows, width), f32),
            pltpu.VMEM((rows, 128), f32),
            pltpu.VMEM((rows, width), f32),
            pltpu.VMEM((rows, width), bf16),
            pltpu.VMEM((width, rows), bf16),
            pltpu.SemaphoreType.DMA((3 + 8 * quads,)),
        ],
        compiler_params=pltpu.CompilerParams(vmem_limit_bytes=60 * 2**20),
        cost_estimate=pl.CostEstimate(
            flops=kernel_cost(12 * rows * width * (hidden_width + width)),
            bytes_accessed=4 * width * (2 * hidden_width + width) + 10 * rows * width,
            transcendentals=2 * rows * hidden_width,
        ),
        name="layer_middle",
    )(place, tokens, cotangent, vectors, inner_offset, *mixed_parts, *weights)


def input_kernel(place_ref, dfirst_ref, weights_ref, *refs, chunks, groups):
    parts, (out_ref, rows_ref) = refs[:-2], refs[-2:]
    cols = parts[0].shape[1]
    for chunk in range(chunks):
        for slot in range(groups):
            start = (chunk * groups + (place_ref[0] ^ slot)) * cols
            span = pl.ds(pl.multiple_of(start, cols), cols)
            rows_ref[:, span] = parts[chunk * groups + slot][...]
    block = 256

    def columns(turn, carried):
        span = pl.ds(pl.multiple_of(turn * block, block), block)
        terms = lax.dot_general(
            rows_ref[...],
            weights_ref[span, :],
            (((1,), (1,)), ((), ())),
            preferred_element_type=f32,
        )
        out_ref[:, span] = (dfirst_ref[:, span] + terms).astype(bf16)
        return carried

    lax.fori_loop(0, out_ref.shape[1] // block, columns, 0)


def input_gradient(place, dfirst, weights, parts, groups):
    rows, width = dfirst.shape
    vmem = pl.BlockSpec(memory_space=pltpu.VMEM)
    return pl.pallas_call(
        functools.partial(input_kernel, chunks=len(parts) // groups, groups=groups),
        in_specs=[pl.BlockSpec(memory_space=pltpu.SMEM)] + [vmem] * (2 + len(parts)),
        out_specs=vmem,
        out_shape=jax.ShapeDtypeStruct((rows, width), bf16),
        scratch_shapes=[pltpu.VMEM((rows, weights.shape[1]), bf16)],
        compiler_params=pltpu.CompilerParams(vmem_limit_bytes=48 * 2**20),
        cost_estimate=pl.CostEstimate(
            flops=kernel_cost(2 * rows * width * weights.shape[1]),
            bytes_accessed=2 * width * weights.shape[1] + 12 * rows * width,
            transcendentals=0,
        ),
        name="input_gradient",
    )(place, dfirst, weights, *parts)


def device_index():
    return lax.axis_index("dp") * lax.axis_size("ctx") + lax.axis_index("ctx")


def bits_of(count):
    return count.bit_length() - 1


def swap(values, bit):
    count = lax.axis_size("dp") * lax.axis_size("ctx")
    return lax.ppermute(values, AXES, [(i, i ^ (1 << bit)) for i in range(count)])


def own_bit(bit):
    return (device_index() >> bit) & 1


def joined(shard, other, bit, axis):
    return jnp.where(
        own_bit(bit) == 1,
        jnp.stack([other, shard], axis=axis),
        jnp.stack([shard, other], axis=axis),
    )


def after(value, *others):
    return lax.optimization_barrier((value,) + others)[0]


def gather_line(block):
    count = lax.axis_size("ctx")
    place = lax.axis_index("ctx")
    held = jnp.broadcast_to(block[None], (count,) + block.shape)
    from_left = from_right = block
    for step in range(1, count):
        from_left, from_right = yield [
            lax.ppermute(from_left, "ctx", [(i, i + 1) for i in range(count - 1)]),
            lax.ppermute(from_right, "ctx", [(i + 1, i) for i in range(count - 1)]),
        ]
        for arrived, source in ((from_left, place - step), (from_right, place + step)):
            inside = (source >= 0) & (source < count)
            held = lax.dynamic_update_index_in_dim(
                held,
                jnp.where(inside, arrived, block),
                jnp.where(inside, source ^ place, 0),
                0,
            )
    return held.reshape((count * block.shape[0],) + block.shape[1:])


def exchange_slots(slots):
    count = lax.axis_size("ctx")
    return [slots[0]] + [
        lax.ppermute(slots[mask], "ctx", [(i, i ^ mask) for i in range(count)])
        for mask in range(1, count)
    ]


def exchange_line(blocks):
    count = lax.axis_size("ctx")
    place = lax.axis_index("ctx")
    arrived = yield [
        lax.ppermute(
            lax.dynamic_index_in_dim(blocks, place ^ mask, 0, keepdims=False),
            "ctx",
            [(i, i ^ mask) for i in range(count)],
        )
        for mask in range(1, count)
    ]
    for mask, value in enumerate(arrived, 1):
        blocks = lax.dynamic_update_index_in_dim(blocks, value, place ^ mask, 0)
    return blocks


def gather_bits(shard, bit_order):
    held = []
    for bit in bit_order:
        (other,) = yield [swap(shard, bit)]
        held = sorted(held + [bit], reverse=True)
        shard = joined(shard, other, bit, held.index(bit))
    return shard.reshape((2 ** len(held),) + shard.shape[len(held) :])


def gather_group(packed, bit_order):
    packed = yield from exchange_line(packed)
    return (yield from gather_bits(packed, bit_order))


def scatter_sum(parts, bit_order, out_dtype, sent):
    left = sorted(bit_order, reverse=True)
    for bit in bit_order:
        axis, mine = left.index(bit), own_bit(bit)
        if bit >= bits_of(lax.axis_size("ctx")):
            given = [lax.index_in_dim(part, 1, axis, keepdims=False) for part in parts]
            parts = [lax.index_in_dim(part, 0, axis, keepdims=False) for part in parts]
        else:
            given = [lax.dynamic_index_in_dim(part, 1 - mine, axis, False) for part in parts]
            parts = [lax.dynamic_index_in_dim(part, mine, axis, False) for part in parts]
        given = total_of(given, parts[0].dtype)
        sent.append(given)
        parts = parts + (yield [swap(given, bit)])
        left.remove(bit)
    return total_of(parts, out_dtype)


def total_of(parts, dtype):
    total = parts[0].astype(f32)
    for part in parts[1:]:
        total = total + part.astype(f32)
    return total.astype(dtype)


def scatter_core(terms, bit):
    mine = own_bit(bit)
    (received,) = yield [swap(lax.dynamic_index_in_dim(terms, 1 - mine, 1, False), bit)]
    kept = lax.dynamic_index_in_dim(terms, mine, 1, False)
    return total_of([kept, received], terms.dtype)


def scatter_at_once(terms, bits):
    masks = range(1, 2 ** len(bits))
    low = min(bits)
    place = (device_index() >> low) & (2 ** len(bits) - 1)
    count = lax.axis_size("dp") * lax.axis_size("ctx")
    received = yield [
        lax.ppermute(
            lax.dynamic_index_in_dim(terms, place ^ mask, 0, keepdims=False),
            AXES,
            [(i, i ^ (mask << low)) for i in range(count)],
        )
        for mask in masks
    ]
    total = lax.dynamic_index_in_dim(terms, place, 0, keepdims=False).astype(f32)
    for value in received:
        total = total + value.astype(f32)
    return total.astype(terms.dtype)


class Process:
    def __init__(self, process):
        self.process = process
        self.arrived = next(process)
        self.result = None

    def advance(self):
        if self.result is not None:
            return
        try:
            self.arrived = self.process.send(self.arrived)
        except StopIteration as stop:
            self.arrived, self.result = [], stop.value

    def finish(self):
        while self.result is None:
            self.advance()
        return self.result


def together(processes, *others):
    flat = [value for process in processes for value in process.arrived]
    flat = list(lax.optimization_barrier(tuple(flat) + tuple(others)))
    for process in processes:
        count = len(process.arrived)
        process.arrived, flat = flat[:count], flat[count:]


def row_sum(values):
    return jnp.sum(values.astype(f32), axis=0)


def local(
    tokens,
    lengths,
    cotangent,
    query_proj,
    query_offset,
    key_proj,
    value_proj,
    value_offset,
    attn_proj,
    attn_offset,
    attn_gain,
    attn_shift,
    inner_proj,
    inner_offset,
    outer_proj,
    outer_offset,
    final_gain,
    final_shift,
):
    n_dp, n_ctx = lax.axis_size("dp"), lax.axis_size("ctx")
    n_dev = n_dp * n_ctx
    dev_bits = bits_of(n_dev)
    ctx_bits = bits_of(n_ctx)
    rows, width = tokens.shape
    seq = rows * n_ctx
    group = width // n_ctx
    part = width // n_dev
    hidden_width = inner_proj.shape[1]
    hidden_part = hidden_width // n_dev
    chunks = group // 128
    place = lax.axis_index("ctx")
    core_bit = ctx_bits
    up_bits = list(range(ctx_bits + 1, dev_bits))
    down_bits = up_bits[::-1]
    ctx_down = list(range(ctx_bits))[::-1]
    ctx_up = list(range(ctx_bits))

    vectors = jnp.concatenate(
        [
            query_offset,
            value_offset,
            attn_offset,
            attn_gain,
            attn_shift,
            outer_offset,
            final_gain,
            final_shift,
            inner_offset,
        ]
    ).astype(bf16)
    triple = jnp.stack([query_proj, key_proj, value_proj], axis=1).astype(bf16)
    by_group = triple.reshape(part, 3, n_ctx, group).transpose(2, 0, 1, 3)
    by_group = by_group.reshape(n_ctx, part, 3 * group)
    vector_rows = -(-vectors.shape[0] // (3 * group))
    vectors = jnp.pad(vectors, (0, vector_rows * 3 * group - vectors.shape[0]))
    vectors = vectors.reshape(vector_rows, 3 * group)
    vectors = jnp.pad(vectors, ((0, 16 - vector_rows), (0, 0)))
    packed = jnp.concatenate(
        [by_group, jnp.broadcast_to(vectors[None], (n_ctx,) + vectors.shape)], axis=1
    )

    first_shard = jnp.concatenate([attn_proj, inner_proj], axis=1).astype(bf16)
    w_first = lax.all_gather(first_shard, AXES, axis=0, tiled=True)
    w_outer = lax.all_gather(outer_proj.astype(bf16), AXES, axis=0, tiled=True)
    line = Process(gather_line(tokens))
    projections = Process(gather_group(packed, down_bits + [core_bit]))
    for turn in range(n_ctx - 1):
        together([line, projections])
        line.advance()
        projections.advance()
    tokens_all, packed = line.result, projections.finish()
    w_group = packed[:, :, :part].reshape(width, 3 * group)
    vectors = packed[:, :, part : part + vector_rows].reshape(n_dev, -1)
    names = [vectors[:, i * part : (i + 1) * part].reshape(width).astype(f32) for i in range(8)]
    b_query, b_value, b_attn, g_attn, s_attn, b_outer, g_final, s_final = names
    b_inner = vectors[:, 8 * part : 8 * part + hidden_part].reshape(1, hidden_width).astype(f32)

    b_group = lax.dynamic_slice_in_dim(
        jnp.stack([b_query, jnp.zeros_like(b_query), b_value]), place * group, group, 1
    ).reshape(3 * group)
    qkv = (jnp.dot(tokens_all, w_group, preferred_element_type=f32) + b_group).astype(bf16)
    where = jnp.stack(
        [place, lengths[0], own_bit(core_bit), lax.axis_index("dp") // 2]
    ).astype(jnp.int32)
    mixed_own, lse, mixed_parts = [], [], []
    for chunk in range(chunks):
        mixed_chunk, lse_chunk = attention_forward(qkv, where, rows, chunk, chunks)
        mixed_own.append(mixed_chunk)
        lse.append(lse_chunk)
        mixed_parts += exchange_slots(
            [mixed_chunk[slot * rows : (slot + 1) * rows] for slot in range(n_ctx)]
        )

    by_chunk = triple.reshape(part, 3, n_ctx, chunks, 128).transpose(0, 3, 2, 1, 4)
    by_chunk = by_chunk.reshape(part, 3 * width)
    by_chunk, _ = lax.optimization_barrier((by_chunk, qkv))
    w_triple = lax.all_gather(by_chunk, AXES, axis=0, tiled=True)
    none = jnp.zeros_like(b_attn)
    layer_vectors = jnp.stack([b_attn, g_attn, s_attn, b_outer, g_final, s_final, none, none])
    quads = n_dp // 2
    middle = layer_middle(
        where,
        tokens,
        cotangent,
        layer_vectors,
        b_inner,
        mixed_parts,
        n_ctx,
        (w_first, w_outer),
        quads,
    )
    layer_out, dfirst, sums, inner_sum = middle[:4]
    dmixed_slots = exchange_slots(middle[4 : 4 + n_ctx])

    gradients = middle[4 + n_ctx :]
    orders = (
        ctx_up[:1] + up_bits + ctx_up[1:],
        up_bits + ctx_up,
        down_bits + ctx_up,
    )
    sums_of, given = [], []
    for which, order in enumerate(orders):
        sent, kept = gradients[2 * which : 2 * which + 2]
        shard = sent.shape[0] * sent.shape[1] // 2 ** (dev_bits - 1)
        split = (2,) * (dev_bits - 1) + (shard, sent.shape[2])
        parts = [kept.reshape(split), swap(sent, core_bit).reshape(split)]
        sums_of.append(Process(scatter_sum(parts, order, f32, given)))
    dmixed_slots[0] = after(dmixed_slots[0], w_triple, *given)
    early = [sums[i].reshape(n_dev, part) for i in range(6)] + [inner_sum.reshape(n_dev, -1)]

    dqkv_rows, triples, late = [], [], []
    for chunk in range(chunks):
        dqkv = attention_backward(
            qkv, mixed_own[chunk], dmixed_slots, lse[chunk], where, chunk, chunks
        )
        if chunk == 0 and chunks > 1:
            together(sums_of[:2], dqkv)
            for one in sums_of[:2]:
                one.advance()
            dqkv_slots = [dqkv[slot * rows : (slot + 1) * rows] for slot in range(n_ctx)]
            dmixed_slots[0] = after(dmixed_slots[0], *given[3:], *dqkv_slots)
        dqkv_rows += exchange_slots(
            [dqkv[slot * rows : (slot + 1) * rows] for slot in range(n_ctx)]
        )
        grad_triple = lax.dot_general(
            tokens_all, dqkv, (((0,), (0,)), ((), ())), preferred_element_type=f32
        ).astype(bf16)
        triples.append(grad_triple.reshape((2,) * (dev_bits - ctx_bits) + (n_ctx, part, 384)))
        late.append(jnp.stack([row_sum(dqkv[:, :128]), row_sum(dqkv[:, 256:])]))
    triple_sum = jnp.concatenate(triples, axis=-1)
    together(sums_of, triple_sum, *dqkv_rows[:n_ctx])
    half_sum = triple_sum.reshape((quads, 2) + triple_sum.shape[dev_bits - ctx_bits :])
    half_sum = Process(scatter_core(half_sum, core_bit))
    for one in sums_of:
        one.advance()
    together(sums_of + [half_sum], *dqkv_rows[n_ctx:])
    half_sum.advance()
    triple_sum = Process(scatter_at_once(half_sum.result, up_bits))
    for one in sums_of:
        one.advance()
    together([one for one in sums_of if one.result is None] + [triple_sum])
    triple_sum.advance()
    triple_sum = Process(exchange_line(triple_sum.result))
    for one in sums_of:
        one.advance()
    triple_sum = triple_sum.finish()
    grad_triple = triple_sum.reshape(n_ctx, part, chunks, 3, 128).transpose(3, 1, 0, 2, 4)
    grad_triple = grad_triple.reshape(3, part, width).astype(f32)
    grad_left, grad_right, grad_outer = [one.finish() for one in sums_of]
    grad_attn = grad_left[:, :width]
    grad_inner = jnp.concatenate([grad_left[:, width:], grad_right], axis=1)
    late = jnp.concatenate(late, axis=1)
    late = lax.dynamic_update_slice_in_dim(
        jnp.zeros((2, width), f32), late, place * group, 1
    )
    late = late.reshape(2, n_dev, part).transpose(1, 0, 2).reshape(n_dev, 2 * part)
    early = jnp.concatenate(early + [late], axis=1)
    early = lax.all_to_all(early, AXES, 0, 0, tiled=True).sum(axis=0)
    late = early[early.shape[0] - 2 * part :].reshape(2, part)
    input_grad = input_gradient(where, dfirst, w_triple, dqkv_rows, n_ctx)

    pieces = [early[i * part : (i + 1) * part] for i in range(6)]
    return (
        layer_out,
        input_grad,
        grad_triple[0],
        late[0],
        grad_triple[1],
        grad_triple[2],
        late[1],
        grad_attn,
        pieces[3],
        pieces[4],
        pieces[5],
        grad_inner,
        early[6 * part : 6 * part + hidden_part],
        grad_outer,
        pieces[0],
        pieces[1],
        pieces[2],
    )


def solution(mesh):
    rows, vector = P(AXES, None), P(AXES)
    in_specs = (rows, P("dp"), rows, rows, vector, rows, rows, vector, rows) + (vector,) * 3
    in_specs += (rows, vector, rows) + (vector,) * 3
    out_specs = (rows,) * 3 + (vector, rows, rows, vector, rows) + (vector,) * 3
    out_specs += (rows, vector, rows) + (vector,) * 3
    return jax.shard_map(local, mesh=mesh, in_specs=in_specs, out_specs=out_specs, check_vma=False)
```

time: 689 us -> 528 us (0.77)
  waiting for transfers between devices: 241 us -> 160 us
  Pallas kernels: 83.6 us -> 157 us
  matrix products: 87.4 us -> 15.7 us
  local copies, waits for them, and re-layouts: 95.5 us -> 44.2 us
  blocking collectives: 39 us -> 0 us
    ppermute x31 -> x19, waiting for transfers between devices: 153 us -> 39 us  [swap(): return lax.ppermute(values, AXES, [(i, i ^ 1 << bit) for i in range(count)])]
    ppermute x0 -> x24, waiting for transfers between devices: none -> 79.2 us  [the longest x6 45.1 us: exchange_line(): lax.ppermute(lax.dynamic_index_in_dim(blocks, place ^ mask, 0, keepdims=F...]
    dot_general x11 -> x2, matrix products: 79.1 us -> 8.38 us  [local(): lax.dot_general(tokens_all, dqkv, (((0,), (0,)), ((), ())), preferred_ele...]
    pallas_call x0 -> x2, Pallas kernels: none -> 62.9 us  [the longest x1 54.8 us: layer_middle(): pl.pallas_call(functools.partial(layer_kernel, chunks=chunks, groups=grou...]
    ppermute x0 -> x24, starting transfers between devices: none -> 42 us  [the longest x15 25.6 us: exchange_slots(): lax.ppermute(slots[mask], 'ctx', [(i, i ^ mask) for i in range(count)])]
    all_to_all x1 -> x0, blocking collectives: 39 us -> none  [local(): packed = gather_dp(lax.all_to_all(packed, 'ctx', 0, 0, tiled=True))]
    ppermute x3, waiting for transfers between devices: 38 us -> 10.2 us  [gather_line(): lax.ppermute(from_right, 'ctx', [(i + 1, i) for i in range(count - 1)])]
    all_to_all x4 -> x1, starting transfers between devices: 19.3 us -> 2.82 us  [local(): early = lax.all_to_all(early, AXES, 0, 0, tiled=True).sum(axis=0)]
  transfers between devices with their start and end apart: 43 -> 53, of which waited for: 17 -> 17; matrix products, arithmetic and copies ran while one was open for 31% -> 18% of each run, Pallas kernels for 12% -> 30%
where the time goes in v2:
time: 528 us; the launch traced here: 524 us
  waiting for transfers between devices  160 us (30%)
  Pallas kernels  157 us (30%)
  starting transfers between devices  81.9 us (16%)
  other arithmetic  48 us (9%)
  local copies, waits for them, and re-layouts  44.2 us (8%)
  between operations  16.1 us (3%)
  matrix products  15.7 us (3%)
    pallas_call x2, Pallas kernels, attention_backward(): pl.pallas_call(functools.partial(attention_backward_kernel, heads=heads,...  55.1 us
    pallas_call x1, Pallas kernels, layer_middle(): pl.pallas_call(functools.partial(layer_kernel, chunks=chunks, groups=grou...  54.8 us
    ppermute x6, waiting for transfers between devices, exchange_line(): lax.ppermute(lax.dynamic_index_in_dim(blocks, place ^ mask, 0, keepdims=F...  45.1 us
    pallas_call x2, Pallas kernels, attention_forward(): pl.pallas_call(functools.partial(attention_forward_kernel, heads=heads, r...  39.4 us
    ppermute x19, waiting for transfers between devices, swap(): return lax.ppermute(values, AXES, [(i, i ^ 1 << bit) for i in range(count)])  39 us
    ppermute x15, waiting for transfers between devices, exchange_slots(): lax.ppermute(slots[mask], 'ctx', [(i, i ^ mask) for i in range(count)])  34.1 us
    ppermute x3, waiting for transfers between devices, gather_line(): lax.ppermute(from_left, 'ctx', [(i, i + 1) for i in range(count - 1)])  31.9 us
    convert_element_type x13, other arithmetic, total_of(): return total.astype(dtype)  26 us
  transfers between devices with their start and end apart: 53, of which 17 were waited for; matrix products, arithmetic and copies ran while one was open for 18% of the time, Pallas kernels for 30%

profile of v2, /device:TPU:0, one launch (start us, length us, event | category | flops | bytes accessed | tf_op | source)
XLA Modules:
  0.0 523.7 jit_solution(14670521427870507769)
XLA Ops:
  12.2 5.9 %collective-permute-start = (bf16[512,1024]{1,0:T(8,128)(2,1)S(1)}, bf16[512,1024]{1,0:T(8,128)(2,1)}, u32[]{:S(2)}, u32[]{:S(2)}) collective-permute-start(bf16[512,1024]{1,0:T(8,128)(2,1)S(1)} %copy-done.2), channel_id=1, source_target_pairs={{0,1},{1,2},{2,3},{4,5},{5,6},{6,7},{8,9},{9,10},{10,11},{12,13},{... | collective-permute-start | bytes 3145736 | tf_op jit(solution)/shard_map/ppermute | solution.py:583
  26.2 37.7 %collective-permute-done.2 = bf16[48,768]{1,0:T(8,128)(2,1)S(1)} collective-permute-done((bf16[48,768]{1,0:T(8,128)(2,1)S(1)}, bf16[48,768]{1,0:T(8,128)(2,1)S(1)}, u32[]{:S(2)}, u32[]{:S(2)}) %collective-permute-start.2) | collective-permute-done | bytes 73760 | tf_op jit(solution)/shard_map/ppermute | solution.py:609
  74.2 11.5 %collective-permute-done.7 = bf16[4,48,768]{2,1,0:T(8,128)(2,1)S(1)} collective-permute-done((bf16[4,48,768]{2,1,0:T(8,128)(2,1)S(1)}, bf16[4,48,768]{2,1,0:T(8,128)(2,1)S(1)}, u32[]{:S(2)}, u32[]{:S(2)}) %collective-permute-start.7) | collective-permute-done | bytes 294944 | tf_op jit(solution)/shard_map/ppermute | solution.py:557
  85.7 24.0 %collective-permute-done.5 = bf16[512,1024]{1,0:T(8,128)(2,1)} collective-permute-done((bf16[512,1024]{1,0:T(8,128)(2,1)}, bf16[512,1024]{1,0:T(8,128)(2,1)}, u32[]{:S(2)}, u32[]{:S(2)}) %collective-permute-start.5) | collective-permute-done | bytes 1048608 | tf_op jit(solution)/shard_map/ppermute | solution.py:583
  109.7 5.1 collective-permute-done.6
  123.7 10.1 %collective-permute-done.10 = bf16[2,4,48,768]{3,2,1,0:T(8,128)(2,1)S(1)} collective-permute-done((bf16[2,4,48,768]{3,2,1,0:T(8,128)(2,1)S(1)}, bf16[2,4,48,768]{3,2,1,0:T(8,128)(2,1)S(1)}, u32[]{:S(2)}, u32[]{:S(2)}) %collective-permute-start.10) | collective-permute-done | bytes 589856 | tf_op jit(solution)/shard_map/ppermute | solution.py:557
  133.8 7.9 %collective-permute-done.8 = bf16[512,1024]{1,0:T(8,128)(2,1)} collective-permute-done((bf16[512,1024]{1,0:T(8,128)(2,1)}, bf16[512,1024]{1,0:T(8,128)(2,1)}, u32[]{:S(2)}, u32[]{:S(2)}) %collective-permute-start.8) | collective-permute-done | bytes 1048608 | tf_op jit(solution)/shard_map/ppermute | solution.py:583
  141.8 5.1 collective-permute-done.9
  154.9 7.3 %add_convert_fusion.q_ref.k_ref.v_ref = bf16[2048,768]{1,0:T(8,128)(2,1)} fusion(bf16[2048,1024]{1,0:T(8,128)(2,1)} %bitcast.236, bf16[1024,768]{1,0:T(8,128)(2,1)S(1)} %bitcast.261, f32[768]{0:T(1024)S(1)} %add.451), kind=kOutput, calls=%fused_computation | convolution fusion | flops 3224371200 | bytes 8915968 | tf_op jit(solution)/shard_map/dot_general | solution.py:798
  163.5 19.9 %attention_forward.3 = (bf16[2048,128]{1,0:T(8,128)(2,1)}, f32[8,2048]{1,0:T(8,128)}) custom-call(s32[4]{0:T(128)} %pad_add_fusion.place_ref, bf16[2048,768]{1,0:T(8,128)(2,1)} %add_convert_fusion.q_ref.k_ref.v_ref, bf16[2048,768]{1,0:T(8,128)(2,1)} %add_convert_fusion.q_ref.k_ref.v_ref, bf16[2048,768]{1,0:T(8,128)(2,1)} %add_convert_fusion.q_ref.k_ref.v_ref), custom_call_target="tpu_custom_call" | custom-call | flops 1073741824 | bytes 2097152 | tf_op jit(solution)/shard_map/attention_forward/pallas_call | solution.py:64
  185.3 4.4 collective-permute-start.17
  189.7 19.4 %attention_forward.2 = (bf16[2048,128]{1,0:T(8,128)(2,1)}, f32[8,2048]{1,0:T(8,128)}) custom-call(s32[4]{0:T(128)} %pad_add_fusion.place_ref, bf16[2048,768]{1,0:T(8,128)(2,1)} %add_convert_fusion.q_ref.k_ref.v_ref, bf16[2048,768]{1,0:T(8,128)(2,1)} %add_convert_fusion.q_ref.k_ref.v_ref, bf16[2048,768]{1,0:T(8,128)(2,1)} %add_convert_fusion.q_ref.k_ref.v_ref), custom_call_target="tpu_custom_call" | custom-call | flops 1073741824 | bytes 2097152 | tf_op jit(solution)/shard_map/attention_forward/pallas_call | solution.py:64
  219.3 4.4 collective-permute-done.13.refs_2_
  224.4 54.8 %layer_middle.1 = (bf16[512,1024]{1,0:T(8,128)(2,1)}, f32[512,1024]{1,0:T(8,128)}, f32[8,1024]{1,0:T(8,128)}, f32[1,4096]{1,0:T(1,128)}, bf16[512,256]{1,0:T(8,1...) custom-call(s32[4]{0:T(128)} %pad_add_fusion.place_ref, ...), custom_call_target="tpu_custom_call" | custom-call | flops 4026531840 | bytes 42991616 | tf_op jit(solution)/shard_map/layer_middle/pallas_call | solution.py:469
  287.5 8.6 %collective-permute-done.18 = bf16[4,128,2048]{2,1,0:T(8,128)(2,1)} collective-permute-done((bf16[4,128,2048]{2,1,0:T(8,128)(2,1)}, bf16[4,128,2048]{2,1,0:T(8,128)(2,1)}, u32[]{:S(2)}, u32[]{:S(2)}) %collective-permute-start.18) | collective-permute-done | bytes 2097184 | tf_op jit(solution)/shard_map/ppermute | solution.py:557
  315.7 27.6 %attention_backward.2 = bf16[2048,384]{1,0:T(8,128)(2,1)} custom-call(s32[4]{0:T(128)} %pad_add_fusion.place_ref, bf16[2048,768]{1,0:T(8,128)(2,1)} %add_convert_fusion.q_ref.k_ref.v_ref, bf16[2048,768]{1,0:T(8,128)(2,1)} %add_convert_fusion.q_ref.k_ref.v_ref, bf16[2048,768]{1,0:T(8,128)(2,1)} %add_convert_fusion.q_ref.k_ref.v_ref, ...), custom_call_target="tpu_custom_call" | custom-call | flops 2684354560 | bytes 4194304 | tf_op jit(solution)/shard_map/attention_backward/pallas_call | solution.py:177
  361.2 27.5 %attention_backward.3 = bf16[2048,384]{1,0:T(8,128)(2,1)} custom-call(s32[4]{0:T(128)} %pad_add_fusion.place_ref, bf16[2048,768]{1,0:T(8,128)(2,1)} %add_convert_fusion.q_ref.k_ref.v_ref, bf16[2048,768]{1,0:T(8,128)(2,1)} %add_convert_fusion.q_ref.k_ref.v_ref, bf16[2048,768]{1,0:T(8,128)(2,1)} %add_convert_fusion.q_ref.k_ref.v_ref, ...), custom_call_target="tpu_custom_call" | custom-call | flops 2684354560 | bytes 4194304 | tf_op jit(solution)/shard_map/attention_backward/pallas_call | solution.py:177
  388.7 5.1 convolution_convert_fusion
  398.6 7.7 %collective-permute-done.26.refs_3_ = bf16[512,384]{1,0:T(8,128)(2,1)S(1)} collective-permute-done((bf16[512,384]{1,0:T(8,128)(2,1)S(1)}, bf16[512,384]{1,0:T(8,128)(2,1)S(1)}, u32[]{:S(2)}, u32[]{:S(2)}) %collective-permute-start.26) | collective-permute-done | bytes 393248 | tf_op jit(solution)/shard_map/ppermute | solution.py:600
  406.3 7.2 %collective-permute-start.29 = (bf16[512,384]{1,0:T(8,128)(2,1)S(1)}, bf16[512,384]{1,0:T(8,128)(2,1)S(1)}, u32[]{:S(2)}, u32[]{:S(2)}) collective-permute-start(bf16[512,384]{1,0:T(8,128)(2,1)S(1)} %get-tuple-element.127), channel_id=1, source_target_pairs={{0,1},{1,0},{2,3},{3,2},{4,5},{5,4},{6,7},{7,6},{8,9},{9,8},{10,11... | collective-permute-start | bytes 1179656 | tf_op jit(solution)/shard_map/ppermute | solution.py:600
  421.7 5.4 %collective-permute-done.29.refs_5_ = bf16[512,384]{1,0:T(8,128)(2,1)S(1)} collective-permute-done((bf16[512,384]{1,0:T(8,128)(2,1)S(1)}, bf16[512,384]{1,0:T(8,128)(2,1)S(1)}, u32[]{:S(2)}, u32[]{:S(2)}) %collective-permute-start.29) | collective-permute-done | bytes 393248 | tf_op jit(solution)/shard_map/ppermute | solution.py:600
  429.1 14.2 %collective-permute-done.30.refs_6_ = bf16[512,384]{1,0:T(8,128)(2,1)S(1)} collective-permute-done((bf16[512,384]{1,0:T(8,128)(2,1)S(1)}, bf16[512,384]{1,0:T(8,128)(2,1)S(1)}, u32[]{:S(2)}, u32[]{:S(2)}) %collective-permute-start.30) | collective-permute-done | bytes 393248 | tf_op jit(solution)/shard_map/ppermute | solution.py:600
  473.4 8.7 %collective-permute-done.39 = bf16[32,2048]{1,0:T(8,128)(2,1)S(1)} collective-permute-done((bf16[32,2048]{1,0:T(8,128)(2,1)S(1)}, bf16[32,2048]{1,0:T(8,128)(2,1)S(1)}, u32[]{:S(2)}, u32[]{:S(2)}) %collective-permute-start.39) | collective-permute-done | bytes 131104 | tf_op jit(solution)/shard_map/ppermute | solution.py:557
  486.1 8.1 %input_gradient.1 = bf16[512,1024]{1,0:T(8,128)(2,1)} custom-call(s32[4]{0:T(128)S(1)} %copy-done.1, f32[512,1024]{1,0:T(8,128)S(1)} %copy-done, bf16[1024,3072]{1,0:T(8,128)(2,1)} %all-gather.8.cloned.1.call-done.weights_ref, bf16[512,384]{1,0:T(8,128)(2,1)S(1)} %get-tuple-element.132.refs_0_, bf16[512,384]{1,0:T(8,128)(2,1)S(1)} %collective-permute-done.24.refs_1_, ...), custom_call_target="tpu_custom_call" | custom-call | flops 402653184 | bytes 12582912 | tf_op jit(solution)/shard_map/input_gradient/pallas_call | solution.py:531
  (348 shorter events, 169.8 us)
Async XLA Ops:
  7.2 216.5 %all-gather.6.cloned.1.call-start = ((), (), s32[]{:S(2)}) async-start(), calls=%async_computation.2 | async-start | bytes 8650752 | tf_op jit(solution)/shard_map/all_gather | solution.py:781
  9.2 214.6 %all-gather.4.cloned.1.call-start = ((), (), s32[]{:S(2)}) async-start(), calls=%async_computation.1 | async-start | bytes 10813440 | tf_op jit(solution)/shard_map/all_gather | solution.py:780
  12.1 301.2 %all-gather.8.cloned.1.call-start = ((), (), s32[]{:S(2)}) async-start(), calls=%async_computation.3 | async-start | bytes 6488064 | tf_op jit(solution)/shard_map/all_gather | solution.py:814
  12.2 54.8 %collective-permute-start = (bf16[512,1024]{1,0:T(8,128)(2,1)S(1)}, bf16[512,1024]{1,0:T(8,128)(2,1)}, u32[]{:S(2)}, u32[]{:S(2)}) collective-permute-start(bf16[512,1024]{1,0:T(8,128)(2,1)S(1)} %copy-done.2), channel_id=1, source_target_pairs={{0,1},{1,2},{2,3},{4,5},{5,6},{6,7},{8,9},{9,10},{10,11},{12,13},{... | collective-permute-start | bytes 3145736 | tf_op jit(solution)/shard_map/ppermute | solution.py:583
  18.1 48.9 %collective-permute-start.1 = (bf16[512,1024]{1,0:T(8,128)(2,1)S(1)}, bf16[512,1024]{1,0:T(8,128)(2,1)S(1)}, u32[]{:S(2)}, u32[]{:S(2)}) collective-permute-start(bf16[512,1024]{1,0:T(8,128)(2,1)S(1)} %copy-done.2), channel_id=1, source_target_pairs={{1,0},{2,1},{3,2},{5,4},{6,5},{7,6},{9,8},{10,9},{11,10},{13,12},{... | collective-permute-start | bytes 3145736 | tf_op jit(solution)/shard_map/ppermute | solution.py:584
  21.0 42.9 %collective-permute-start.2 = (bf16[48,768]{1,0:T(8,128)(2,1)S(1)}, bf16[48,768]{1,0:T(8,128)(2,1)S(1)}, u32[]{:S(2)}, u32[]{:S(2)}) collective-permute-start(bf16[48,768]{1,0:T(8,128)(2,1)S(1)} %get-tuple-element.150), channel_id=1, source_target_pairs={{0,1},{1,0},{2,3},{3,2},{4,5},{5,4},{6,7},{7,6},{8,9},{9,8},{10,11... | collective-permute-start | bytes 221192 | tf_op jit(solution)/shard_map/ppermute | solution.py:609
  23.7 43.2 %collective-permute-start.3 = (bf16[48,768]{1,0:T(8,128)(2,1)S(1)}, bf16[48,768]{1,0:T(8,128)(2,1)S(1)}, u32[]{:S(2)}, u32[]{:S(2)}) collective-permute-start(bf16[48,768]{1,0:T(8,128)(2,1)S(1)} %get-tuple-element.151), channel_id=1, source_target_pairs={{0,2},{1,3},{2,0},{3,1},{4,6},{5,7},{6,4},{7,5},{8,10},{9,11},{10,... | collective-permute-start | bytes 221192 | tf_op jit(solution)/shard_map/ppermute | solution.py:609
  25.4 41.6 %collective-permute-start.4 = (bf16[48,768]{1,0:T(8,128)(2,1)S(1)}, bf16[48,768]{1,0:T(8,128)(2,1)S(1)}, u32[]{:S(2)}, u32[]{:S(2)}) collective-permute-start(bf16[48,768]{1,0:T(8,128)(2,1)S(1)} %get-tuple-element.149), channel_id=1, source_target_pairs={{0,3},{1,2},{2,1},{3,0},{4,7},{5,6},{6,5},{7,4},{8,11},{9,10},{10,... | collective-permute-start | bytes 221192 | tf_op jit(solution)/shard_map/ppermute | solution.py:609
  67.0 42.8 %collective-permute-start.5 = (bf16[512,1024]{1,0:T(8,128)(2,1)}, bf16[512,1024]{1,0:T(8,128)(2,1)}, u32[]{:S(2)}, u32[]{:S(2)}) collective-permute-start(bf16[512,1024]{1,0:T(8,128)(2,1)} %collective-permute-done), channel_id=1, source_target_pairs={{0,1},{1,2},{2,3},{4,5},{5,6},{6,7},{8,9},{9,10},{10,11},{12,13},{... | collective-permute-start | bytes 3145736 | tf_op jit(solution)/shard_map/ppermute | solution.py:583
  71.3 43.6 %collective-permute-start.6 = (bf16[512,1024]{1,0:T(8,128)(2,1)S(1)}, bf16[512,1024]{1,0:T(8,128)(2,1)}, u32[]{:S(2)}, u32[]{:S(2)}) collective-permute-start(bf16[512,1024]{1,0:T(8,128)(2,1)S(1)} %collective-permute-done.1), channel_id=1, source_target_pairs={{1,0},{2,1},{3,2},{5,4},{6,5},{7,6},{9,8},{10,9},{11,10},{13,12},{... | collective-permute-start | bytes 3145736 | tf_op jit(solution)/shard_map/ppermute | solution.py:584
  279.9 33.5 %collective-permute-start.21 = (bf16[512,256]{1,0:T(8,128)(2,1)}, bf16[512,256]{1,0:T(8,128)(2,1)S(1)}, u32[]{:S(2)}, u32[]{:S(2)}) collective-permute-start(bf16[512,256]{1,0:T(8,128)(2,1)} %get-tuple-element.89), channel_id=1, source_target_pairs={{0,1},{1,0},{2,3},{3,2},{4,5},{5,4},{6,7},{7,6},{8,9},{9,8},{10,11... | collective-permute-start | bytes 786440 | tf_op jit(solution)/shard_map/ppermute | solution.py:600
  282.1 32.8 %collective-permute-start.22 = (bf16[512,256]{1,0:T(8,128)(2,1)}, bf16[512,256]{1,0:T(8,128)(2,1)S(1)}, u32[]{:S(2)}, u32[]{:S(2)}) collective-permute-start(bf16[512,256]{1,0:T(8,128)(2,1)} %get-tuple-element.90), channel_id=1, source_target_pairs={{0,2},{1,3},{2,0},{3,1},{4,6},{5,7},{6,4},{7,5},{8,10},{9,11},{10,... | collective-permute-start | bytes 786440 | tf_op jit(solution)/shard_map/ppermute | solution.py:600
  301.1 54.2 %collective-permute-start.27 = (bf16[2,2,2,32,2048]{4,3,2,0,1:T(8,128)(2,1)}, bf16[2,2,2,32,2048]{4,3,2,0,1:T(8,128)(2,1)S(1)}, u32[]{:S(2)}, u32[]{:S(2)}) collective-permute-start(bf16[2,2,2,32,2048]{4,3,2,0,1:T(8,128)(2,1)} %fusion.4), channel_id=1, source_target_pairs={{0,1},{1,0},{2,3},{3,2},{4,5},{5,4},{6,7},{7,6},{8,9},{9,8},{10,11... | collective-permute-start | bytes 3145736 | tf_op jit(solution)/shard_map/ppermute | solution.py:557
  308.3 47.0 %collective-permute-start.28 = (bf16[2,2,2,32,3072]{4,3,2,1,0:T(8,128)(2,1)}, bf16[2,2,2,32,3072]{4,3,2,1,0:T(8,128)(2,1)}, u32[]{:S(2)}, u32[]{:S(2)}) collective-permute-start(bf16[2,2,2,32,3072]{4,3,2,1,0:T(8,128)(2,1)} %fusion.1), channel_id=1, source_target_pairs={{0,8},{1,9},{2,10},{3,11},{4,12},{5,13},{6,14},{7,15},{8,0},{9,1},... | collective-permute-start | bytes 4718600 | tf_op jit(solution)/shard_map/ppermute | solution.py:557
  313.4 102.4 %collective-permute-start.34 = (bf16[2,2,2,128,1024]{4,3,2,1,0:T(8,128)(2,1)}, bf16[2,2,2,128,1024]{4,3,2,1,0:T(8,128)(2,1)}, u32[]{:S(2)}, u32[]{:S(2)}) collective-permute-start(bf16[2,2,2,128,1024]{4,3,2,1,0:T(8,128)(2,1)} %bitcast.258), channel_id=1, source_target_pairs={{0,16},{1,17},{2,18},{3,19},{4,20},{5,21},{6,22},{7,23},{8,24},{9,... | collective-permute-start | bytes 6291464 | tf_op jit(solution)/shard_map/ppermute | solution.py:557
  345.9 49.5 %collective-permute-start.24 = (bf16[512,384]{1,0:T(8,128)(2,1)}, bf16[512,384]{1,0:T(8,128)(2,1)S(1)}, u32[]{:S(2)}, u32[]{:S(2)}) collective-permute-start(bf16[512,384]{1,0:T(8,128)(2,1)} %get-tuple-element.131), channel_id=1, source_target_pairs={{0,1},{1,0},{2,3},{3,2},{4,5},{5,4},{6,7},{7,6},{8,9},{9,8},{10,11... | collective-permute-start | bytes 1179656 | tf_op jit(solution)/shard_map/ppermute | solution.py:600
  346.5 52.1 %collective-permute-start.25 = (bf16[512,384]{1,0:T(8,128)(2,1)}, bf16[512,384]{1,0:T(8,128)(2,1)S(1)}, u32[]{:S(2)}, u32[]{:S(2)}) collective-permute-start(bf16[512,384]{1,0:T(8,128)(2,1)} %get-tuple-element.130), channel_id=1, source_target_pairs={{0,2},{1,3},{2,0},{3,1},{4,6},{5,7},{6,4},{7,5},{8,10},{9,11},{10,... | collective-permute-start | bytes 1179656 | tf_op jit(solution)/shard_map/ppermute | solution.py:600
  358.6 54.8 %collective-permute-start.33 = (bf16[2,2,32,3072]{3,2,1,0:T(8,128)(2,1)}, bf16[2,2,32,3072]{3,2,1,0:T(8,128)(2,1)}, u32[]{:S(2)}, u32[]{:S(2)}) collective-permute-start(bf16[2,2,32,3072]{3,2,1,0:T(8,128)(2,1)} %fusion.3), channel_id=1, source_target_pairs={{0,16},{1,17},{2,18},{3,19},{4,20},{5,21},{6,22},{7,23},{8,24},{9,... | collective-permute-start | bytes 2359304 | tf_op jit(solution)/shard_map/ppermute | solution.py:557
  360.6 52.9 %collective-permute-start.32 = (bf16[2,2,32,2048]{3,2,1,0:T(8,128)(2,1)}, bf16[2,2,32,2048]{3,2,1,0:T(8,128)(2,1)}, u32[]{:S(2)}, u32[]{:S(2)}) collective-permute-start(bf16[2,2,32,2048]{3,2,1,0:T(8,128)(2,1)} %fusion.11), channel_id=1, source_target_pairs={{0,8},{1,9},{2,10},{3,11},{4,12},{5,13},{6,14},{7,15},{8,0},{9,1},... | collective-permute-start | bytes 1572872 | tf_op jit(solution)/shard_map/ppermute | solution.py:557
  398.6 61.5 %collective-permute-start.38 = (bf16[4,4,32,768]{3,2,1,0:T(8,128)(2,1)}, bf16[4,4,32,768]{3,2,1,0:T(8,128)(2,1)}, u32[]{:S(2)}, u32[]{:S(2)}) collective-permute-start(bf16[4,4,32,768]{3,2,1,0:T(8,128)(2,1)} %fusion.7), channel_id=1, source_target_pairs={{0,4},{1,5},{2,6},{3,7},{4,0},{5,1},{6,2},{7,3},{8,12},{9,13},{10,... | collective-permute-start | bytes 2359304 | tf_op jit(solution)/shard_map/ppermute | solution.py:557
  413.5 46.5 %collective-permute-start.31 = (bf16[512,384]{1,0:T(8,128)(2,1)}, bf16[512,384]{1,0:T(8,128)(2,1)S(1)}, u32[]{:S(2)}, u32[]{:S(2)}) collective-permute-start(bf16[512,384]{1,0:T(8,128)(2,1)} %get-tuple-element.125), channel_id=1, source_target_pairs={{0,3},{1,2},{2,1},{3,0},{4,7},{5,6},{6,5},{7,4},{8,11},{9,10},{10,... | collective-permute-start | bytes 1179656 | tf_op jit(solution)/shard_map/ppermute | solution.py:600
  418.5 41.5 %collective-permute-start.37 = (bf16[2,2,128,1024]{3,2,1,0:T(8,128)(2,1)}, bf16[2,2,128,1024]{3,2,1,0:T(8,128)(2,1)}, u32[]{:S(2)}, u32[]{:S(2)}) collective-permute-start(bf16[2,2,128,1024]{3,2,1,0:T(8,128)(2,1)} %fusion), channel_id=1, source_target_pairs={{0,8},{1,9},{2,10},{3,11},{4,12},{5,13},{6,14},{7,15},{8,0},{9,1},... | collective-permute-start | bytes 3145736 | tf_op jit(solution)/shard_map/ppermute | solution.py:557
  427.2 32.9 %collective-permute-start.36 = (bf16[2,32,3072]{2,1,0:T(8,128)(2,1)}, bf16[2,32,3072]{2,1,0:T(8,128)(2,1)}, u32[]{:S(2)}, u32[]{:S(2)}) collective-permute-start(bf16[2,32,3072]{2,1,0:T(8,128)(2,1)} %fusion.10), channel_id=1, source_target_pairs={{0,1},{1,0},{2,3},{3,2},{4,5},{5,4},{6,7},{7,6},{8,9},{9,8},{10,11... | collective-permute-start | bytes 1179656 | tf_op jit(solution)/shard_map/ppermute | solution.py:557
  461.7 32.6 %collective-permute-start.42 = (bf16[4,32,768]{2,1,0:T(8,128)(2,1)S(1)}, bf16[4,32,768]{2,1,0:T(8,128)(2,1)S(1)}, u32[]{:S(2)}, u32[]{:S(2)}) collective-permute-start(bf16[4,32,768]{2,1,0:T(8,128)(2,1)S(1)} %get-tuple-element.135), channel_id=1, source_target_pairs={{0,8},{1,9},{2,10},{3,11},{4,12},{5,13},{6,14},{7,15},{8,0},{9,1},... | collective-permute-start | bytes 589832 | tf_op jit(solution)/shard_map/ppermute | solution.py:672
  (84 other events, 1075.8 us)
Sparse Core Ops, SparseCore 0:
  11.6 98.3 all-gather.5
  113.4 103.2 all-gather.3
  219.5 70.7 all-gather.7

commit v3 on v2

--- a/solution.py
+++ b/solution.py
@@ -101,7 +101,7 @@
     rows,
 ):
     step = pl.program_id(0)
-    dmixed_refs, (out_ref, keys_t_ref, dk_sum, dv_sum, dmixed_ref) = refs[:-5], refs[-5:]
+    dmixed_refs, (out_ref, placed_ref, keys_t_ref, dk_sum, dv_sum, dmixed_ref) = refs[:-6], refs[-6:]
     seq, width = dk_sum.shape
     for slot, slot_ref in enumerate(dmixed_refs):
 
@@ -167,6 +167,8 @@
     def _():
         out_ref[:, width : 2 * width] = (dk_sum[...] * score_scale).astype(bf16)
         out_ref[:, 2 * width :] = dv_sum[...].astype(bf16)
+        for slot in range(seq // rows):
+            placed_ref[place_ref[0] ^ slot] = out_ref[slot * rows : (slot + 1) * rows, :]
 
 
 def attention_backward(qkv, mixed, dmixed_slots, lse, place, chunk, chunks):
@@ -186,8 +188,14 @@
             pl.BlockSpec((8, rows), lambda i: (0, i)),
         ]
         + [pl.BlockSpec((rows, width), lambda i: (0, chunk))] * len(dmixed_slots),
-        out_specs=pl.BlockSpec((seq, 3 * width), lambda i: (0, 0)),
-        out_shape=jax.ShapeDtypeStruct((seq, 3 * width), bf16),
+        out_specs=[
+            pl.BlockSpec((seq, 3 * width), lambda i: (0, 0)),
+            pl.BlockSpec((seq // rows, rows, 3 * width), lambda i: (0, 0, 0)),
+        ],
+        out_shape=[
+            jax.ShapeDtypeStruct((seq, 3 * width), bf16),
+            jax.ShapeDtypeStruct((seq // rows, rows, 3 * width), bf16),
+        ],
         scratch_shapes=[
             pltpu.VMEM((width, seq), bf16),
             pltpu.VMEM((seq, width), f32),
@@ -217,7 +225,7 @@
     mixed_refs, refs = refs[: chunks * groups], refs[chunks * groups :]
     weight_refs, refs = refs[:2], refs[2:]
     (layer_out_ref, dfirst_ref, sums_ref, inner_sum_ref), refs = refs[:4], refs[4:]
-    dmixed_refs, gradient_refs, refs = refs[:groups], refs[groups : groups + 6], refs[groups + 6 :]
+    dmixed_refs, gradient_refs, refs = refs[:groups], refs[groups : groups + 4], refs[groups + 4 :]
     (w_attn, w_inner, w_outer), refs = refs[:3], refs[3:]
     (mixed_ref, hidden_ref, act_ref, douter_ref, dpre_ref, dattn_ref), refs = refs[:6], refs[6:]
     (wide_ref, normed_ref, inverse_ref, total_ref, dmixed_ref, turned_ref, sems) = refs
@@ -344,23 +352,29 @@
 
     quads = gradient_refs[0].shape[0]
     slab, outer_slab = width // (2 * quads), hidden_width // (2 * quads)
-    left_width = gradient_refs[0].shape[2]
     down = (((0,), (0,)), ((), ()))
 
-    def leave(first_sem, plan, height):
+    def leave(first_sem, source, which, to_col, height):
         started = []
-        for source, from_col, cols, which, to_col in plan:
-            for side in range(2):
-                owner = 1 - core if side == 0 else core
-                for slot in range(quads):
-                    row = pl.multiple_of((2 * (slot ^ quad) + owner) * height, height)
-                    copy = pltpu.make_async_copy(
-                        source.at[pl.ds(row, height), from_col : from_col + cols],
-                        gradient_refs[2 * which + side].at[slot, :, to_col : to_col + cols],
-                        sems.at[first_sem + len(started)],
-                    )
-                    copy.start()
-                    started.append(copy)
+        levels = quads.bit_length() - 1
+        if which == 0:
+            order = [
+                sum(((slot >> i) & 1) << (levels - 1 - i) for i in range(levels))
+                for slot in range(quads)
+            ]
+        else:
+            order = list(range(quads))
+        for side in range(2):
+            owner = 1 - core if side == 0 else core
+            for slot in range(quads):
+                row = pl.multiple_of((2 * (order[slot] ^ quad) + owner) * height, height)
+                copy = pltpu.make_async_copy(
+                    source.at[pl.ds(row, height), :],
+                    gradient_refs[2 * which + side].at[slot, :, to_col : to_col + source.shape[1]],
+                    sems.at[first_sem + len(started)],
+                )
+                copy.start()
+                started.append(copy)
         return started
 
     def outer_gradient(turn, carried):
@@ -372,7 +386,7 @@
         return carried
 
     lax.fori_loop(0, hidden_width // block, outer_gradient, 0)
-    leaving = leave(3, ((w_outer, 0, width, 2, 0),), outer_slab)
+    leaving = leave(3, w_outer, 1, 0, outer_slab)
 
     def back_in(turn, carried):
         span = pl.ds(pl.multiple_of(turn * narrow, narrow), narrow)
@@ -427,20 +441,13 @@
         return carried
 
     lax.fori_loop(0, hidden_width // wide_block, inner_gradient, 0)
-    leaving += leave(
-        3 + len(leaving),
-        (
-            (w_inner, left_width - width, hidden_width + width - left_width, 1, 0),
-            (w_inner, 0, left_width - width, 0, width),
-        ),
-        slab,
-    )
+    leaving += leave(3 + len(leaving), w_inner, 0, width, slab)
     turned_ref[...] = mixed_ref[...].T
     for half in range(width // block):
         rows_of = slice(half * block, (half + 1) * block)
         terms = jnp.dot(turned_ref[rows_of, :], dattn_ref[...], preferred_element_type=f32)
         w_attn[rows_of, :] = terms.astype(bf16)
-    leaving += leave(3 + len(leaving), ((w_attn, 0, width, 0, 0),), slab)
+    leaving += leave(3 + len(leaving), w_attn, 0, 0, slab)
     for copy in leaving:
         copy.wait()
 
@@ -451,7 +458,6 @@
     chunk_width = mixed_parts[0].shape[1]
     chunks = len(mixed_parts) // groups
     slab, outer_slab = width // (2 * quads), hidden_width // (2 * quads)
-    left_width = 2 * width
     vmem = pl.BlockSpec(memory_space=pltpu.VMEM)
     anywhere = pl.BlockSpec(memory_space=pl.ANY)
     shapes = [
@@ -461,8 +467,7 @@
         jax.ShapeDtypeStruct((1, hidden_width), f32),
     ] + [jax.ShapeDtypeStruct((rows, chunks * chunk_width), bf16)] * groups
     gradients = [
-        jax.ShapeDtypeStruct((quads, slab, left_width), bf16),
-        jax.ShapeDtypeStruct((quads, slab, width + hidden_width - left_width), bf16),
+        jax.ShapeDtypeStruct((quads, slab, width + hidden_width), bf16),
         jax.ShapeDtypeStruct((quads, outer_slab, width), bf16),
     ]
     gradients = [shape for shape in gradients for _ in range(2)]
@@ -471,7 +476,7 @@
         in_specs=[pl.BlockSpec(memory_space=pltpu.SMEM)]
         + [vmem] * (4 + chunks * groups)
         + [anywhere] * 2,
-        out_specs=[vmem] * len(shapes) + [anywhere] * 6,
+        out_specs=[vmem] * len(shapes) + [anywhere] * 4,
         out_shape=shapes + gradients,
         scratch_shapes=[
             pltpu.VMEM((width, width), bf16),
@@ -489,7 +494,7 @@
             pltpu.VMEM((rows, width), f32),
             pltpu.VMEM((rows, width), bf16),
             pltpu.VMEM((width, rows), bf16),
-            pltpu.SemaphoreType.DMA((3 + 8 * quads,)),
+            pltpu.SemaphoreType.DMA((3 + 6 * quads,)),
         ],
         compiler_params=pltpu.CompilerParams(vmem_limit_bytes=60 * 2**20),
         cost_estimate=pl.CostEstimate(
@@ -501,15 +506,22 @@
     )(place, tokens, cotangent, vectors, inner_offset, *mixed_parts, *weights)
 
 
-def input_kernel(place_ref, dfirst_ref, weights_ref, *refs, chunks, groups):
-    parts, (out_ref, rows_ref) = refs[:-2], refs[-2:]
-    cols = parts[0].shape[1]
-    for chunk in range(chunks):
+def input_kernel(place_ref, dfirst_ref, weights_ref, *refs, slotted, placed, groups):
+    slots, parts, (out_ref, rows_ref) = refs[:slotted], refs[slotted:-2], refs[-2:]
+    cols = weights_ref.shape[1] // (groups * (slotted // groups + placed))
+    chunk = 0
+    for first in range(0, slotted, groups):
         for slot in range(groups):
             start = (chunk * groups + (place_ref[0] ^ slot)) * cols
             span = pl.ds(pl.multiple_of(start, cols), cols)
-            rows_ref[:, span] = parts[chunk * groups + slot][...]
-    block = 256
+            rows_ref[:, span] = slots[first + slot][...]
+        chunk += 1
+    for part in parts:
+        for group in range(groups):
+            start = (chunk * groups + group) * cols
+            rows_ref[:, start : start + cols] = part[group]
+        chunk += 1
+    block = 512
 
     def columns(turn, carried):
         span = pl.ds(pl.multiple_of(turn * block, block), block)
@@ -525,12 +537,13 @@
     lax.fori_loop(0, out_ref.shape[1] // block, columns, 0)
 
 
-def input_gradient(place, dfirst, weights, parts, groups):
+def input_gradient(place, dfirst, weights, slots, parts, groups):
     rows, width = dfirst.shape
     vmem = pl.BlockSpec(memory_space=pltpu.VMEM)
+    given = list(slots) + list(parts)
     return pl.pallas_call(
-        functools.partial(input_kernel, chunks=len(parts) // groups, groups=groups),
-        in_specs=[pl.BlockSpec(memory_space=pltpu.SMEM)] + [vmem] * (2 + len(parts)),
+        functools.partial(input_kernel, slotted=len(slots), placed=len(parts), groups=groups),
+        in_specs=[pl.BlockSpec(memory_space=pltpu.SMEM)] + [vmem] * (2 + len(given)),
         out_specs=vmem,
         out_shape=jax.ShapeDtypeStruct((rows, width), bf16),
         scratch_shapes=[pltpu.VMEM((rows, weights.shape[1]), bf16)],
@@ -541,7 +554,7 @@
             transcendentals=0,
         ),
         name="input_gradient",
-    )(place, dfirst, weights, *parts)
+    )(place, dfirst, weights, *given)
 
 
 def device_index():
@@ -633,19 +646,20 @@
 
 
 def scatter_sum(parts, bit_order, out_dtype, sent):
-    left = sorted(bit_order, reverse=True)
+    left = sorted([bit for bit in bit_order if bit < bits_of(lax.axis_size("ctx"))], reverse=True)
     for bit in bit_order:
-        axis, mine = left.index(bit), own_bit(bit)
-        if bit >= bits_of(lax.axis_size("ctx")):
-            given = [lax.index_in_dim(part, 1, axis, keepdims=False) for part in parts]
-            parts = [lax.index_in_dim(part, 0, axis, keepdims=False) for part in parts]
+        if bit not in left:
+            given, parts = [part[1] for part in parts], [part[0] for part in parts]
         else:
+            axis, mine = left.index(bit), own_bit(bit)
             given = [lax.dynamic_index_in_dim(part, 1 - mine, axis, False) for part in parts]
             parts = [lax.dynamic_index_in_dim(part, mine, axis, False) for part in parts]
         given = total_of(given, parts[0].dtype)
         sent.append(given)
-        parts = parts + (yield [swap(given, bit)])
-        left.remove(bit)
+        kept = total_of(parts, parts[0].dtype)
+        parts = [kept] + (yield [swap(given, bit)])
+        if bit in left:
+            left.remove(bit)
     return total_of(parts, out_dtype)
 
 
@@ -831,9 +845,8 @@
 
     gradients = middle[4 + n_ctx :]
     orders = (
-        ctx_up[:1] + up_bits + ctx_up[1:],
         up_bits + ctx_up,
-        down_bits + ctx_up,
+        down_bits + ctx_down,
     )
     sums_of, given = [], []
     for which, order in enumerate(orders):
@@ -845,36 +858,38 @@
     dmixed_slots[0] = after(dmixed_slots[0], w_triple, *given)
     early = [sums[i].reshape(n_dev, part) for i in range(6)] + [inner_sum.reshape(n_dev, -1)]
 
-    dqkv_rows, triples, late = [], [], []
+    dqkv_chunks, dqkv_slots, dqkv_parts, triples, late = [], [], [], [], []
     for chunk in range(chunks):
-        dqkv = attention_backward(
+        dqkv, dqkv_placed = attention_backward(
             qkv, mixed_own[chunk], dmixed_slots, lse[chunk], where, chunk, chunks
         )
-        if chunk == 0 and chunks > 1:
-            together(sums_of[:2], dqkv)
-            for one in sums_of[:2]:
-                one.advance()
-            dqkv_slots = [dqkv[slot * rows : (slot + 1) * rows] for slot in range(n_ctx)]
-            dmixed_slots[0] = after(dmixed_slots[0], *given[3:], *dqkv_slots)
-        dqkv_rows += exchange_slots(
-            [dqkv[slot * rows : (slot + 1) * rows] for slot in range(n_ctx)]
-        )
+        if chunk < chunks - 1:
+            slots = [dqkv[slot * rows : (slot + 1) * rows] for slot in range(n_ctx)]
+            dqkv_slots += exchange_slots(slots)
+            dmixed_slots[0] = after(dmixed_slots[0], *slots)
+        else:
+            dqkv_parts.append(lax.all_to_all(dqkv_placed, "ctx", 0, 0, tiled=True))
+        dqkv_chunks.append(dqkv)
+
+    together(sums_of, dqkv, *dqkv_slots)
+    for one in sums_of:
+        one.advance()
+    for dqkv in dqkv_chunks:
+        dqkv = after(dqkv, *given[-2:])
         grad_triple = lax.dot_general(
             tokens_all, dqkv, (((0,), (0,)), ((), ())), preferred_element_type=f32
         ).astype(bf16)
         triples.append(grad_triple.reshape((2,) * (dev_bits - ctx_bits) + (n_ctx, part, 384)))
         late.append(jnp.stack([row_sum(dqkv[:, :128]), row_sum(dqkv[:, 256:])]))
     triple_sum = jnp.concatenate(triples, axis=-1)
-    together(sums_of, triple_sum, *dqkv_rows[:n_ctx])
     half_sum = triple_sum.reshape((quads, 2) + triple_sum.shape[dev_bits - ctx_bits :])
     half_sum = Process(scatter_core(half_sum, core_bit))
-    for one in sums_of:
-        one.advance()
-    together(sums_of + [half_sum], *dqkv_rows[n_ctx:])
+    together(sums_of + [half_sum], *dqkv_parts)
     half_sum.advance()
     triple_sum = Process(scatter_at_once(half_sum.result, up_bits))
     for one in sums_of:
         one.advance()
+    dqkv_parts = [after(part, *given[-2:]) for part in dqkv_parts]
     together([one for one in sums_of if one.result is None] + [triple_sum])
     triple_sum.advance()
     triple_sum = Process(exchange_line(triple_sum.result))
@@ -883,18 +898,17 @@
     triple_sum = triple_sum.finish()
     grad_triple = triple_sum.reshape(n_ctx, part, chunks, 3, 128).transpose(3, 1, 0, 2, 4)
     grad_triple = grad_triple.reshape(3, part, width).astype(f32)
-    grad_left, grad_right, grad_outer = [one.finish() for one in sums_of]
-    grad_attn = grad_left[:, :width]
-    grad_inner = jnp.concatenate([grad_left[:, width:], grad_right], axis=1)
+    grad_first, grad_outer = [one.finish() for one in sums_of]
+    grad_attn, grad_inner = grad_first[:, :width], grad_first[:, width:]
     late = jnp.concatenate(late, axis=1)
     late = lax.dynamic_update_slice_in_dim(
         jnp.zeros((2, width), f32), late, place * group, 1
     )
     late = late.reshape(2, n_dev, part).transpose(1, 0, 2).reshape(n_dev, 2 * part)
-    early = jnp.concatenate(early + [late], axis=1)
+    early = after(jnp.concatenate(early + [late], axis=1), *dqkv_parts)
     early = lax.all_to_all(early, AXES, 0, 0, tiled=True).sum(axis=0)
     late = early[early.shape[0] - 2 * part :].reshape(2, part)
-    input_grad = input_gradient(where, dfirst, w_triple, dqkv_rows, n_ctx)
+    input_grad = input_gradient(where, dfirst, w_triple, dqkv_slots, dqkv_parts, n_ctx)
 
     pieces = [early[i * part : (i + 1) * part] for i in range(6)]
     return (

time: 528 us -> 496 us (0.939)
  local copies, waits for them, and re-layouts: 44.2 us -> 29.1 us
  waiting for transfers between devices: 160 us -> 149 us
  starting transfers between devices: 81.9 us -> 73.6 us
    ppermute x15 -> x12, waiting for transfers between devices: 34.1 us -> 6.7 us  [exchange_slots(): lax.ppermute(slots[mask], 'ctx', [(i, i ^ mask) for i in range(count)])]
    all_to_all x0 -> x1, waiting for transfers between devices: none -> 14 us  [local(): dqkv_parts.append(lax.all_to_all(dqkv_placed, 'ctx', 0, 0, tiled=True))]
    slice x13 -> x5, local copies, waits for them, and re-layouts: 20.2 us -> 7.18 us  [the longest x2 3.16 us: scatter_sum(): given, parts = ([part[1] for part in parts], [part[0] for part in parts])]
    ppermute x19 -> x14, waiting for transfers between devices: 39 us -> 30.7 us  [swap(): return lax.ppermute(values, AXES, [(i, i ^ 1 << bit) for i in range(count)])]
    ppermute x15 -> x12, starting transfers between devices: 25.6 us -> 18.6 us  [exchange_slots(): lax.ppermute(slots[mask], 'ctx', [(i, i ^ mask) for i in range(count)])]
    ppermute x6, waiting for transfers between devices: 45.1 us -> 51.5 us  [exchange_line(): lax.ppermute(lax.dynamic_index_in_dim(blocks, place ^ mask, 0, keepdims=F...]
    convert_element_type x13 -> x9, other arithmetic: 26 us -> 28.9 us  [total_of(): return total.astype(dtype)]
    ppermute x19 -> x14, starting transfers between devices: 20.3 us -> 17.7 us  [swap(): return lax.ppermute(values, AXES, [(i, i ^ 1 << bit) for i in range(count)])]
  transfers between devices with their start and end apart: 53 -> 46, of which waited for: 17 -> 17; matrix products, arithmetic and copies ran while one was open for 18% -> 16% of each run, Pallas kernels for 30% -> 32%
where the time goes in v3:
time: 496 us; the launch traced here: 489 us
  Pallas kernels  159 us (32%)
  waiting for transfers between devices  149 us (30%)
  starting transfers between devices  73.6 us (15%)
  other arithmetic  50.9 us (10%)
  local copies, waits for them, and re-layouts  29.1 us (6%)
  between operations  15.9 us (3%)
  matrix products  12 us (2%)
    pallas_call x2, Pallas kernels, attention_backward(): pl.pallas_call(functools.partial(attention_backward_kernel, heads=heads,...  56.6 us
    pallas_call x1, Pallas kernels, layer_middle(): pl.pallas_call(functools.partial(layer_kernel, chunks=chunks, groups=grou...  54.9 us
    ppermute x6, waiting for transfers between devices, exchange_line(): lax.ppermute(lax.dynamic_index_in_dim(blocks, place ^ mask, 0, keepdims=F...  51.5 us
    pallas_call x2, Pallas kernels, attention_forward(): pl.pallas_call(functools.partial(attention_forward_kernel, heads=heads, r...  39.4 us
    ppermute x3, waiting for transfers between devices, gather_line(): lax.ppermute(from_left, 'ctx', [(i, i + 1) for i in range(count - 1)])  32 us
    ppermute x14, waiting for transfers between devices, swap(): return lax.ppermute(values, AXES, [(i, i ^ 1 << bit) for i in range(count)])  30.7 us
    convert_element_type x9, other arithmetic, total_of(): return total.astype(dtype)  28.9 us
    ppermute x12, starting transfers between devices, exchange_slots(): lax.ppermute(slots[mask], 'ctx', [(i, i ^ mask) for i in range(count)])  18.6 us
  transfers between devices with their start and end apart: 46, of which 17 were waited for; matrix products, arithmetic and copies ran while one was open for 16% of the time, Pallas kernels for 32%

profile of v3, /device:TPU:0, one launch (start us, length us, event | category | flops | bytes accessed | tf_op | source)
XLA Modules:
  0.0 489.2 jit_solution(4442590475172377255)
XLA Ops:
  12.2 5.9 %collective-permute-start = (bf16[512,1024]{1,0:T(8,128)(2,1)S(1)}, bf16[512,1024]{1,0:T(8,128)(2,1)}, u32[]{:S(2)}, u32[]{:S(2)}) collective-permute-start(bf16[512,1024]{1,0:T(8,128)(2,1)S(1)} %copy-done.2), channel_id=1, source_target_pairs={{0,1},{1,2},{2,3},{4,5},{5,6},{6,7},{8,9},{9,10},{10,11},{12,13},{... | collective-permute-start | bytes 3145736 | tf_op jit(solution)/shard_map/ppermute | solution.py:596
  26.2 37.9 %collective-permute-done.2 = bf16[48,768]{1,0:T(8,128)(2,1)S(1)} collective-permute-done((bf16[48,768]{1,0:T(8,128)(2,1)S(1)}, bf16[48,768]{1,0:T(8,128)(2,1)S(1)}, u32[]{:S(2)}, u32[]{:S(2)}) %collective-permute-start.2) | collective-permute-done | bytes 73760 | tf_op jit(solution)/shard_map/ppermute | solution.py:622
  67.0 4.2 collective-permute-start.5
  74.2 11.5 %collective-permute-done.7 = bf16[4,48,768]{2,1,0:T(8,128)(2,1)S(1)} collective-permute-done((bf16[4,48,768]{2,1,0:T(8,128)(2,1)S(1)}, bf16[4,48,768]{2,1,0:T(8,128)(2,1)S(1)}, u32[]{:S(2)}, u32[]{:S(2)}) %collective-permute-start.7) | collective-permute-done | bytes 294944 | tf_op jit(solution)/shard_map/ppermute | solution.py:570
  85.7 24.1 %collective-permute-done.5 = bf16[512,1024]{1,0:T(8,128)(2,1)} collective-permute-done((bf16[512,1024]{1,0:T(8,128)(2,1)}, bf16[512,1024]{1,0:T(8,128)(2,1)}, u32[]{:S(2)}, u32[]{:S(2)}) %collective-permute-start.5) | collective-permute-done | bytes 1048608 | tf_op jit(solution)/shard_map/ppermute | solution.py:596
  109.7 5.1 %collective-permute-done.6 = bf16[512,1024]{1,0:T(8,128)(2,1)} collective-permute-done((bf16[512,1024]{1,0:T(8,128)(2,1)S(1)}, bf16[512,1024]{1,0:T(8,128)(2,1)}, u32[]{:S(2)}, u32[]{:S(2)}) %collective-permute-start.6) | collective-permute-done | bytes 1048608 | tf_op jit(solution)/shard_map/ppermute | solution.py:597
  123.6 10.1 %collective-permute-done.10 = bf16[2,4,48,768]{3,2,1,0:T(8,128)(2,1)S(1)} collective-permute-done((bf16[2,4,48,768]{3,2,1,0:T(8,128)(2,1)S(1)}, bf16[2,4,48,768]{3,2,1,0:T(8,128)(2,1)S(1)}, u32[]{:S(2)}, u32[]{:S(2)}) %collective-permute-start.10) | collective-permute-done | bytes 589856 | tf_op jit(solution)/shard_map/ppermute | solution.py:570
  133.7 7.9 %collective-permute-done.8 = bf16[512,1024]{1,0:T(8,128)(2,1)} collective-permute-done((bf16[512,1024]{1,0:T(8,128)(2,1)}, bf16[512,1024]{1,0:T(8,128)(2,1)}, u32[]{:S(2)}, u32[]{:S(2)}) %collective-permute-start.8) | collective-permute-done | bytes 1048608 | tf_op jit(solution)/shard_map/ppermute | solution.py:596
  141.7 5.1 %collective-permute-done.9 = bf16[512,1024]{1,0:T(8,128)(2,1)} collective-permute-done((bf16[512,1024]{1,0:T(8,128)(2,1)}, bf16[512,1024]{1,0:T(8,128)(2,1)}, u32[]{:S(2)}, u32[]{:S(2)}) %collective-permute-start.9) | collective-permute-done | bytes 1048608 | tf_op jit(solution)/shard_map/ppermute | solution.py:597
  154.7 7.3 %add_convert_fusion.q_ref.k_ref.v_ref = bf16[2048,768]{1,0:T(8,128)(2,1)} fusion(bf16[2048,1024]{1,0:T(8,128)(2,1)} %bitcast.161, bf16[1024,768]{1,0:T(8,128)(2,1)S(1)} %bitcast.175, f32[768]{0:T(1024)S(1)} %add.231), kind=kOutput, calls=%fused_computation | convolution fusion | flops 3224371200 | bytes 8915968 | tf_op jit(solution)/shard_map/dot_general | solution.py:812
  163.3 19.9 %attention_forward.3 = (bf16[2048,128]{1,0:T(8,128)(2,1)}, f32[8,2048]{1,0:T(8,128)}) custom-call(s32[4]{0:T(128)} %pad_add_fusion.place_ref, bf16[2048,768]{1,0:T(8,128)(2,1)} %add_convert_fusion.q_ref.k_ref.v_ref, bf16[2048,768]{1,0:T(8,128)(2,1)} %add_convert_fusion.q_ref.k_ref.v_ref, bf16[2048,768]{1,0:T(8,128)(2,1)} %add_convert_fusion.q_ref.k_ref.v_ref), custom_call_target="tpu_custom_call" | custom-call | flops 1073741824 | bytes 2097152 | tf_op jit(solution)/shard_map/attention_forward/pallas_call | solution.py:64
  185.0 4.4 collective-permute-start.17
  189.4 19.4 %attention_forward.2 = (bf16[2048,128]{1,0:T(8,128)(2,1)}, f32[8,2048]{1,0:T(8,128)}) custom-call(s32[4]{0:T(128)} %pad_add_fusion.place_ref, bf16[2048,768]{1,0:T(8,128)(2,1)} %add_convert_fusion.q_ref.k_ref.v_ref, bf16[2048,768]{1,0:T(8,128)(2,1)} %add_convert_fusion.q_ref.k_ref.v_ref, bf16[2048,768]{1,0:T(8,128)(2,1)} %add_convert_fusion.q_ref.k_ref.v_ref), custom_call_target="tpu_custom_call" | custom-call | flops 1073741824 | bytes 2097152 | tf_op jit(solution)/shard_map/attention_forward/pallas_call | solution.py:64
  219.0 4.4 collective-permute-done.13.refs_2_
  224.2 54.9 %layer_middle.1 = (bf16[512,1024]{1,0:T(8,128)(2,1)}, f32[512,1024]{1,0:T(8,128)}, f32[8,1024]{1,0:T(8,128)}, f32[1,4096]{1,0:T(1,128)}, bf16[512,256]{1,0:T(8,1...) custom-call(s32[4]{0:T(128)} %pad_add_fusion.place_ref, ...), custom_call_target="tpu_custom_call" | custom-call | flops 4026531840 | bytes 42991616 | tf_op jit(solution)/shard_map/layer_middle/pallas_call | solution.py:474
  288.1 6.1 %add_convert_fusion.1 = (bf16[2,128,5120]{2,1,0:T(8,128)(2,1)}, bf16[2,128,5120]{2,1,0:T(8,128)(2,1)S(1)}) fusion(bf16[4,128,5120]{2,1,0:T(8,128)(2,1)} %collective-permute-done.18, bf16[4,128,5120]{2,1,0:T(8,128)(2,1)} %get-tuple-element.82), kind=kLoop, calls=%fused_computation.1 | loop fusion | flops 10485760 | bytes 15728640 | tf_op jit(solution)/shard_map/convert_element_type | solution.py:670
  297.3 4.4 add_convert_fusion.3
  307.2 28.4 %attention_backward.2 = (bf16[2048,384]{1,0:T(8,128)(2,1)}, bf16[4,512,384]{2,1,0:T(8,128)(2,1)}) custom-call(s32[4]{0:T(128)} %pad_add_fusion.place_ref, bf16[2048,768]{1,0:T(8,128)(2,1)} %add_convert_fusion.q_ref.k_ref.v_ref, bf16[2048,768]{1,0:T(8,128)(2,1)} %add_convert_fusion.q_ref.k_ref.v_ref, bf16[2048,768]{1,0:T(8,128)(2,1)} %add_convert_fusion.q_ref.k_ref.v_ref, ...), custom_call_target="tpu_custom_call" | custom-call | flops 2684354560 | bytes 4194304 | tf_op jit(solution)/shard_map/attention_backward/pallas_call | solution.py:179
  345.0 28.1 %attention_backward.3 = (bf16[2048,384]{1,0:T(8,128)(2,1)}, bf16[4,512,384]{2,1,0:T(8,128)(2,1)}) custom-call(s32[4]{0:T(128)} %pad_add_fusion.place_ref, bf16[2048,768]{1,0:T(8,128)(2,1)} %add_convert_fusion.q_ref.k_ref.v_ref, bf16[2048,768]{1,0:T(8,128)(2,1)} %add_convert_fusion.q_ref.k_ref.v_ref, bf16[2048,768]{1,0:T(8,128)(2,1)} %add_convert_fusion.q_ref.k_ref.v_ref, ...), custom_call_target="tpu_custom_call" | custom-call | flops 2684354560 | bytes 4194304 | tf_op jit(solution)/shard_map/attention_backward/pallas_call | solution.py:179
  376.8 4.7 fusion.1
  399.1 14.0 %all-to-all-done.refs_4_ = bf16[4,512,384]{2,1,0:T(8,128)(2,1)S(1)} async-done(((bf16[4,512,384]{2,1,0:T(8,128)(2,1)}), bf16[4,512,384]{2,1,0:T(8,128)(2,1)S(1)}, u32[]{:S(2)}, u32[]{:S(2)}) %all-to-all-start) | async-done | bytes 1572896 | tf_op jit(solution)/shard_map/all_to_all | solution.py:871
  413.1 4.8 collective-permute-done.28
  438.6 7.7 %input_gradient.1 = bf16[512,1024]{1,0:T(8,128)(2,1)} custom-call(s32[4]{0:T(128)S(1)} %copy-done.1, f32[512,1024]{1,0:T(8,128)S(1)} %copy-done, bf16[1024,3072]{1,0:T(8,128)(2,1)} %all-gather.8.cloned.1.call-done.weights_ref, bf16[512,384]{1,0:T(8,128)(2,1)S(1)} %get-tuple-element.140.refs_0_, bf16[512,384]{1,0:T(8,128)(2,1)S(1)} %collective-permute-done.23.refs_1_, ...), custom_call_target="tpu_custom_call" | custom-call | flops 402653184 | bytes 12582912 | tf_op jit(solution)/shard_map/input_gradient/pallas_call | solution.py:544
  464.8 9.6 %collective-permute-done.38 = bf16[32,768]{1,0:T(8,128)(2,1)S(1)} collective-permute-done((bf16[32,768]{1,0:T(8,128)(2,1)S(1)}, bf16[32,768]{1,0:T(8,128)(2,1)S(1)}, u32[]{:S(2)}, u32[]{:S(2)}) %collective-permute-start.38) | collective-permute-done | bytes 49184 | tf_op jit(solution)/shard_map/ppermute | solution.py:622
  (287 shorter events, 143.3 us)
Async XLA Ops:
  7.2 216.3 %all-gather.6.cloned.1.call-start = ((), (), s32[]{:S(2)}) async-start(), calls=%async_computation.3 | async-start | bytes 8650752 | tf_op jit(solution)/shard_map/all_gather | solution.py:795
  9.2 214.3 %all-gather.4.cloned.1.call-start = ((), (), s32[]{:S(2)}) async-start(), calls=%async_computation.2 | async-start | bytes 10813440 | tf_op jit(solution)/shard_map/all_gather | solution.py:794
  12.1 294.2 %all-gather.8.cloned.1.call-start = ((), (), s32[]{:S(2)}) async-start(), calls=%async_computation.4 | async-start | bytes 6488064 | tf_op jit(solution)/shard_map/all_gather | solution.py:828
  12.2 54.8 %collective-permute-start = (bf16[512,1024]{1,0:T(8,128)(2,1)S(1)}, bf16[512,1024]{1,0:T(8,128)(2,1)}, u32[]{:S(2)}, u32[]{:S(2)}) collective-permute-start(bf16[512,1024]{1,0:T(8,128)(2,1)S(1)} %copy-done.2), channel_id=1, source_target_pairs={{0,1},{1,2},{2,3},{4,5},{5,6},{6,7},{8,9},{9,10},{10,11},{12,13},{... | collective-permute-start | bytes 3145736 | tf_op jit(solution)/shard_map/ppermute | solution.py:596
  18.1 48.9 %collective-permute-start.1 = (bf16[512,1024]{1,0:T(8,128)(2,1)S(1)}, bf16[512,1024]{1,0:T(8,128)(2,1)S(1)}, u32[]{:S(2)}, u32[]{:S(2)}) collective-permute-start(bf16[512,1024]{1,0:T(8,128)(2,1)S(1)} %copy-done.2), channel_id=1, source_target_pairs={{1,0},{2,1},{3,2},{5,4},{6,5},{7,6},{9,8},{10,9},{11,10},{13,12},{... | collective-permute-start | bytes 3145736 | tf_op jit(solution)/shard_map/ppermute | solution.py:597
  21.0 43.1 %collective-permute-start.2 = (bf16[48,768]{1,0:T(8,128)(2,1)S(1)}, bf16[48,768]{1,0:T(8,128)(2,1)S(1)}, u32[]{:S(2)}, u32[]{:S(2)}) collective-permute-start(bf16[48,768]{1,0:T(8,128)(2,1)S(1)} %get-tuple-element.158), channel_id=1, source_target_pairs={{0,1},{1,0},{2,3},{3,2},{4,5},{5,4},{6,7},{7,6},{8,9},{9,8},{10,11... | collective-permute-start | bytes 221192 | tf_op jit(solution)/shard_map/ppermute | solution.py:622
  23.8 43.2 %collective-permute-start.3 = (bf16[48,768]{1,0:T(8,128)(2,1)S(1)}, bf16[48,768]{1,0:T(8,128)(2,1)S(1)}, u32[]{:S(2)}, u32[]{:S(2)}) collective-permute-start(bf16[48,768]{1,0:T(8,128)(2,1)S(1)} %get-tuple-element.159), channel_id=1, source_target_pairs={{0,2},{1,3},{2,0},{3,1},{4,6},{5,7},{6,4},{7,5},{8,10},{9,11},{10,... | collective-permute-start | bytes 221192 | tf_op jit(solution)/shard_map/ppermute | solution.py:622
  25.4 41.6 %collective-permute-start.4 = (bf16[48,768]{1,0:T(8,128)(2,1)S(1)}, bf16[48,768]{1,0:T(8,128)(2,1)S(1)}, u32[]{:S(2)}, u32[]{:S(2)}) collective-permute-start(bf16[48,768]{1,0:T(8,128)(2,1)S(1)} %get-tuple-element.157), channel_id=1, source_target_pairs={{0,3},{1,2},{2,1},{3,0},{4,7},{5,6},{6,5},{7,4},{8,11},{9,10},{10,... | collective-permute-start | bytes 221192 | tf_op jit(solution)/shard_map/ppermute | solution.py:622
  67.0 42.8 %collective-permute-start.5 = (bf16[512,1024]{1,0:T(8,128)(2,1)}, bf16[512,1024]{1,0:T(8,128)(2,1)}, u32[]{:S(2)}, u32[]{:S(2)}) collective-permute-start(bf16[512,1024]{1,0:T(8,128)(2,1)} %collective-permute-done), channel_id=1, source_target_pairs={{0,1},{1,2},{2,3},{4,5},{5,6},{6,7},{8,9},{9,10},{10,11},{12,13},{... | collective-permute-start | bytes 3145736 | tf_op jit(solution)/shard_map/ppermute | solution.py:596
  71.2 43.6 %collective-permute-start.6 = (bf16[512,1024]{1,0:T(8,128)(2,1)S(1)}, bf16[512,1024]{1,0:T(8,128)(2,1)}, u32[]{:S(2)}, u32[]{:S(2)}) collective-permute-start(bf16[512,1024]{1,0:T(8,128)(2,1)S(1)} %collective-permute-done.1), channel_id=1, source_target_pairs={{1,0},{2,1},{3,2},{5,4},{6,5},{7,6},{9,8},{10,9},{11,10},{13,12},{... | collective-permute-start | bytes 3145736 | tf_op jit(solution)/shard_map/ppermute | solution.py:597
  117.1 29.6 %collective-permute-start.9 = (bf16[512,1024]{1,0:T(8,128)(2,1)}, bf16[512,1024]{1,0:T(8,128)(2,1)}, u32[]{:S(2)}, u32[]{:S(2)}) collective-permute-start(bf16[512,1024]{1,0:T(8,128)(2,1)} %collective-permute-done.6), channel_id=1, source_target_pairs={{1,0},{2,1},{3,2},{5,4},{6,5},{7,6},{9,8},{10,9},{11,10},{13,12},{... | collective-permute-start | bytes 3145736 | tf_op jit(solution)/shard_map/ppermute | solution.py:597
  185.0 27.3 %collective-permute-start.15 = (bf16[512,128]{1,0:T(8,128)(2,1)S(1)}, bf16[512,128]{1,0:T(8,128)(2,1)S(1)}, u32[]{:S(2)}, u32[]{:S(2)}) collective-permute-start(bf16[512,128]{1,0:T(8,128)(2,1)S(1)} %get-tuple-element.151), channel_id=1, source_target_pairs={{0,1},{1,0},{2,3},{3,2},{4,5},{5,4},{6,7},{7,6},{8,9},{9,8},{10,11... | collective-permute-start | bytes 393224 | tf_op jit(solution)/shard_map/ppermute | solution.py:613
  185.0 31.7 %collective-permute-start.16 = (bf16[512,128]{1,0:T(8,128)(2,1)S(1)}, bf16[512,128]{1,0:T(8,128)(2,1)S(1)}, u32[]{:S(2)}, u32[]{:S(2)}) collective-permute-start(bf16[512,128]{1,0:T(8,128)(2,1)S(1)} %get-tuple-element.150), channel_id=1, source_target_pairs={{0,2},{1,3},{2,0},{3,1},{4,6},{5,7},{6,4},{7,5},{8,10},{9,11},{10,... | collective-permute-start | bytes 393224 | tf_op jit(solution)/shard_map/ppermute | solution.py:613
  185.0 31.7 %collective-permute-start.17 = (bf16[512,128]{1,0:T(8,128)(2,1)S(1)}, bf16[512,128]{1,0:T(8,128)(2,1)S(1)}, u32[]{:S(2)}, u32[]{:S(2)}) collective-permute-start(bf16[512,128]{1,0:T(8,128)(2,1)S(1)} %get-tuple-element.149), channel_id=1, source_target_pairs={{0,3},{1,2},{2,1},{3,0},{4,7},{5,6},{6,5},{7,4},{8,11},{9,10},{10,... | collective-permute-start | bytes 393224 | tf_op jit(solution)/shard_map/ppermute | solution.py:613
  295.9 80.8 %collective-permute-start.26 = (bf16[2,2,2,32,5120]{4,3,1,2,0:T(8,128)(2,1)}, bf16[2,2,2,32,5120]{4,3,1,2,0:T(8,128)(2,1)}, u32[]{:S(2)}, u32[]{:S(2)}) collective-permute-start(bf16[2,2,2,32,5120]{4,3,1,2,0:T(8,128)(2,1)} %copy.92), channel_id=1, source_target_pairs={{0,8},{1,9},{2,10},{3,11},{4,12},{5,13},{6,14},{7,15},{8,0},{9,1},... | collective-permute-start | bytes 7864328 | tf_op jit(solution)/shard_map/ppermute | solution.py:570
  301.8 75.0 %collective-permute-start.27 = (bf16[2,2,2,128,1024]{4,3,2,1,0:T(8,128)(2,1)}, bf16[2,2,2,128,1024]{4,3,2,1,0:T(8,128)(2,1)}, u32[]{:S(2)}, u32[]{:S(2)}) collective-permute-start(bf16[2,2,2,128,1024]{4,3,2,1,0:T(8,128)(2,1)} %bitcast.32), channel_id=1, source_target_pairs={{0,16},{1,17},{2,18},{3,19},{4,20},{5,21},{6,22},{7,23},{8,24},{9,... | collective-permute-start | bytes 6291464 | tf_op jit(solution)/shard_map/ppermute | solution.py:570
  338.2 38.5 %collective-permute-start.23 = (bf16[512,384]{1,0:T(8,128)(2,1)}, bf16[512,384]{1,0:T(8,128)(2,1)S(1)}, u32[]{:S(2)}, u32[]{:S(2)}) collective-permute-start(bf16[512,384]{1,0:T(8,128)(2,1)} %get-tuple-element.139), channel_id=1, source_target_pairs={{0,1},{1,0},{2,3},{3,2},{4,5},{5,4},{6,7},{7,6},{8,9},{9,8},{10,11... | collective-permute-start | bytes 1179656 | tf_op jit(solution)/shard_map/ppermute | solution.py:613
  340.9 35.8 %collective-permute-start.24 = (bf16[512,384]{1,0:T(8,128)(2,1)}, bf16[512,384]{1,0:T(8,128)(2,1)S(1)}, u32[]{:S(2)}, u32[]{:S(2)}) collective-permute-start(bf16[512,384]{1,0:T(8,128)(2,1)} %get-tuple-element.138), channel_id=1, source_target_pairs={{0,2},{1,3},{2,0},{3,1},{4,6},{5,7},{6,4},{7,5},{8,10},{9,11},{10,... | collective-permute-start | bytes 1179656 | tf_op jit(solution)/shard_map/ppermute | solution.py:613
  340.9 35.8 %collective-permute-start.25 = (bf16[512,384]{1,0:T(8,128)(2,1)S(1)}, bf16[512,384]{1,0:T(8,128)(2,1)S(1)}, u32[]{:S(2)}, u32[]{:S(2)}) collective-permute-start(bf16[512,384]{1,0:T(8,128)(2,1)S(1)} %get-tuple-element.137), channel_id=1, source_target_pairs={{0,3},{1,2},{2,1},{3,0},{4,7},{5,6},{6,5},{7,4},{8,11},{9,10},{10,... | collective-permute-start | bytes 1179656 | tf_op jit(solution)/shard_map/ppermute | solution.py:613
  373.1 40.0 %all-to-all-start = ((bf16[4,512,384]{2,1,0:T(8,128)(2,1)}), bf16[4,512,384]{2,1,0:T(8,128)(2,1)S(1)}, u32[]{:S(2)}, u32[]{:S(2)}) async-start(bf16[4,512,384]{2,1,0:T(8,128)(2,1)} %get-tuple-element.93), calls=%async_computation | async-start | bytes 3145728 | tf_op jit(solution)/shard_map/all_to_all | solution.py:871
  385.6 27.5 %collective-permute-start.29 = (bf16[2,2,128,1024]{3,2,1,0:T(8,128)(2,1)}, bf16[2,2,128,1024]{3,2,1,0:T(8,128)(2,1)}, u32[]{:S(2)}, u32[]{:S(2)}) collective-permute-start(bf16[2,2,128,1024]{3,2,1,0:T(8,128)(2,1)} %get-tuple-element.134), channel_id=1, source_target_pairs={{0,8},{1,9},{2,10},{3,11},{4,12},{5,13},{6,14},{7,15},{8,0},{9,1},... | collective-permute-start | bytes 3145736 | tf_op jit(solution)/shard_map/ppermute | solution.py:570
  388.3 29.6 %collective-permute-start.28 = (bf16[2,2,32,5120]{3,2,1,0:T(8,128)(2,1)}, bf16[2,2,32,5120]{3,2,1,0:T(8,128)(2,1)}, u32[]{:S(2)}, u32[]{:S(2)}) collective-permute-start(bf16[2,2,32,5120]{3,2,1,0:T(8,128)(2,1)} %copy.95), channel_id=1, source_target_pairs={{0,16},{1,17},{2,18},{3,19},{4,20},{5,21},{6,22},{7,23},{8,24},{9,... | collective-permute-start | bytes 3932168 | tf_op jit(solution)/shard_map/ppermute | solution.py:570
  420.9 31.6 %collective-permute-start.31 = (bf16[2,32,5120]{2,1,0:T(8,128)(2,1)}, bf16[2,32,5120]{2,1,0:T(8,128)(2,1)}, u32[]{:S(2)}, u32[]{:S(2)}) collective-permute-start(bf16[2,32,5120]{2,1,0:T(8,128)(2,1)} %get-tuple-element.126), channel_id=1, source_target_pairs={{0,1},{1,0},{2,3},{3,2},{4,5},{5,4},{6,7},{7,6},{8,9},{9,8},{10,11... | collective-permute-start | bytes 1966088 | tf_op jit(solution)/shard_map/ppermute | solution.py:570
  425.2 27.3 %collective-permute-start.32 = (bf16[2,128,1024]{2,1,0:T(8,128)(2,1)}, bf16[2,128,1024]{2,1,0:T(8,128)(2,1)}, u32[]{:S(2)}, u32[]{:S(2)}) collective-permute-start(bf16[2,128,1024]{2,1,0:T(8,128)(2,1)} %get-tuple-element.132), channel_id=1, source_target_pairs={{0,2},{1,3},{2,0},{3,1},{4,6},{5,7},{6,4},{7,5},{8,10},{9,11},{10,... | collective-permute-start | bytes 1572872 | tf_op jit(solution)/shard_map/ppermute | solution.py:570
  (62 other events, 614.8 us)
Sparse Core Ops, SparseCore 0:
  11.6 98.3 all-gather.5
  113.4 103.0 all-gather.3
  219.4 72.1 all-gather.7

commit v4 on v3

--- a/solution.py
+++ b/solution.py
@@ -159,7 +159,7 @@
         return tuple(new_dq_t)
 
     start = tuple(jnp.zeros((HD, rows), f32) for _ in range(heads))
-    dq_t = jnp.concatenate(lax.fori_loop(0, seq // rows, chunk, start), axis=0)
+    dq_t = jnp.concatenate(lax.fori_loop(0, seq // rows, chunk, start, unroll=4), axis=0)
     own_rows = pl.ds(pl.multiple_of(step * rows, rows), rows)
     out_ref[own_rows, :width] = (dq_t * score_scale).T.astype(bf16)
 
@@ -276,7 +276,7 @@
         hidden_ref[span, :] = hidden.astype(bf16)
         return carried
 
-    lax.fori_loop(0, rows // step, norm_one, 0)
+    lax.fori_loop(0, rows // step, norm_one, 0, unroll=2)
 
     copies[1].wait()
     block = 512
@@ -293,7 +293,7 @@
         dpre_ref[:, span] = slope.astype(bf16)
         return carried
 
-    lax.fori_loop(0, hidden_width // block, feed_in, 0)
+    lax.fori_loop(0, hidden_width // block, feed_in, 0, unroll=4)
 
     copies[2].wait()
     narrow = 512
@@ -303,7 +303,7 @@
         wide_ref[:, span] = jnp.dot(act_ref[...], w_outer[:, span], preferred_element_type=f32)
         return carried
 
-    lax.fori_loop(0, width // narrow, feed_out, 0)
+    lax.fori_loop(0, width // narrow, feed_out, 0, unroll=2)
 
     def norm_two(turn, carried):
         span = pl.ds(pl.multiple_of(turn * step, step), step)
@@ -330,7 +330,7 @@
 
     none = jnp.zeros((1, width), f32)
     shift_sum, gain_sum, offset_sum = lax.fori_loop(
-        0, rows // step, norm_two, (none, none, none)
+        0, rows // step, norm_two, (none, none, none), unroll=2
     )
     sums_ref[0:1] = offset_sum
     sums_ref[1:2] = gain_sum
@@ -348,7 +348,7 @@
         inner_sum_ref[:, span] = jnp.sum(dpre.astype(f32), axis=0, keepdims=True)
         return carried
 
-    lax.fori_loop(0, hidden_width // block, back_out, 0)
+    lax.fori_loop(0, hidden_width // block, back_out, 0, unroll=4)
 
     quads = gradient_refs[0].shape[0]
     slab, outer_slab = width // (2 * quads), hidden_width // (2 * quads)
@@ -385,7 +385,7 @@
         w_outer[span, :] = terms.astype(bf16)
         return carried
 
-    lax.fori_loop(0, hidden_width // block, outer_gradient, 0)
+    lax.fori_loop(0, hidden_width // block, outer_gradient, 0, unroll=2)
     leaving = leave(3, w_outer, 1, 0, outer_slab)
 
     def back_in(turn, carried):
@@ -395,7 +395,7 @@
         )
         return carried
 
-    lax.fori_loop(0, width // narrow, back_in, 0)
+    lax.fori_loop(0, width // narrow, back_in, 0, unroll=2)
 
     def norm_one_back(turn, carried):
         span = pl.ds(pl.multiple_of(turn * step, step), step)
@@ -418,7 +418,7 @@
         return (shift_sum, gain_sum, offset_sum)
 
     shift_sum, gain_sum, offset_sum = lax.fori_loop(
-        0, rows // step, norm_one_back, (none, none, none)
+        0, rows // step, norm_one_back, (none, none, none), unroll=2
     )
     sums_ref[3:4] = offset_sum
     sums_ref[4:5] = gain_sum
@@ -440,7 +440,7 @@
             w_inner[rows_of, span] = terms.astype(bf16)
         return carried
 
-    lax.fori_loop(0, hidden_width // wide_block, inner_gradient, 0)
+    lax.fori_loop(0, hidden_width // wide_block, inner_gradient, 0, unroll=2)
     leaving += leave(3 + len(leaving), w_inner, 0, width, slab)
     turned_ref[...] = mixed_ref[...].T
     for half in range(width // block):
@@ -654,9 +654,11 @@
             axis, mine = left.index(bit), own_bit(bit)
             given = [lax.dynamic_index_in_dim(part, 1 - mine, axis, False) for part in parts]
             parts = [lax.dynamic_index_in_dim(part, mine, axis, False) for part in parts]
-        given = total_of(given, parts[0].dtype)
+        if bit == bit_order[0]:
+            given, kept = total_of(given, parts[0].dtype), total_of(parts, parts[0].dtype)
+        else:
+            given, kept = given[0] + given[1], parts[0] + parts[1]
         sent.append(given)
-        kept = total_of(parts, parts[0].dtype)
         parts = [kept] + (yield [swap(given, bit)])
         if bit in left:
             left.remove(bit)

time: 496 us -> 489 us (0.986)
  Pallas kernels: 159 us -> 150 us
    convert_element_type x9 -> x3, other arithmetic: 28.9 us -> 12.3 us  [total_of(): return total.astype(dtype)]
    add x0 -> x6, other arithmetic: none -> 15.2 us  [scatter_sum(): given, kept = (given[0] + given[1], parts[0] + parts[1])]
    pallas_call x2, Pallas kernels: 56.6 us -> 51.4 us  [attention_backward(): pl.pallas_call(functools.partial(attention_backward_kernel, heads=heads,...]
  transfers between devices with their start and end apart: 46 -> 46, of which waited for: 17 -> 19; matrix products, arithmetic and copies ran while one was open for 16% -> 16% of each run, Pallas kernels for 32% -> 31%
where the time goes in v4:
time: 489 us; the launch traced here: 482 us
  waiting for transfers between devices  152 us (31%)
  Pallas kernels  150 us (31%)
  starting transfers between devices  74.9 us (15%)
  other arithmetic  49.6 us (10%)
  local copies, waits for them, and re-layouts  28.1 us (6%)
  between operations  16.1 us (3%)
  matrix products  12 us (2%)
    ppermute x6, waiting for transfers between devices, exchange_line(): lax.ppermute(lax.dynamic_index_in_dim(blocks, place ^ mask, 0, keepdims=F...  51.5 us
    pallas_call x2, Pallas kernels, attention_backward(): pl.pallas_call(functools.partial(attention_backward_kernel, heads=heads,...  51.4 us
    pallas_call x1, Pallas kernels, layer_middle(): pl.pallas_call(functools.partial(layer_kernel, chunks=chunks, groups=grou...  51.4 us
    pallas_call x2, Pallas kernels, attention_forward(): pl.pallas_call(functools.partial(attention_forward_kernel, heads=heads, r...  39.1 us
    ppermute x3, waiting for transfers between devices, gather_line(): lax.ppermute(from_left, 'ctx', [(i, i + 1) for i in range(count - 1)])  32.1 us
    ppermute x14, waiting for transfers between devices, swap(): return lax.ppermute(values, AXES, [(i, i ^ 1 << bit) for i in range(count)])  28 us
    ppermute x12, starting transfers between devices, exchange_slots(): lax.ppermute(slots[mask], 'ctx', [(i, i ^ mask) for i in range(count)])  21.8 us
    all_to_all x1, waiting for transfers between devices, local(): dqkv_parts.append(lax.all_to_all(dqkv_placed, 'ctx', 0, 0, tiled=True))  17.6 us
  transfers between devices with their start and end apart: 46, of which 19 were waited for; matrix products, arithmetic and copies ran while one was open for 16% of the time, Pallas kernels for 31%

profile of v4, /device:TPU:0, one launch (start us, length us, event | category | flops | bytes accessed | tf_op | source)
XLA Modules:
  0.0 482.2 jit_solution(7765632808086423370)
XLA Ops:
  12.2 5.9 %collective-permute-start = (bf16[512,1024]{1,0:T(8,128)(2,1)S(1)}, bf16[512,1024]{1,0:T(8,128)(2,1)}, u32[]{:S(2)}, u32[]{:S(2)}) collective-permute-start(bf16[512,1024]{1,0:T(8,128)(2,1)S(1)} %copy-done.2), channel_id=1, source_target_pairs={{0,1},{1,2},{2,3},{4,5},{5,6},{6,7},{8,9},{9,10},{10,11},{12,13},{... | collective-permute-start | bytes 3145736 | tf_op jit(solution)/shard_map/ppermute | solution.py:596
  26.2 37.9 %collective-permute-done.2 = bf16[48,768]{1,0:T(8,128)(2,1)S(1)} collective-permute-done((bf16[48,768]{1,0:T(8,128)(2,1)S(1)}, bf16[48,768]{1,0:T(8,128)(2,1)S(1)}, u32[]{:S(2)}, u32[]{:S(2)}) %collective-permute-start.2) | collective-permute-done | bytes 73760 | tf_op jit(solution)/shard_map/ppermute | solution.py:622
  67.0 4.2 collective-permute-start.5
  74.2 11.5 %collective-permute-done.7 = bf16[4,48,768]{2,1,0:T(8,128)(2,1)S(1)} collective-permute-done((bf16[4,48,768]{2,1,0:T(8,128)(2,1)S(1)}, bf16[4,48,768]{2,1,0:T(8,128)(2,1)S(1)}, u32[]{:S(2)}, u32[]{:S(2)}) %collective-permute-start.7) | collective-permute-done | bytes 294944 | tf_op jit(solution)/shard_map/ppermute | solution.py:570
  85.7 24.1 %collective-permute-done.5 = bf16[512,1024]{1,0:T(8,128)(2,1)} collective-permute-done((bf16[512,1024]{1,0:T(8,128)(2,1)}, bf16[512,1024]{1,0:T(8,128)(2,1)}, u32[]{:S(2)}, u32[]{:S(2)}) %collective-permute-start.5) | collective-permute-done | bytes 1048608 | tf_op jit(solution)/shard_map/ppermute | solution.py:596
  109.7 5.1 %collective-permute-done.6 = bf16[512,1024]{1,0:T(8,128)(2,1)} collective-permute-done((bf16[512,1024]{1,0:T(8,128)(2,1)S(1)}, bf16[512,1024]{1,0:T(8,128)(2,1)}, u32[]{:S(2)}, u32[]{:S(2)}) %collective-permute-start.6) | collective-permute-done | bytes 1048608 | tf_op jit(solution)/shard_map/ppermute | solution.py:597
  123.6 10.1 %collective-permute-done.10 = bf16[2,4,48,768]{3,2,1,0:T(8,128)(2,1)S(1)} collective-permute-done((bf16[2,4,48,768]{3,2,1,0:T(8,128)(2,1)S(1)}, bf16[2,4,48,768]{3,2,1,0:T(8,128)(2,1)S(1)}, u32[]{:S(2)}, u32[]{:S(2)}) %collective-permute-start.10) | collective-permute-done | bytes 589856 | tf_op jit(solution)/shard_map/ppermute | solution.py:570
  133.7 8.0 %collective-permute-done.8 = bf16[512,1024]{1,0:T(8,128)(2,1)} collective-permute-done((bf16[512,1024]{1,0:T(8,128)(2,1)}, bf16[512,1024]{1,0:T(8,128)(2,1)}, u32[]{:S(2)}, u32[]{:S(2)}) %collective-permute-start.8) | collective-permute-done | bytes 1048608 | tf_op jit(solution)/shard_map/ppermute | solution.py:596
  141.7 5.1 %collective-permute-done.9 = bf16[512,1024]{1,0:T(8,128)(2,1)} collective-permute-done((bf16[512,1024]{1,0:T(8,128)(2,1)}, bf16[512,1024]{1,0:T(8,128)(2,1)}, u32[]{:S(2)}, u32[]{:S(2)}) %collective-permute-start.9) | collective-permute-done | bytes 1048608 | tf_op jit(solution)/shard_map/ppermute | solution.py:597
  154.7 7.3 %add_convert_fusion.q_ref.k_ref.v_ref = bf16[2048,768]{1,0:T(8,128)(2,1)} fusion(bf16[2048,1024]{1,0:T(8,128)(2,1)} %bitcast.154, bf16[1024,768]{1,0:T(8,128)(2,1)S(1)} %bitcast.168, f32[768]{0:T(1024)S(1)} %add.243), kind=kOutput, calls=%fused_computation | convolution fusion | flops 3224371200 | bytes 8915968 | tf_op jit(solution)/shard_map/dot_general | solution.py:814
  163.3 19.7 %attention_forward.3 = (bf16[2048,128]{1,0:T(8,128)(2,1)}, f32[8,2048]{1,0:T(8,128)}) custom-call(s32[4]{0:T(128)} %pad_add_fusion.place_ref, bf16[2048,768]{1,0:T(8,128)(2,1)} %add_convert_fusion.q_ref.k_ref.v_ref, bf16[2048,768]{1,0:T(8,128)(2,1)} %add_convert_fusion.q_ref.k_ref.v_ref, bf16[2048,768]{1,0:T(8,128)(2,1)} %add_convert_fusion.q_ref.k_ref.v_ref), custom_call_target="tpu_custom_call" | custom-call | flops 1073741824 | bytes 2097152 | tf_op jit(solution)/shard_map/attention_forward/pallas_call | solution.py:64
  184.7 4.4 collective-permute-start.17
  189.1 19.4 %attention_forward.2 = (bf16[2048,128]{1,0:T(8,128)(2,1)}, f32[8,2048]{1,0:T(8,128)}) custom-call(s32[4]{0:T(128)} %pad_add_fusion.place_ref, bf16[2048,768]{1,0:T(8,128)(2,1)} %add_convert_fusion.q_ref.k_ref.v_ref, bf16[2048,768]{1,0:T(8,128)(2,1)} %add_convert_fusion.q_ref.k_ref.v_ref, bf16[2048,768]{1,0:T(8,128)(2,1)} %add_convert_fusion.q_ref.k_ref.v_ref), custom_call_target="tpu_custom_call" | custom-call | flops 1073741824 | bytes 2097152 | tf_op jit(solution)/shard_map/attention_forward/pallas_call | solution.py:64
  218.7 4.5 collective-permute-done.13.refs_2_
  223.9 51.4 %layer_middle.1 = (bf16[512,1024]{1,0:T(8,128)(2,1)}, f32[512,1024]{1,0:T(8,128)}, f32[8,1024]{1,0:T(8,128)}, f32[1,4096]{1,0:T(1,128)}, bf16[512,256]{1,0:T(8,1...) custom-call(s32[4]{0:T(128)} %pad_add_fusion.place_ref, ...), custom_call_target="tpu_custom_call" | custom-call | flops 4026531840 | bytes 42991616 | tf_op jit(solution)/shard_map/layer_middle/pallas_call | solution.py:474
  284.3 6.2 %add_convert_fusion.1 = (bf16[2,128,5120]{2,1,0:T(8,128)(2,1)}, bf16[2,128,5120]{2,1,0:T(8,128)(2,1)S(1)}) fusion(bf16[4,128,5120]{2,1,0:T(8,128)(2,1)} %collective-permute-done.18, bf16[4,128,5120]{2,1,0:T(8,128)(2,1)} %get-tuple-element.82), kind=kLoop, calls=%fused_computation.1 | loop fusion | flops 10485760 | bytes 15728640 | tf_op jit(solution)/shard_map/convert_element_type | solution.py:672
  293.8 4.5 add_convert_fusion.3
  303.7 25.9 %attention_backward.2 = (bf16[2048,384]{1,0:T(8,128)(2,1)}, bf16[4,512,384]{2,1,0:T(8,128)(2,1)}) custom-call(s32[4]{0:T(128)} %pad_add_fusion.place_ref, bf16[2048,768]{1,0:T(8,128)(2,1)} %add_convert_fusion.q_ref.k_ref.v_ref, bf16[2048,768]{1,0:T(8,128)(2,1)} %add_convert_fusion.q_ref.k_ref.v_ref, bf16[2048,768]{1,0:T(8,128)(2,1)} %add_convert_fusion.q_ref.k_ref.v_ref, ...), custom_call_target="tpu_custom_call" | custom-call | flops 2684354560 | bytes 4194304 | tf_op jit(solution)/shard_map/attention_backward/pallas_call | solution.py:179
  332.1 5.8 %collective-permute-start.23 = (bf16[512,384]{1,0:T(8,128)(2,1)}, bf16[512,384]{1,0:T(8,128)(2,1)S(1)}, u32[]{:S(2)}, u32[]{:S(2)}) collective-permute-start(bf16[512,384]{1,0:T(8,128)(2,1)} %get-tuple-element.139), channel_id=1, source_target_pairs={{0,1},{1,0},{2,3},{3,2},{4,5},{5,4},{6,7},{7,6},{8,9},{9,8},{10,11... | collective-permute-start | bytes 1179656 | tf_op jit(solution)/shard_map/ppermute | solution.py:613
  341.9 25.5 %attention_backward.3 = (bf16[2048,384]{1,0:T(8,128)(2,1)}, bf16[4,512,384]{2,1,0:T(8,128)(2,1)}) custom-call(s32[4]{0:T(128)} %pad_add_fusion.place_ref, bf16[2048,768]{1,0:T(8,128)(2,1)} %add_convert_fusion.q_ref.k_ref.v_ref, bf16[2048,768]{1,0:T(8,128)(2,1)} %add_convert_fusion.q_ref.k_ref.v_ref, bf16[2048,768]{1,0:T(8,128)(2,1)} %add_convert_fusion.q_ref.k_ref.v_ref, ...), custom_call_target="tpu_custom_call" | custom-call | flops 2684354560 | bytes 4194304 | tf_op jit(solution)/shard_map/attention_backward/pallas_call | solution.py:179
  371.3 4.5 copy_add_fusion.1
  390.9 17.6 %all-to-all-done.refs_4_ = bf16[4,512,384]{2,1,0:T(8,128)(2,1)S(1)} async-done(((bf16[4,512,384]{2,1,0:T(8,128)(2,1)}), bf16[4,512,384]{2,1,0:T(8,128)(2,1)S(1)}, u32[]{:S(2)}, u32[]{:S(2)}) %all-to-all-start) | async-done | bytes 1572896 | tf_op jit(solution)/shard_map/all_to_all | solution.py:873
  431.5 7.7 %input_gradient.1 = bf16[512,1024]{1,0:T(8,128)(2,1)} custom-call(s32[4]{0:T(128)S(1)} %copy-done.1, f32[512,1024]{1,0:T(8,128)S(1)} %copy-done, bf16[1024,3072]{1,0:T(8,128)(2,1)} %all-gather.8.cloned.1.call-done.weights_ref, bf16[512,384]{1,0:T(8,128)(2,1)S(1)} %get-tuple-element.140.refs_0_, bf16[512,384]{1,0:T(8,128)(2,1)S(1)} %collective-permute-done.23.refs_1_, ...), custom_call_target="tpu_custom_call" | custom-call | flops 402653184 | bytes 12582912 | tf_op jit(solution)/shard_map/input_gradient/pallas_call | solution.py:544
  457.6 9.4 %collective-permute-done.38 = bf16[32,768]{1,0:T(8,128)(2,1)S(1)} collective-permute-done((bf16[32,768]{1,0:T(8,128)(2,1)S(1)}, bf16[32,768]{1,0:T(8,128)(2,1)S(1)}, u32[]{:S(2)}, u32[]{:S(2)}) %collective-permute-start.38) | collective-permute-done | bytes 49184 | tf_op jit(solution)/shard_map/ppermute | solution.py:622
  (286 shorter events, 140.6 us)
Async XLA Ops:
  7.2 216.0 %all-gather.6.cloned.1.call-start = ((), (), s32[]{:S(2)}) async-start(), calls=%async_computation.3 | async-start | bytes 8650752 | tf_op jit(solution)/shard_map/all_gather | solution.py:797
  9.2 214.1 %all-gather.4.cloned.1.call-start = ((), (), s32[]{:S(2)}) async-start(), calls=%async_computation.2 | async-start | bytes 10813440 | tf_op jit(solution)/shard_map/all_gather | solution.py:796
  12.1 289.1 %all-gather.8.cloned.1.call-start = ((), (), s32[]{:S(2)}) async-start(), calls=%async_computation.4 | async-start | bytes 6488064 | tf_op jit(solution)/shard_map/all_gather | solution.py:830
  12.2 54.8 %collective-permute-start = (bf16[512,1024]{1,0:T(8,128)(2,1)S(1)}, bf16[512,1024]{1,0:T(8,128)(2,1)}, u32[]{:S(2)}, u32[]{:S(2)}) collective-permute-start(bf16[512,1024]{1,0:T(8,128)(2,1)S(1)} %copy-done.2), channel_id=1, source_target_pairs={{0,1},{1,2},{2,3},{4,5},{5,6},{6,7},{8,9},{9,10},{10,11},{12,13},{... | collective-permute-start | bytes 3145736 | tf_op jit(solution)/shard_map/ppermute | solution.py:596
  18.1 48.9 %collective-permute-start.1 = (bf16[512,1024]{1,0:T(8,128)(2,1)S(1)}, bf16[512,1024]{1,0:T(8,128)(2,1)S(1)}, u32[]{:S(2)}, u32[]{:S(2)}) collective-permute-start(bf16[512,1024]{1,0:T(8,128)(2,1)S(1)} %copy-done.2), channel_id=1, source_target_pairs={{1,0},{2,1},{3,2},{5,4},{6,5},{7,6},{9,8},{10,9},{11,10},{13,12},{... | collective-permute-start | bytes 3145736 | tf_op jit(solution)/shard_map/ppermute | solution.py:597
  21.0 43.1 %collective-permute-start.2 = (bf16[48,768]{1,0:T(8,128)(2,1)S(1)}, bf16[48,768]{1,0:T(8,128)(2,1)S(1)}, u32[]{:S(2)}, u32[]{:S(2)}) collective-permute-start(bf16[48,768]{1,0:T(8,128)(2,1)S(1)} %get-tuple-element.158), channel_id=1, source_target_pairs={{0,1},{1,0},{2,3},{3,2},{4,5},{5,4},{6,7},{7,6},{8,9},{9,8},{10,11... | collective-permute-start | bytes 221192 | tf_op jit(solution)/shard_map/ppermute | solution.py:622
  23.8 43.2 %collective-permute-start.3 = (bf16[48,768]{1,0:T(8,128)(2,1)S(1)}, bf16[48,768]{1,0:T(8,128)(2,1)S(1)}, u32[]{:S(2)}, u32[]{:S(2)}) collective-permute-start(bf16[48,768]{1,0:T(8,128)(2,1)S(1)} %get-tuple-element.159), channel_id=1, source_target_pairs={{0,2},{1,3},{2,0},{3,1},{4,6},{5,7},{6,4},{7,5},{8,10},{9,11},{10,... | collective-permute-start | bytes 221192 | tf_op jit(solution)/shard_map/ppermute | solution.py:622
  25.4 41.6 %collective-permute-start.4 = (bf16[48,768]{1,0:T(8,128)(2,1)S(1)}, bf16[48,768]{1,0:T(8,128)(2,1)S(1)}, u32[]{:S(2)}, u32[]{:S(2)}) collective-permute-start(bf16[48,768]{1,0:T(8,128)(2,1)S(1)} %get-tuple-element.157), channel_id=1, source_target_pairs={{0,3},{1,2},{2,1},{3,0},{4,7},{5,6},{6,5},{7,4},{8,11},{9,10},{10,... | collective-permute-start | bytes 221192 | tf_op jit(solution)/shard_map/ppermute | solution.py:622
  67.0 42.8 %collective-permute-start.5 = (bf16[512,1024]{1,0:T(8,128)(2,1)}, bf16[512,1024]{1,0:T(8,128)(2,1)}, u32[]{:S(2)}, u32[]{:S(2)}) collective-permute-start(bf16[512,1024]{1,0:T(8,128)(2,1)} %collective-permute-done), channel_id=1, source_target_pairs={{0,1},{1,2},{2,3},{4,5},{5,6},{6,7},{8,9},{9,10},{10,11},{12,13},{... | collective-permute-start | bytes 3145736 | tf_op jit(solution)/shard_map/ppermute | solution.py:596
  71.2 43.6 %collective-permute-start.6 = (bf16[512,1024]{1,0:T(8,128)(2,1)S(1)}, bf16[512,1024]{1,0:T(8,128)(2,1)}, u32[]{:S(2)}, u32[]{:S(2)}) collective-permute-start(bf16[512,1024]{1,0:T(8,128)(2,1)S(1)} %collective-permute-done.1), channel_id=1, source_target_pairs={{1,0},{2,1},{3,2},{5,4},{6,5},{7,6},{9,8},{10,9},{11,10},{13,12},{... | collective-permute-start | bytes 3145736 | tf_op jit(solution)/shard_map/ppermute | solution.py:597
  114.8 26.9 %collective-permute-start.8 = (bf16[512,1024]{1,0:T(8,128)(2,1)}, bf16[512,1024]{1,0:T(8,128)(2,1)}, u32[]{:S(2)}, u32[]{:S(2)}) collective-permute-start(bf16[512,1024]{1,0:T(8,128)(2,1)} %collective-permute-done.5), channel_id=1, source_target_pairs={{0,1},{1,2},{2,3},{4,5},{5,6},{6,7},{8,9},{9,10},{10,11},{12,13},{... | collective-permute-start | bytes 3145736 | tf_op jit(solution)/shard_map/ppermute | solution.py:596
  117.1 29.6 %collective-permute-start.9 = (bf16[512,1024]{1,0:T(8,128)(2,1)}, bf16[512,1024]{1,0:T(8,128)(2,1)}, u32[]{:S(2)}, u32[]{:S(2)}) collective-permute-start(bf16[512,1024]{1,0:T(8,128)(2,1)} %collective-permute-done.6), channel_id=1, source_target_pairs={{1,0},{2,1},{3,2},{5,4},{6,5},{7,6},{9,8},{10,9},{11,10},{13,12},{... | collective-permute-start | bytes 3145736 | tf_op jit(solution)/shard_map/ppermute | solution.py:597
  184.7 27.3 %collective-permute-start.15 = (bf16[512,128]{1,0:T(8,128)(2,1)S(1)}, bf16[512,128]{1,0:T(8,128)(2,1)S(1)}, u32[]{:S(2)}, u32[]{:S(2)}) collective-permute-start(bf16[512,128]{1,0:T(8,128)(2,1)S(1)} %get-tuple-element.151), channel_id=1, source_target_pairs={{0,1},{1,0},{2,3},{3,2},{4,5},{5,4},{6,7},{7,6},{8,9},{9,8},{10,11... | collective-permute-start | bytes 393224 | tf_op jit(solution)/shard_map/ppermute | solution.py:613
  184.7 31.7 %collective-permute-start.16 = (bf16[512,128]{1,0:T(8,128)(2,1)S(1)}, bf16[512,128]{1,0:T(8,128)(2,1)S(1)}, u32[]{:S(2)}, u32[]{:S(2)}) collective-permute-start(bf16[512,128]{1,0:T(8,128)(2,1)S(1)} %get-tuple-element.150), channel_id=1, source_target_pairs={{0,2},{1,3},{2,0},{3,1},{4,6},{5,7},{6,4},{7,5},{8,10},{9,11},{10,... | collective-permute-start | bytes 393224 | tf_op jit(solution)/shard_map/ppermute | solution.py:613
  184.7 31.7 %collective-permute-start.17 = (bf16[512,128]{1,0:T(8,128)(2,1)S(1)}, bf16[512,128]{1,0:T(8,128)(2,1)S(1)}, u32[]{:S(2)}, u32[]{:S(2)}) collective-permute-start(bf16[512,128]{1,0:T(8,128)(2,1)S(1)} %get-tuple-element.149), channel_id=1, source_target_pairs={{0,3},{1,2},{2,1},{3,0},{4,7},{5,6},{6,5},{7,4},{8,11},{9,10},{10,... | collective-permute-start | bytes 393224 | tf_op jit(solution)/shard_map/ppermute | solution.py:613
  292.2 79.1 %collective-permute-start.26 = (bf16[2,2,2,32,5120]{4,3,1,2,0:T(8,128)(2,1)}, bf16[2,2,2,32,5120]{4,3,1,2,0:T(8,128)(2,1)}, u32[]{:S(2)}, u32[]{:S(2)}) collective-permute-start(bf16[2,2,2,32,5120]{4,3,1,2,0:T(8,128)(2,1)} %copy.86), channel_id=1, source_target_pairs={{0,8},{1,9},{2,10},{3,11},{4,12},{5,13},{6,14},{7,15},{8,0},{9,1},... | collective-permute-start | bytes 7864328 | tf_op jit(solution)/shard_map/ppermute | solution.py:570
  298.2 73.0 %collective-permute-start.27 = (bf16[2,2,2,128,1024]{4,3,2,1,0:T(8,128)(2,1)}, bf16[2,2,2,128,1024]{4,3,2,1,0:T(8,128)(2,1)}, u32[]{:S(2)}, u32[]{:S(2)}) collective-permute-start(bf16[2,2,2,128,1024]{4,3,2,1,0:T(8,128)(2,1)} %bitcast.32), channel_id=1, source_target_pairs={{0,16},{1,17},{2,18},{3,19},{4,20},{5,21},{6,22},{7,23},{8,24},{9,... | collective-permute-start | bytes 6291464 | tf_op jit(solution)/shard_map/ppermute | solution.py:570
  332.1 39.2 %collective-permute-start.23 = (bf16[512,384]{1,0:T(8,128)(2,1)}, bf16[512,384]{1,0:T(8,128)(2,1)S(1)}, u32[]{:S(2)}, u32[]{:S(2)}) collective-permute-start(bf16[512,384]{1,0:T(8,128)(2,1)} %get-tuple-element.139), channel_id=1, source_target_pairs={{0,1},{1,0},{2,3},{3,2},{4,5},{5,4},{6,7},{7,6},{8,9},{9,8},{10,11... | collective-permute-start | bytes 1179656 | tf_op jit(solution)/shard_map/ppermute | solution.py:613
  337.8 33.4 %collective-permute-start.24 = (bf16[512,384]{1,0:T(8,128)(2,1)}, bf16[512,384]{1,0:T(8,128)(2,1)S(1)}, u32[]{:S(2)}, u32[]{:S(2)}) collective-permute-start(bf16[512,384]{1,0:T(8,128)(2,1)} %get-tuple-element.138), channel_id=1, source_target_pairs={{0,2},{1,3},{2,0},{3,1},{4,6},{5,7},{6,4},{7,5},{8,10},{9,11},{10,... | collective-permute-start | bytes 1179656 | tf_op jit(solution)/shard_map/ppermute | solution.py:613
  337.8 33.4 %collective-permute-start.25 = (bf16[512,384]{1,0:T(8,128)(2,1)S(1)}, bf16[512,384]{1,0:T(8,128)(2,1)S(1)}, u32[]{:S(2)}, u32[]{:S(2)}) collective-permute-start(bf16[512,384]{1,0:T(8,128)(2,1)S(1)} %get-tuple-element.137), channel_id=1, source_target_pairs={{0,3},{1,2},{2,1},{3,0},{4,7},{5,6},{6,5},{7,4},{8,11},{9,10},{10,... | collective-permute-start | bytes 1179656 | tf_op jit(solution)/shard_map/ppermute | solution.py:613
  367.4 41.2 %all-to-all-start = ((bf16[4,512,384]{2,1,0:T(8,128)(2,1)}), bf16[4,512,384]{2,1,0:T(8,128)(2,1)S(1)}, u32[]{:S(2)}, u32[]{:S(2)}) async-start(bf16[4,512,384]{2,1,0:T(8,128)(2,1)} %get-tuple-element.93), calls=%async_computation | async-start | bytes 3145728 | tf_op jit(solution)/shard_map/all_to_all | solution.py:873
  379.1 29.4 %collective-permute-start.29 = (bf16[2,2,128,1024]{3,2,1,0:T(8,128)(2,1)}, bf16[2,2,128,1024]{3,2,1,0:T(8,128)(2,1)}, u32[]{:S(2)}, u32[]{:S(2)}) collective-permute-start(bf16[2,2,128,1024]{3,2,1,0:T(8,128)(2,1)} %get-tuple-element.134), channel_id=1, source_target_pairs={{0,8},{1,9},{2,10},{3,11},{4,12},{5,13},{6,14},{7,15},{8,0},{9,1},... | collective-permute-start | bytes 3145736 | tf_op jit(solution)/shard_map/ppermute | solution.py:570
  380.6 30.1 %collective-permute-start.28 = (bf16[2,2,32,5120]{3,2,0,1:T(8,128)(2,1)}, bf16[2,2,32,5120]{3,2,0,1:T(8,128)(2,1)}, u32[]{:S(2)}, u32[]{:S(2)}) collective-permute-start(bf16[2,2,32,5120]{3,2,0,1:T(8,128)(2,1)} %get-tuple-element.128), channel_id=1, source_target_pairs={{0,16},{1,17},{2,18},{3,19},{4,20},{5,21},{6,22},{7,23},{8,24},{9,... | collective-permute-start | bytes 3932168 | tf_op jit(solution)/shard_map/ppermute | solution.py:570
  413.6 31.8 %collective-permute-start.31 = (bf16[2,32,5120]{2,1,0:T(8,128)(2,1)}, bf16[2,32,5120]{2,1,0:T(8,128)(2,1)}, u32[]{:S(2)}, u32[]{:S(2)}) collective-permute-start(bf16[2,32,5120]{2,1,0:T(8,128)(2,1)} %get-tuple-element.126), channel_id=1, source_target_pairs={{0,1},{1,0},{2,3},{3,2},{4,5},{5,4},{6,7},{7,6},{8,9},{9,8},{10,11... | collective-permute-start | bytes 1966088 | tf_op jit(solution)/shard_map/ppermute | solution.py:570
  (62 other events, 619.6 us)
Sparse Core Ops, SparseCore 0:
  11.6 98.3 all-gather.5
  113.4 103.0 all-gather.3
  219.4 75.7 all-gather.7

commit v5 on v4

--- a/solution.py
+++ b/solution.py
@@ -22,8 +22,9 @@
 
 
 def attention_forward_kernel(
-    place_ref, q_ref, k_ref, v_ref, mixed_ref, lse_ref, keys_t_ref, *, heads, rows
+    place_ref, q_ref, k_ref, v_ref, mixed_ref, lse_ref, *refs, heads, rows
 ):
+    slot_refs, keys_t_ref = refs[:-1], refs[-1]
     width = k_ref.shape[1]
     seq = keys_t_ref.shape[1]
 
@@ -54,6 +55,12 @@
         mixed = jnp.where(head_of == head, part * (1.0 / total), mixed)
         lse = jnp.where(lane == head, top + jnp.log2(total), lse)
     mixed_ref[...] = mixed.astype(bf16)
+    for slot, slot_ref in enumerate(slot_refs):
+
+        @pl.when(pl.program_id(0) == slot)
+        def _(slot_ref=slot_ref):
+            slot_ref[...] = mixed_ref[...]
+
     lse_ref[...] = lse.T[:8]
 
 
@@ -73,11 +80,13 @@
         out_specs=[
             pl.BlockSpec((rows, width), lambda i: (i, 0)),
             pl.BlockSpec((8, rows), lambda i: (0, i)),
-        ],
+        ]
+        + [pl.BlockSpec((rows, width), lambda i: (0, 0))] * (seq // rows),
         out_shape=[
             jax.ShapeDtypeStruct((seq, width), bf16),
             jax.ShapeDtypeStruct((8, seq), f32),
-        ],
+        ]
+        + [jax.ShapeDtypeStruct((rows, width), bf16)] * (seq // rows),
         scratch_shapes=[pltpu.VMEM((width, seq), bf16)],
         compiler_params=pltpu.CompilerParams(vmem_limit_bytes=56 * 2**20),
         cost_estimate=pl.CostEstimate(
@@ -385,7 +394,7 @@
         w_outer[span, :] = terms.astype(bf16)
         return carried
 
-    lax.fori_loop(0, hidden_width // block, outer_gradient, 0, unroll=2)
+    lax.fori_loop(0, hidden_width // block, outer_gradient, 0, unroll=4)
     leaving = leave(3, w_outer, 1, 0, outer_slab)
 
     def back_in(turn, carried):
@@ -440,7 +449,7 @@
             w_inner[rows_of, span] = terms.astype(bf16)
         return carried
 
-    lax.fori_loop(0, hidden_width // wide_block, inner_gradient, 0, unroll=2)
+    lax.fori_loop(0, hidden_width // wide_block, inner_gradient, 0, unroll=4)
     leaving += leave(3 + len(leaving), w_inner, 0, width, slab)
     turned_ref[...] = mixed_ref[...].T
     for half in range(width // block):
@@ -817,12 +826,10 @@
     ).astype(jnp.int32)
     mixed_own, lse, mixed_parts = [], [], []
     for chunk in range(chunks):
-        mixed_chunk, lse_chunk = attention_forward(qkv, where, rows, chunk, chunks)
+        mixed_chunk, lse_chunk, *mixed_slots = attention_forward(qkv, where, rows, chunk, chunks)
         mixed_own.append(mixed_chunk)
         lse.append(lse_chunk)
-        mixed_parts += exchange_slots(
-            [mixed_chunk[slot * rows : (slot + 1) * rows] for slot in range(n_ctx)]
-        )
+        mixed_parts += exchange_slots(mixed_slots)
 
     by_chunk = triple.reshape(part, 3, n_ctx, chunks, 128).transpose(0, 3, 2, 1, 4)
     by_chunk = by_chunk.reshape(part, 3 * width)

time: 489 us -> 494 us (1.010)
  waiting for transfers between devices: 152 us -> 162 us
    all_gather x1, waiting for transfers between devices: 0.01 us -> 10.8 us  [local(): w_triple = lax.all_gather(by_chunk, AXES, axis=0, tiled=True)]
  transfers between devices with their start and end apart: 46 -> 46, of which waited for: 19 -> 20; matrix products, arithmetic and copies ran while one was open for 16% -> 15% of each run, Pallas kernels for 31% -> 31%
where the time goes in v5:
time: 494 us; the launch traced here: 487 us
  waiting for transfers between devices  162 us (33%)
  Pallas kernels  149 us (30%)
  starting transfers between devices  74.5 us (15%)
  other arithmetic  49.7 us (10%)
  local copies, waits for them, and re-layouts  23.8 us (5%)
  between operations  16.1 us (3%)
  matrix products  12 us (2%)
    ppermute x6, waiting for transfers between devices, exchange_line(): lax.ppermute(lax.dynamic_index_in_dim(blocks, place ^ mask, 0, keepdims=F...  51.5 us
    pallas_call x2, Pallas kernels, attention_backward(): pl.pallas_call(functools.partial(attention_backward_kernel, heads=heads,...  51.4 us
    pallas_call x1, Pallas kernels, layer_middle(): pl.pallas_call(functools.partial(layer_kernel, chunks=chunks, groups=grou...  50.3 us
    pallas_call x2, Pallas kernels, attention_forward(): pl.pallas_call(functools.partial(attention_forward_kernel, heads=heads, r...  39.6 us
    ppermute x3, waiting for transfers between devices, gather_line(): lax.ppermute(from_left, 'ctx', [(i, i + 1) for i in range(count - 1)])  32.1 us
    ppermute x14, waiting for transfers between devices, swap(): return lax.ppermute(values, AXES, [(i, i ^ 1 << bit) for i in range(count)])  27.6 us
    ppermute x12, starting transfers between devices, exchange_slots(): lax.ppermute(slots[mask], 'ctx', [(i, i ^ mask) for i in range(count)])  19.9 us
    ppermute x14, starting transfers between devices, swap(): return lax.ppermute(values, AXES, [(i, i ^ 1 << bit) for i in range(count)])  17.1 us
  transfers between devices with their start and end apart: 46, of which 20 were waited for; matrix products, arithmetic and copies ran while one was open for 15% of the time, Pallas kernels for 31%

profile of v5, /device:TPU:0, one launch (start us, length us, event | category | flops | bytes accessed | tf_op | source)
XLA Modules:
  0.0 487.0 jit_solution(4648227393645389768)
XLA Ops:
  12.2 5.9 %collective-permute-start = (bf16[512,1024]{1,0:T(8,128)(2,1)S(1)}, bf16[512,1024]{1,0:T(8,128)(2,1)}, u32[]{:S(2)}, u32[]{:S(2)}) collective-permute-start(bf16[512,1024]{1,0:T(8,128)(2,1)S(1)} %copy-done.2), channel_id=1, source_target_pairs={{0,1},{1,2},{2,3},{4,5},{5,6},{6,7},{8,9},{9,10},{10,11},{12,13},{... | collective-permute-start | bytes 3145736 | tf_op jit(solution)/shard_map/ppermute | solution.py:605
  26.2 38.0 %collective-permute-done.2 = bf16[48,768]{1,0:T(8,128)(2,1)S(1)} collective-permute-done((bf16[48,768]{1,0:T(8,128)(2,1)S(1)}, bf16[48,768]{1,0:T(8,128)(2,1)S(1)}, u32[]{:S(2)}, u32[]{:S(2)}) %collective-permute-start.2) | collective-permute-done | bytes 73760 | tf_op jit(solution)/shard_map/ppermute | solution.py:631
  74.2 11.5 %collective-permute-done.7 = bf16[4,48,768]{2,1,0:T(8,128)(2,1)S(1)} collective-permute-done((bf16[4,48,768]{2,1,0:T(8,128)(2,1)S(1)}, bf16[4,48,768]{2,1,0:T(8,128)(2,1)S(1)}, u32[]{:S(2)}, u32[]{:S(2)}) %collective-permute-start.7) | collective-permute-done | bytes 294944 | tf_op jit(solution)/shard_map/ppermute | solution.py:579
  85.7 24.1 %collective-permute-done.5 = bf16[512,1024]{1,0:T(8,128)(2,1)} collective-permute-done((bf16[512,1024]{1,0:T(8,128)(2,1)}, bf16[512,1024]{1,0:T(8,128)(2,1)}, u32[]{:S(2)}, u32[]{:S(2)}) %collective-permute-start.5) | collective-permute-done | bytes 1048608 | tf_op jit(solution)/shard_map/ppermute | solution.py:605
  109.7 5.0 %collective-permute-done.6 = bf16[512,1024]{1,0:T(8,128)(2,1)} collective-permute-done((bf16[512,1024]{1,0:T(8,128)(2,1)S(1)}, bf16[512,1024]{1,0:T(8,128)(2,1)}, u32[]{:S(2)}, u32[]{:S(2)}) %collective-permute-start.6) | collective-permute-done | bytes 1048608 | tf_op jit(solution)/shard_map/ppermute | solution.py:606
  123.6 10.1 %collective-permute-done.10 = bf16[2,4,48,768]{3,2,1,0:T(8,128)(2,1)S(1)} collective-permute-done((bf16[2,4,48,768]{3,2,1,0:T(8,128)(2,1)S(1)}, bf16[2,4,48,768]{3,2,1,0:T(8,128)(2,1)S(1)}, u32[]{:S(2)}, u32[]{:S(2)}) %collective-permute-start.10) | collective-permute-done | bytes 589856 | tf_op jit(solution)/shard_map/ppermute | solution.py:579
  133.7 8.0 %collective-permute-done.8 = bf16[512,1024]{1,0:T(8,128)(2,1)} collective-permute-done((bf16[512,1024]{1,0:T(8,128)(2,1)}, bf16[512,1024]{1,0:T(8,128)(2,1)}, u32[]{:S(2)}, u32[]{:S(2)}) %collective-permute-start.8) | collective-permute-done | bytes 1048608 | tf_op jit(solution)/shard_map/ppermute | solution.py:605
  141.6 5.1 %collective-permute-done.9 = bf16[512,1024]{1,0:T(8,128)(2,1)} collective-permute-done((bf16[512,1024]{1,0:T(8,128)(2,1)}, bf16[512,1024]{1,0:T(8,128)(2,1)}, u32[]{:S(2)}, u32[]{:S(2)}) %collective-permute-start.9) | collective-permute-done | bytes 1048608 | tf_op jit(solution)/shard_map/ppermute | solution.py:606
  154.7 7.3 %add_convert_fusion.q_ref.k_ref.v_ref = bf16[2048,768]{1,0:T(8,128)(2,1)} fusion(bf16[2048,1024]{1,0:T(8,128)(2,1)} %bitcast.154, bf16[1024,768]{1,0:T(8,128)(2,1)S(1)} %bitcast.168, f32[768]{0:T(1024)S(1)} %add.243), kind=kOutput, calls=%fused_computation | convolution fusion | flops 3224371200 | bytes 8915968 | tf_op jit(solution)/shard_map/dot_general | solution.py:823
  163.2 19.9 %attention_forward.3 = (bf16[2048,128]{1,0:T(8,128)(2,1)}, f32[8,2048]{1,0:T(8,128)}, bf16[512,128]{1,0:T(8,128)(2,1)}, bf16[512,128]{1,0:T(8,128)(2,1)}, bf16[5...) custom-call(s32[4]{0:T(128)} %pad_add_fusion.place_ref, bf16[2048,768]{1,0:T(8,128)(2,1)} %add_convert_fusion.q_ref.k_ref.v_ref, ...), custom_call_target="tpu_custom_call" | custom-call | flops 1073741824 | bytes 2097152 | tf_op jit(solution)/shard_map/attention_forward/pallas_call | solution.py:71
  183.3 4.3 collective-permute-start.17
  187.6 19.7 %attention_forward.2 = (bf16[2048,128]{1,0:T(8,128)(2,1)}, f32[8,2048]{1,0:T(8,128)}, bf16[512,128]{1,0:T(8,128)(2,1)}, bf16[512,128]{1,0:T(8,128)(2,1)}, bf16[5...) custom-call(s32[4]{0:T(128)} %pad_add_fusion.place_ref, bf16[2048,768]{1,0:T(8,128)(2,1)} %add_convert_fusion.q_ref.k_ref.v_ref, ...), custom_call_target="tpu_custom_call" | custom-call | flops 1073741824 | bytes 2097152 | tf_op jit(solution)/shard_map/attention_forward/pallas_call | solution.py:71
  215.6 6.5 %collective-permute-done.13.refs_2_ = bf16[512,128]{1,0:T(8,128)(2,1)S(1)} collective-permute-done((bf16[512,128]{1,0:T(8,128)(2,1)}, bf16[512,128]{1,0:T(8,128)(2,1)S(1)}, u32[]{:S(2)}, u32[]{:S(2)}) %collective-permute-start.13) | collective-permute-done | bytes 131104 | tf_op jit(solution)/shard_map/ppermute | solution.py:622
  223.0 50.3 %layer_middle.1 = (bf16[512,1024]{1,0:T(8,128)(2,1)}, f32[512,1024]{1,0:T(8,128)}, f32[8,1024]{1,0:T(8,128)}, f32[1,4096]{1,0:T(1,128)}, bf16[512,256]{1,0:T(8,1...) custom-call(s32[4]{0:T(128)} %pad_add_fusion.place_ref, ...), custom_call_target="tpu_custom_call" | custom-call | flops 4026531840 | bytes 42991616 | tf_op jit(solution)/shard_map/layer_middle/pallas_call | solution.py:483
  282.5 6.1 %add_convert_fusion.1 = (bf16[2,128,5120]{2,1,0:T(8,128)(2,1)}, bf16[2,128,5120]{2,1,0:T(8,128)(2,1)S(1)}) fusion(bf16[4,128,5120]{2,1,0:T(8,128)(2,1)} %collective-permute-done.18, bf16[4,128,5120]{2,1,0:T(8,128)(2,1)} %get-tuple-element.97), kind=kLoop, calls=%fused_computation.1 | loop fusion | flops 10485760 | bytes 15728640 | tf_op jit(solution)/shard_map/convert_element_type | solution.py:681
  291.7 4.7 add_convert_fusion.3
  299.3 10.8 %all-gather.8.cloned.1.call-done.weights_ref = bf16[1024,3072]{1,0:T(8,128)(2,1)} async-done(((bf16[32,3072]{1,0:T(8,128)(2,1)}), bf16[1024,3072]{1,0:T(8,128)(2,1)}) %all-gather.8.cloned.1.call-update) | async-done | bytes 6291472 | tf_op jit(solution)/shard_map/all_gather | solution.py:837
  311.1 25.6 %attention_backward.2 = (bf16[2048,384]{1,0:T(8,128)(2,1)}, bf16[4,512,384]{2,1,0:T(8,128)(2,1)}) custom-call(s32[4]{0:T(128)} %pad_add_fusion.place_ref, bf16[2048,768]{1,0:T(8,128)(2,1)} %add_convert_fusion.q_ref.k_ref.v_ref, bf16[2048,768]{1,0:T(8,128)(2,1)} %add_convert_fusion.q_ref.k_ref.v_ref, bf16[2048,768]{1,0:T(8,128)(2,1)} %add_convert_fusion.q_ref.k_ref.v_ref, ...), custom_call_target="tpu_custom_call" | custom-call | flops 2684354560 | bytes 4194304 | tf_op jit(solution)/shard_map/attention_backward/pallas_call | solution.py:188
  346.3 25.8 %attention_backward.3 = (bf16[2048,384]{1,0:T(8,128)(2,1)}, bf16[4,512,384]{2,1,0:T(8,128)(2,1)}) custom-call(s32[4]{0:T(128)} %pad_add_fusion.place_ref, bf16[2048,768]{1,0:T(8,128)(2,1)} %add_convert_fusion.q_ref.k_ref.v_ref, bf16[2048,768]{1,0:T(8,128)(2,1)} %add_convert_fusion.q_ref.k_ref.v_ref, bf16[2048,768]{1,0:T(8,128)(2,1)} %add_convert_fusion.q_ref.k_ref.v_ref, ...), custom_call_target="tpu_custom_call" | custom-call | flops 2684354560 | bytes 4194304 | tf_op jit(solution)/shard_map/attention_backward/pallas_call | solution.py:188
  375.7 4.5 copy_add_fusion.1
  396.3 16.3 %all-to-all-done.refs_4_ = bf16[4,512,384]{2,1,0:T(8,128)(2,1)S(1)} async-done(((bf16[4,512,384]{2,1,0:T(8,128)(2,1)}), bf16[4,512,384]{2,1,0:T(8,128)(2,1)S(1)}, u32[]{:S(2)}, u32[]{:S(2)}) %all-to-all-start) | async-done | bytes 1572896 | tf_op jit(solution)/shard_map/all_to_all | solution.py:880
  424.8 4.4 all-to-all-start.1
  436.2 7.7 %input_gradient.1 = bf16[512,1024]{1,0:T(8,128)(2,1)} custom-call(s32[4]{0:T(128)S(1)} %copy-done.1, f32[512,1024]{1,0:T(8,128)S(1)} %copy-done, bf16[1024,3072]{1,0:T(8,128)(2,1)} %all-gather.8.cloned.1.call-done.weights_ref, bf16[512,384]{1,0:T(8,128)(2,1)S(1)} %get-tuple-element.156.refs_0_, bf16[512,384]{1,0:T(8,128)(2,1)S(1)} %collective-permute-done.23.refs_1_, ...), custom_call_target="tpu_custom_call" | custom-call | flops 402653184 | bytes 12582912 | tf_op jit(solution)/shard_map/input_gradient/pallas_call | solution.py:553
  462.3 9.5 %collective-permute-done.38 = bf16[32,768]{1,0:T(8,128)(2,1)S(1)} collective-permute-done((bf16[32,768]{1,0:T(8,128)(2,1)S(1)}, bf16[32,768]{1,0:T(8,128)(2,1)S(1)}, u32[]{:S(2)}, u32[]{:S(2)}) %collective-permute-start.38) | collective-permute-done | bytes 49184 | tf_op jit(solution)/shard_map/ppermute | solution.py:631
  (284 shorter events, 139.8 us)
Async XLA Ops:
  7.2 214.9 %all-gather.6.cloned.1.call-start = ((), (), s32[]{:S(2)}) async-start(), calls=%async_computation.3 | async-start | bytes 8650752 | tf_op jit(solution)/shard_map/all_gather | solution.py:806
  9.2 213.8 %all-gather.4.cloned.1.call-start = ((), (), s32[]{:S(2)}) async-start(), calls=%async_computation.2 | async-start | bytes 10813440 | tf_op jit(solution)/shard_map/all_gather | solution.py:805
  12.1 298.0 %all-gather.8.cloned.1.call-start = ((), (), s32[]{:S(2)}) async-start(), calls=%async_computation.4 | async-start | bytes 6488064 | tf_op jit(solution)/shard_map/all_gather | solution.py:837
  12.2 54.8 %collective-permute-start = (bf16[512,1024]{1,0:T(8,128)(2,1)S(1)}, bf16[512,1024]{1,0:T(8,128)(2,1)}, u32[]{:S(2)}, u32[]{:S(2)}) collective-permute-start(bf16[512,1024]{1,0:T(8,128)(2,1)S(1)} %copy-done.2), channel_id=1, source_target_pairs={{0,1},{1,2},{2,3},{4,5},{5,6},{6,7},{8,9},{9,10},{10,11},{12,13},{... | collective-permute-start | bytes 3145736 | tf_op jit(solution)/shard_map/ppermute | solution.py:605
  18.1 48.9 %collective-permute-start.1 = (bf16[512,1024]{1,0:T(8,128)(2,1)S(1)}, bf16[512,1024]{1,0:T(8,128)(2,1)S(1)}, u32[]{:S(2)}, u32[]{:S(2)}) collective-permute-start(bf16[512,1024]{1,0:T(8,128)(2,1)S(1)} %copy-done.2), channel_id=1, source_target_pairs={{1,0},{2,1},{3,2},{5,4},{6,5},{7,6},{9,8},{10,9},{11,10},{13,12},{... | collective-permute-start | bytes 3145736 | tf_op jit(solution)/shard_map/ppermute | solution.py:606
  21.1 43.1 %collective-permute-start.2 = (bf16[48,768]{1,0:T(8,128)(2,1)S(1)}, bf16[48,768]{1,0:T(8,128)(2,1)S(1)}, u32[]{:S(2)}, u32[]{:S(2)}) collective-permute-start(bf16[48,768]{1,0:T(8,128)(2,1)S(1)} %get-tuple-element.166), channel_id=1, source_target_pairs={{0,1},{1,0},{2,3},{3,2},{4,5},{5,4},{6,7},{7,6},{8,9},{9,8},{10,11... | collective-permute-start | bytes 221192 | tf_op jit(solution)/shard_map/ppermute | solution.py:631
  23.8 43.2 %collective-permute-start.3 = (bf16[48,768]{1,0:T(8,128)(2,1)S(1)}, bf16[48,768]{1,0:T(8,128)(2,1)S(1)}, u32[]{:S(2)}, u32[]{:S(2)}) collective-permute-start(bf16[48,768]{1,0:T(8,128)(2,1)S(1)} %get-tuple-element.167), channel_id=1, source_target_pairs={{0,2},{1,3},{2,0},{3,1},{4,6},{5,7},{6,4},{7,5},{8,10},{9,11},{10,... | collective-permute-start | bytes 221192 | tf_op jit(solution)/shard_map/ppermute | solution.py:631
  25.4 41.6 %collective-permute-start.4 = (bf16[48,768]{1,0:T(8,128)(2,1)S(1)}, bf16[48,768]{1,0:T(8,128)(2,1)S(1)}, u32[]{:S(2)}, u32[]{:S(2)}) collective-permute-start(bf16[48,768]{1,0:T(8,128)(2,1)S(1)} %get-tuple-element.165), channel_id=1, source_target_pairs={{0,3},{1,2},{2,1},{3,0},{4,7},{5,6},{6,5},{7,4},{8,11},{9,10},{10,... | collective-permute-start | bytes 221192 | tf_op jit(solution)/shard_map/ppermute | solution.py:631
  67.0 42.8 %collective-permute-start.5 = (bf16[512,1024]{1,0:T(8,128)(2,1)}, bf16[512,1024]{1,0:T(8,128)(2,1)}, u32[]{:S(2)}, u32[]{:S(2)}) collective-permute-start(bf16[512,1024]{1,0:T(8,128)(2,1)} %collective-permute-done), channel_id=1, source_target_pairs={{0,1},{1,2},{2,3},{4,5},{5,6},{6,7},{8,9},{9,10},{10,11},{12,13},{... | collective-permute-start | bytes 3145736 | tf_op jit(solution)/shard_map/ppermute | solution.py:605
  71.2 43.6 %collective-permute-start.6 = (bf16[512,1024]{1,0:T(8,128)(2,1)S(1)}, bf16[512,1024]{1,0:T(8,128)(2,1)}, u32[]{:S(2)}, u32[]{:S(2)}) collective-permute-start(bf16[512,1024]{1,0:T(8,128)(2,1)S(1)} %collective-permute-done.1), channel_id=1, source_target_pairs={{1,0},{2,1},{3,2},{5,4},{6,5},{7,6},{9,8},{10,9},{11,10},{13,12},{... | collective-permute-start | bytes 3145736 | tf_op jit(solution)/shard_map/ppermute | solution.py:606
  117.1 29.6 %collective-permute-start.9 = (bf16[512,1024]{1,0:T(8,128)(2,1)}, bf16[512,1024]{1,0:T(8,128)(2,1)}, u32[]{:S(2)}, u32[]{:S(2)}) collective-permute-start(bf16[512,1024]{1,0:T(8,128)(2,1)} %collective-permute-done.6), channel_id=1, source_target_pairs={{1,0},{2,1},{3,2},{5,4},{6,5},{7,6},{9,8},{10,9},{11,10},{13,12},{... | collective-permute-start | bytes 3145736 | tf_op jit(solution)/shard_map/ppermute | solution.py:606
  183.3 30.3 %collective-permute-start.16 = (bf16[512,128]{1,0:T(8,128)(2,1)}, bf16[512,128]{1,0:T(8,128)(2,1)S(1)}, u32[]{:S(2)}, u32[]{:S(2)}) collective-permute-start(bf16[512,128]{1,0:T(8,128)(2,1)} %get-tuple-element.89), channel_id=1, source_target_pairs={{0,2},{1,3},{2,0},{3,1},{4,6},{5,7},{6,4},{7,5},{8,10},{9,11},{10,... | collective-permute-start | bytes 393224 | tf_op jit(solution)/shard_map/ppermute | solution.py:622
  183.3 30.2 %collective-permute-start.17 = (bf16[512,128]{1,0:T(8,128)(2,1)}, bf16[512,128]{1,0:T(8,128)(2,1)S(1)}, u32[]{:S(2)}, u32[]{:S(2)}) collective-permute-start(bf16[512,128]{1,0:T(8,128)(2,1)} %get-tuple-element.90), channel_id=1, source_target_pairs={{0,3},{1,2},{2,1},{3,0},{4,7},{5,6},{6,5},{7,4},{8,11},{9,10},{10,... | collective-permute-start | bytes 393224 | tf_op jit(solution)/shard_map/ppermute | solution.py:622
  273.8 36.4 %collective-permute-start.20 = (bf16[512,256]{1,0:T(8,128)(2,1)}, bf16[512,256]{1,0:T(8,128)(2,1)S(1)}, u32[]{:S(2)}, u32[]{:S(2)}) collective-permute-start(bf16[512,256]{1,0:T(8,128)(2,1)} %get-tuple-element.102), channel_id=1, source_target_pairs={{0,1},{1,0},{2,3},{3,2},{4,5},{5,4},{6,7},{7,6},{8,9},{9,8},{10,11... | collective-permute-start | bytes 786440 | tf_op jit(solution)/shard_map/ppermute | solution.py:622
  277.1 33.1 %collective-permute-start.21 = (bf16[512,256]{1,0:T(8,128)(2,1)}, bf16[512,256]{1,0:T(8,128)(2,1)S(1)}, u32[]{:S(2)}, u32[]{:S(2)}) collective-permute-start(bf16[512,256]{1,0:T(8,128)(2,1)} %get-tuple-element.103), channel_id=1, source_target_pairs={{0,2},{1,3},{2,0},{3,1},{4,6},{5,7},{6,4},{7,5},{8,10},{9,11},{10,... | collective-permute-start | bytes 786440 | tf_op jit(solution)/shard_map/ppermute | solution.py:622
  277.1 33.1 %collective-permute-start.22 = (bf16[512,256]{1,0:T(8,128)(2,1)}, bf16[512,256]{1,0:T(8,128)(2,1)S(1)}, u32[]{:S(2)}, u32[]{:S(2)}) collective-permute-start(bf16[512,256]{1,0:T(8,128)(2,1)} %get-tuple-element.104), channel_id=1, source_target_pairs={{0,3},{1,2},{2,1},{3,0},{4,7},{5,6},{6,5},{7,4},{8,11},{9,10},{10,... | collective-permute-start | bytes 786440 | tf_op jit(solution)/shard_map/ppermute | solution.py:622
  290.3 85.4 %collective-permute-start.26 = (bf16[2,2,2,32,5120]{4,3,1,2,0:T(8,128)(2,1)}, bf16[2,2,2,32,5120]{4,3,1,2,0:T(8,128)(2,1)}, u32[]{:S(2)}, u32[]{:S(2)}) collective-permute-start(bf16[2,2,2,32,5120]{4,3,1,2,0:T(8,128)(2,1)} %copy.86), channel_id=1, source_target_pairs={{0,8},{1,9},{2,10},{3,11},{4,12},{5,13},{6,14},{7,15},{8,0},{9,1},... | collective-permute-start | bytes 7864328 | tf_op jit(solution)/shard_map/ppermute | solution.py:579
  296.4 79.3 %collective-permute-start.27 = (bf16[2,2,2,128,1024]{4,3,2,1,0:T(8,128)(2,1)}, bf16[2,2,2,128,1024]{4,3,2,1,0:T(8,128)(2,1)}, u32[]{:S(2)}, u32[]{:S(2)}) collective-permute-start(bf16[2,2,2,128,1024]{4,3,2,1,0:T(8,128)(2,1)} %bitcast.32), channel_id=1, source_target_pairs={{0,16},{1,17},{2,18},{3,19},{4,20},{5,21},{6,22},{7,23},{8,24},{9,... | collective-permute-start | bytes 6291464 | tf_op jit(solution)/shard_map/ppermute | solution.py:579
  339.2 36.4 %collective-permute-start.23 = (bf16[512,384]{1,0:T(8,128)(2,1)}, bf16[512,384]{1,0:T(8,128)(2,1)S(1)}, u32[]{:S(2)}, u32[]{:S(2)}) collective-permute-start(bf16[512,384]{1,0:T(8,128)(2,1)} %get-tuple-element.155), channel_id=1, source_target_pairs={{0,1},{1,0},{2,3},{3,2},{4,5},{5,4},{6,7},{7,6},{8,9},{9,8},{10,11... | collective-permute-start | bytes 1179656 | tf_op jit(solution)/shard_map/ppermute | solution.py:622
  342.3 33.4 %collective-permute-start.24 = (bf16[512,384]{1,0:T(8,128)(2,1)}, bf16[512,384]{1,0:T(8,128)(2,1)S(1)}, u32[]{:S(2)}, u32[]{:S(2)}) collective-permute-start(bf16[512,384]{1,0:T(8,128)(2,1)} %get-tuple-element.154), channel_id=1, source_target_pairs={{0,2},{1,3},{2,0},{3,1},{4,6},{5,7},{6,4},{7,5},{8,10},{9,11},{10,... | collective-permute-start | bytes 1179656 | tf_op jit(solution)/shard_map/ppermute | solution.py:622
  342.3 33.4 %collective-permute-start.25 = (bf16[512,384]{1,0:T(8,128)(2,1)S(1)}, bf16[512,384]{1,0:T(8,128)(2,1)S(1)}, u32[]{:S(2)}, u32[]{:S(2)}) collective-permute-start(bf16[512,384]{1,0:T(8,128)(2,1)S(1)} %get-tuple-element.153), channel_id=1, source_target_pairs={{0,3},{1,2},{2,1},{3,0},{4,7},{5,6},{6,5},{7,4},{8,11},{9,10},{10,... | collective-permute-start | bytes 1179656 | tf_op jit(solution)/shard_map/ppermute | solution.py:622
  372.1 40.5 %all-to-all-start = ((bf16[4,512,384]{2,1,0:T(8,128)(2,1)}), bf16[4,512,384]{2,1,0:T(8,128)(2,1)S(1)}, u32[]{:S(2)}, u32[]{:S(2)}) async-start(bf16[4,512,384]{2,1,0:T(8,128)(2,1)} %get-tuple-element.109), calls=%async_computation | async-start | bytes 3145728 | tf_op jit(solution)/shard_map/all_to_all | solution.py:880
  385.1 29.7 %collective-permute-start.28 = (bf16[2,2,32,5120]{3,2,0,1:T(8,128)(2,1)}, bf16[2,2,32,5120]{3,2,0,1:T(8,128)(2,1)}, u32[]{:S(2)}, u32[]{:S(2)}) collective-permute-start(bf16[2,2,32,5120]{3,2,0,1:T(8,128)(2,1)} %get-tuple-element.144), channel_id=1, source_target_pairs={{0,16},{1,17},{2,18},{3,19},{4,20},{5,21},{6,22},{7,23},{8,24},{9,... | collective-permute-start | bytes 3932168 | tf_op jit(solution)/shard_map/ppermute | solution.py:579
  417.8 32.3 %collective-permute-start.31 = (bf16[2,32,5120]{2,1,0:T(8,128)(2,1)}, bf16[2,32,5120]{2,1,0:T(8,128)(2,1)}, u32[]{:S(2)}, u32[]{:S(2)}) collective-permute-start(bf16[2,32,5120]{2,1,0:T(8,128)(2,1)} %get-tuple-element.142), channel_id=1, source_target_pairs={{0,1},{1,0},{2,3},{3,2},{4,5},{5,4},{6,7},{7,6},{8,9},{9,8},{10,11... | collective-permute-start | bytes 1966088 | tf_op jit(solution)/shard_map/ppermute | solution.py:579
  (62 other events, 640.5 us)
Sparse Core Ops, SparseCore 0:
  11.6 98.3 all-gather.5
  113.4 109.5 all-gather.3
  225.8 84.2 all-gather.7
